TPU v7x, 32 devices: a whole 2x2x4 slice. The times are simulated.
32 devices in a mesh: tm: 8 (over z, y), fsdp: 4 (over x, core).
Axes of the slice: x: 2, y: 2, z: 4, core: 2. Of those that a mesh axis runs over, the one named last changes fastest.
Arguments:
- inputs: bfloat16 [4, 2048, 2048], P('fsdp', 'tm'), may hold values from -6 to 6
- query_rows: bfloat16 [4, 2048, 1024], P('fsdp', 'tm'), may hold values from -8 to 8
- saved_key_rows: bfloat16 [4, 2048, 1024], P('fsdp', 'tm'), may hold values from -8 to 8
- value_rows: bfloat16 [4, 2048, 1024], P('fsdp', 'tm'), may hold values from -6 to 6
- grad_out: bfloat16 [4, 2048, 1024], P('fsdp', 'tm'), may hold values from -24 to 24
- key_weight: bfloat16 [2048, 1024], P('fsdp'), may hold values from -0.125 to 0.125
- value_weight: bfloat16 [2048, 1024], P('fsdp'), may hold values from -0.125 to 0.125
- block_pairs: int32 [8, 8, 2], P('tm'), may hold values from 0 to 15, as said below
- pair_counts: int32 [8], P('tm'), may hold values from 2 to 8, as said below
Outputs:
- grad_query: bfloat16 [4, 2048, 1024], P('fsdp', 'tm')
- input_gradient_rows: bfloat16 [4, 2048, 2048], P('fsdp', 'tm')
- grad_key_weight: float32 [2048, 1024], P('fsdp', 'tm')
- grad_value_weight: float32 [2048, 1024], P('fsdp', 'tm')
Inputs may be any that keep to these rules, and one draw needn't show every extreme that they name: `block_pairs`: row r of shard j names (query block, key block) by block numbers along the sequence. The first pair_counts[j] rows are shard j's part of the mask: the query block is one of shard j's 2 blocks, the key block is at most the query block and above the query block minus 4, no pair stands twice, and each of the shard's query blocks is paired with itself. Rows from pair_counts[j] on are not part of the mask. `pair_counts`: some shard holds all 8 pairs of its band in every draw.
All inputs are finite; a program needn't handle non-finite values.
Results may differ from a plain program's by a relative error of at most 0.012.
Values may be sent and summed in bfloat16 or wider, within the bound.
No kernel may reach another device: no remote copies, remote signals or barrier semaphores. Data moves between devices by JAX's collectives and lax.ppermute only.
A program may use at most 128 MiB of HBM per device.

v0:
```python
import jax
import jax.numpy as jnp
from jax import lax
from jax.sharding import PartitionSpec as P

H = 8
HS = 128
BLK = 128
HD = 1024
QBD = 2
REACH = 2
MAXP = 8


def from_behind(value, axis, steps):
    count = lax.axis_size(axis)
    leading, last = (max(0, -steps), min(count, count - steps))
    return lax.ppermute(value, axis, [(source, source + steps) for source in range(leading, last)])


def head_terms(allowed, query_head, key_head, value_head, cotangent_head):
    score_scale = query_head.shape[-1] ** (-0.5)
    scores = (
        jnp.einsum("qd,kd->qk", query_head, key_head, preferred_element_type=jnp.float32)
        * score_scale
    )
    scores = jnp.where(allowed, scores, -jnp.inf)
    largest = jnp.max(scores, axis=1, keepdims=True)
    weights = jnp.exp(scores - largest)
    weights = weights / jnp.sum(weights, axis=1, keepdims=True)
    weights_low = weights.astype(jnp.bfloat16)
    attended = jnp.dot(weights_low, value_head, preferred_element_type=jnp.float32)
    row_dot = jnp.sum(cotangent_head.astype(jnp.float32) * attended, axis=1, keepdims=True)
    grad_probs = jnp.einsum(
        "qd,kd->qk", cotangent_head, value_head, preferred_element_type=jnp.float32
    )
    grad_low = (weights * (grad_probs - row_dot)).astype(jnp.bfloat16)
    grad_q = jnp.dot(grad_low, key_head, preferred_element_type=jnp.float32) * score_scale
    grad_k = (
        jnp.einsum("qk,qd->kd", grad_low, query_head, preferred_element_type=jnp.float32)
        * score_scale
    )
    grad_v = jnp.einsum(
        "qk,qd->kd", weights_low, cotangent_head, preferred_element_type=jnp.float32
    )
    return (grad_q, grad_k, grad_v)


def split_heads(array):
    return jnp.transpose(array.reshape(array.shape[0], H, HS), (1, 0, 2))


def join_heads(array):
    return jnp.transpose(array, (1, 0, 2)).reshape(array.shape[1], H * HS)


def shards(
    inputs,
    query_rows,
    saved_key_rows,
    value_rows,
    grad_out,
    key_weight,
    value_weight,
    block_pairs,
    pair_counts,
):
    tokens = query_rows.shape[1]
    shard_id = lax.axis_index("tm")
    key_local = saved_key_rows[0]
    value_local = value_rows[0]
    panels = [(key_local, value_local)]
    for offset in range(1, REACH + 1):
        panels.append(from_behind((key_local, value_local), "tm", offset))
    window_keys = jnp.concatenate([panels[offset][0] for offset in range(REACH, -1, -1)], axis=0)
    window_values = jnp.concatenate([panels[offset][1] for offset in range(REACH, -1, -1)], axis=0)
    window_len = (REACH + 1) * tokens
    is_valid = jnp.arange(MAXP) < pair_counts[0]
    query_blocks = shard_id * QBD + jnp.arange(QBD, dtype=jnp.int32)
    key_blocks = (shard_id - REACH) * QBD + jnp.arange((REACH + 1) * QBD, dtype=jnp.int32)
    pair_hits = (
        is_valid[:, None, None]
        & (block_pairs[0, :, 0][:, None, None] == query_blocks[None, :, None])
        & (block_pairs[0, :, 1][:, None, None] == key_blocks[None, None, :])
    )
    block_allowed = jnp.any(pair_hits, axis=0)
    tile_allowed = jnp.repeat(jnp.repeat(block_allowed, BLK, axis=0), BLK, axis=1)
    query_pos = shard_id * tokens + jnp.arange(tokens, dtype=jnp.int32)
    key_pos = (shard_id - REACH) * tokens + jnp.arange(window_len, dtype=jnp.int32)
    allowed = tile_allowed & (key_pos[None, :] <= query_pos[:, None])

    def per_head(head_ops):
        return head_terms(allowed, head_ops[0], head_ops[1], head_ops[2], head_ops[3])

    head_q, head_k, head_v = lax.map(
        per_head,
        (
            split_heads(query_rows[0]),
            split_heads(window_keys),
            split_heads(window_values),
            split_heads(grad_out[0]),
        ),
    )
    grad_query = join_heads(head_q).astype(jnp.bfloat16)[None]
    key_window = join_heads(head_k)
    value_window = join_heads(head_v)

    def key_piece(offset):
        return key_window[(REACH - offset) * tokens : (REACH - offset + 1) * tokens]

    def value_piece(offset):
        return value_window[(REACH - offset) * tokens : (REACH - offset + 1) * tokens]

    grad_keys = key_piece(0)
    grad_values = value_piece(0)
    for offset in range(1, REACH + 1):
        returned = from_behind((key_piece(offset), value_piece(offset)), "tm", -offset)
        grad_keys = grad_keys + returned[0]
        grad_values = grad_values + returned[1]
    keys_low = grad_keys.astype(jnp.bfloat16)
    values_low = grad_values.astype(jnp.bfloat16)
    paired_lower_rows = jnp.concatenate((keys_low, values_low), axis=1)
    pieces = lax.all_gather((key_weight, value_weight), "fsdp", axis=0, tiled=True)
    key_part = jnp.einsum("tc,rc->tr", keys_low, pieces[0], preferred_element_type=jnp.float32)
    value_part = jnp.einsum("tc,rc->tr", values_low, pieces[1], preferred_element_type=jnp.float32)
    input_gradient_rows = (key_part + value_part).astype(jnp.bfloat16)[None]
    input_slab = inputs[0]
    weight_grad = lax.psum_scatter(
        jnp.einsum("tr,tc->rc", input_slab, paired_lower_rows, preferred_element_type=jnp.float32),
        "fsdp",
        scatter_dimension=0,
        tiled=True,
    )
    key_total, value_total = (
        lax.psum_scatter(weight_grad[:, :HD], "tm", scatter_dimension=1, tiled=True),
        lax.psum_scatter(weight_grad[:, HD:], "tm", scatter_dimension=1, tiled=True),
    )
    return (grad_query, input_gradient_rows, key_total, value_total)


def solution(mesh):
    return jax.shard_map(
        shards,
        mesh=mesh,
        in_specs=(
            P("fsdp", "tm", None),
            P("fsdp", "tm", None),
            P("fsdp", "tm", None),
            P("fsdp", "tm", None),
            P("fsdp", "tm", None),
            P("fsdp", None),
            P("fsdp", None),
            P("tm", None, None),
            P("tm"),
        ),
        out_specs=(P("fsdp", "tm", None), P("fsdp", "tm", None), P("fsdp", "tm"), P("fsdp", "tm")),
        check_vma=False,
    )
```

profile of v0, /device:TPU:0, one launch (start us, length us, event | category | flops | bytes accessed | tf_op | source)
XLA Modules:
  0.0 583.1 jit_solution(2054450636299632086)
XLA Ops:
  7.2 1.4 copy.49
  8.6 4.9 collective-permute-start.1
  13.5 4.3 collective-permute-start
  17.8 1.2 copy.52
  19.0 4.3 collective-permute-start.3
  23.3 2.7 collective-permute-start.2
  27.6 2.0 copy.48
  31.6 1.5 maximum_bitcast_fusion
  33.1 2.8 collective-permute-done.3
  35.9 3.2 collective-permute-done.2
  39.1 2.5 maximum_bitcast_fusion.1
  41.6 78.1 %while.15 = (s32[]{:T(128)}, bf16[8,256,128]{2,1,0:T(8,128)(2,1)}, f32[8,768,128]{1,2,0:T(8,128)}, f32[8,768,128]{1,2,0:T(8,128)}, bf16[8,256,128]{1,2,0:T(8,128...) while((s32[]{:T(128)}, bf16[8,256,128]{2,1,0:T(8,128)(2,1)}, ...), condition=%wide.region_5.6_spmd.clone, body=%wide.region_1.5_spmd.clone.sunk | while | flops 305757440 | bytes 22108860 | solution.py:95
  41.9 1.3 fusion.87
  43.5 1.4 fusion.89
  44.9 1.3 fusion.90
  49.2 2.1 fusion.93
  51.7 1.4 fusion.87
  53.3 1.4 fusion.89
  54.7 1.3 fusion.90
  56.9 1.1 fusion.92
  59.0 2.1 fusion.93
  61.5 1.4 fusion.87
  63.1 1.4 fusion.89
  64.5 1.3 fusion.90
  68.8 2.1 fusion.93
  71.2 1.4 fusion.87
  72.9 1.4 fusion.89
  74.2 1.3 fusion.90
  78.6 2.1 fusion.93
  81.0 1.3 fusion.87
  82.6 1.4 fusion.89
  84.0 1.3 fusion.90
  88.3 2.1 fusion.93
  90.7 1.3 fusion.87
  92.4 1.4 fusion.89
  93.7 1.3 fusion.90
  98.1 2.1 fusion.93
  100.5 1.3 fusion.87
  102.1 1.4 fusion.89
  103.5 1.3 fusion.90
  107.8 2.1 fusion.93
  110.3 1.4 fusion.87
  111.9 1.4 fusion.89
  113.3 1.3 fusion.90
  117.6 2.1 fusion.93
  119.7 2.3 fusion.52
  122.0 1.3 collective-permute-start.7
  123.3 1.3 collective-permute-start.6
  125.0 1.3 collective-permute-start.5
  126.3 1.3 collective-permute-start.4
  127.6 33.1 %collective-permute-done.7 = f32[256,1024]{0,1:T(8,128)S(1)} collective-permute-done((f32[256,1024]{0,1:T(8,128)S(1)}, f32[256,1024]{0,1:T(8,128)S(1)}, u32[]{:S(2)}, u32[]{:S(2)}) %collective-permute-start.7) | collective-permute-done | bytes 1048608 | tf_op jit(solution)/shard_map/ppermute | solution.py:18
  160.7 9.4 %collective-permute-done.6 = f32[256,1024]{0,1:T(8,128)S(1)} collective-permute-done((f32[256,1024]{0,1:T(8,128)S(1)}, f32[256,1024]{0,1:T(8,128)S(1)}, u32[]{:S(2)}, u32[]{:S(2)}) %collective-permute-start.6) | collective-permute-done | bytes 1048608 | tf_op jit(solution)/shard_map/ppermute | solution.py:18
  170.3 35.3 %collective-permute-done.5 = f32[256,1024]{0,1:T(8,128)S(1)} collective-permute-done((f32[256,1024]{0,1:T(8,128)S(1)}, f32[256,1024]{0,1:T(8,128)S(1)}, u32[]{:S(2)}, u32[]{:S(2)}) %collective-permute-start.5) | collective-permute-done | bytes 1048608 | tf_op jit(solution)/shard_map/ppermute | solution.py:18
  205.9 8.1 %convolution_bitcast_fusion.1 = f32[2048,2048]{0,1:T(8,128)} fusion(bf16[256,1024]{0,1:T(8,128)(2,1)S(1)} %fusion.45, bf16[256,1024]{0,1:T(8,128)(2,1)S(1)} %fusion.47, bf16[1,256,2048]{2,1,0:T(8,128)(2,1)S(1)} %copy-done), kind=kOutput, calls=%fused_computation.43 | convolution fusion | flops 2149580800 | bytes 18874368 | tf_op jit(solution)/shard_map/tr,tc->rc/dot_general | solution.py:129
  215.6 144.6 %reduce-scatter.4.cloned.1.call-done = f32[512,2048]{0,1:T(8,128)} async-done(((f32[2048,2048]{0,1:T(8,128)}), f32[512,2048]{0,1:T(8,128)}) %reduce-scatter.4.cloned.1.call-update) | async-done | bytes 4194320 | tf_op jit(solution)/shard_map/reduce_scatter | solution.py:128
  360.2 4.6 fusion.50
  367.2 29.1 %all-gather.5.cloned.1.call-done = bf16[2048,1024]{1,0:T(8,128)(2,1)} async-done(((bf16[512,1024]{1,0:T(8,128)(2,1)}), bf16[2048,1024]{1,0:T(8,128)(2,1)}) %all-gather.5.cloned.1.call-update) | async-done | bytes 4194320 | tf_op jit(solution)/shard_map/all_gather | solution.py:123
  396.3 4.8 fusion.53
  401.2 31.3 %all-gather.3.cloned.1.call-done = bf16[2048,1024]{1,0:T(8,128)(2,1)} async-done(((bf16[512,1024]{1,0:T(8,128)(2,1)}), bf16[2048,1024]{1,0:T(8,128)(2,1)}) %all-gather.3.cloned.1.call-update) | async-done | bytes 4194320 | tf_op jit(solution)/shard_map/all_gather | solution.py:123
  432.5 5.1 fusion.39
  437.6 66.4 %reduce-scatter.6.cloned.1.call-done = f32[512,128]{0,1:T(8,128)} async-done(((f32[512,1024]{0,1:T(8,128)}), f32[512,128]{0,1:T(8,128)}) %reduce-scatter.6.cloned.1.call-update) | async-done | bytes 262160 | tf_op jit(solution)/shard_map/reduce_scatter | solution.py:135
  504.1 1.8 copy.60
  505.8 68.9 %reduce-scatter.8.cloned.1.call-done = f32[512,128]{0,1:T(8,128)} async-done(((f32[512,1024]{0,1:T(8,128)}), f32[512,128]{0,1:T(8,128)}) %reduce-scatter.8.cloned.1.call-update) | async-done | bytes 262160 | tf_op jit(solution)/shard_map/reduce_scatter | solution.py:136
  574.8 1.8 copy.61
  (131 shorter events, 35.4 us)
Async XLA Ops:
  7.2 198.8 %copy-start = (bf16[1,256,2048]{2,1,0:T(8,128)(2,1)S(1)}, bf16[1,256,2048]{2,1,0:T(8,128)(2,1)}, u32[]{:S(2)}) copy-start(bf16[1,256,2048]{2,1,0:T(8,128)(2,1)} %param.11) | copy-start | bytes 3145732
  7.2 22.5 %copy-start.5 = (bf16[1,256,1024]{2,1,0:T(8,128)(2,1)S(1)}, bf16[1,256,1024]{2,1,0:T(8,128)(2,1)}, u32[]{:S(2)}) copy-start(bf16[1,256,1024]{2,1,0:T(8,128)(2,1)} %param.15) | copy-start | bytes 1572868
  7.2 353.0 %reduce-scatter.4.cloned.1.call-start = ((), (), s32[]{:S(2)}) async-start(), calls=%async_computation.5 | async-start | bytes 20971520 | tf_op jit(solution)/shard_map/reduce_scatter | solution.py:128
  8.6 22.3 %copy-start.4 = (bf16[1,256,1024]{1,2,0:T(8,128)(2,1)}, bf16[1,256,1024]{1,2,0:T(8,128)(2,1)S(1)}, u32[]{:S(2)}) copy-start(bf16[1,256,1024]{1,2,0:T(8,128)(2,1)S(1)} %copy.49) | copy-start | bytes 1572868
  8.6 22.2 %collective-permute-start.1 = (bf16[256,1024]{0,1:T(8,128)(2,1)S(1)}, bf16[256,1024]{0,1:T(8,128)(2,1)S(1)}, u32[]{:S(2)}, u32[]{:S(2)}) collective-permute-start(bf16[256,1024]{0,1:T(8,128)(2,1)S(1)} %bitcast.139), channel_id=1, source_target_pairs={{0,4},{4,8},{8,12},{12,16},{16,20},{20,24},{24,28},{1,5},{5,9},{9,... | collective-permute-start | bytes 1572872 | tf_op jit(solution)/shard_map/ppermute | solution.py:18
  13.5 17.3 %collective-permute-start = (bf16[256,1024]{0,1:T(8,128)(2,1)S(1)}, bf16[256,1024]{0,1:T(8,128)(2,1)}, u32[]{:S(2)}, u32[]{:S(2)}) collective-permute-start(bf16[256,1024]{0,1:T(8,128)(2,1)S(1)} %bitcast.140), channel_id=1, source_target_pairs={{0,8},{4,12},{8,16},{12,20},{16,24},{20,28},{1,9},{5,13},{9,17},{1... | collective-permute-start | bytes 1572872 | tf_op jit(solution)/shard_map/ppermute | solution.py:18
  19.0 16.9 %collective-permute-start.3 = (bf16[256,1024]{0,1:T(8,128)(2,1)S(1)}, bf16[256,1024]{0,1:T(8,128)(2,1)}, u32[]{:S(2)}, u32[]{:S(2)}) collective-permute-start(bf16[256,1024]{0,1:T(8,128)(2,1)S(1)} %bitcast.136), channel_id=1, source_target_pairs={{0,4},{4,8},{8,12},{12,16},{16,20},{20,24},{24,28},{1,5},{5,9},{9,... | collective-permute-start | bytes 1572872 | tf_op jit(solution)/shard_map/ppermute | solution.py:18
  23.3 15.8 %collective-permute-start.2 = (bf16[256,1024]{0,1:T(8,128)(2,1)S(1)}, bf16[256,1024]{0,1:T(8,128)(2,1)}, u32[]{:S(2)}, u32[]{:S(2)}) collective-permute-start(bf16[256,1024]{0,1:T(8,128)(2,1)S(1)} %bitcast.137), channel_id=1, source_target_pairs={{0,8},{4,12},{8,16},{12,20},{16,24},{20,28},{1,9},{5,13},{9,17},{1... | collective-permute-start | bytes 1572872 | tf_op jit(solution)/shard_map/ppermute | solution.py:18
  30.9 0.8 copy-start.7
  41.6 4.6 copy-start.1
  49.2 2.1 copy-start.2
  51.3 4.7 copy-start.1
  59.0 2.1 copy-start.2
  61.1 4.7 copy-start.1
  68.8 2.1 copy-start.2
  70.9 4.6 copy-start.1
  78.6 2.1 copy-start.2
  80.6 4.6 copy-start.1
  88.3 2.1 copy-start.2
  90.4 4.6 copy-start.1
  98.1 2.1 copy-start.2
  100.2 4.6 copy-start.1
  107.8 2.1 copy-start.2
  109.9 4.7 copy-start.1
  117.6 2.1 copy-start.2
  119.7 4.9 copy-start.3
  122.0 38.7 %collective-permute-start.7 = (f32[256,1024]{0,1:T(8,128)S(1)}, f32[256,1024]{0,1:T(8,128)S(1)}, u32[]{:S(2)}, u32[]{:S(2)}) collective-permute-start(f32[256,1024]{0,1:T(8,128)S(1)} %bitcast.145), channel_id=1, source_target_pairs={{8,0},{12,4},{16,8},{20,12},{24,16},{28,20},{9,1},{13,5},{17,9},{2... | collective-permute-start | bytes 3145736 | tf_op jit(solution)/shard_map/ppermute | solution.py:18
  123.3 46.7 %collective-permute-start.6 = (f32[256,1024]{0,1:T(8,128)S(1)}, f32[256,1024]{0,1:T(8,128)S(1)}, u32[]{:S(2)}, u32[]{:S(2)}) collective-permute-start(f32[256,1024]{0,1:T(8,128)S(1)} %bitcast.143), channel_id=1, source_target_pairs={{4,0},{8,4},{12,8},{16,12},{20,16},{24,20},{28,24},{5,1},{9,5},{13... | collective-permute-start | bytes 3145736 | tf_op jit(solution)/shard_map/ppermute | solution.py:18
  125.0 80.7 %collective-permute-start.5 = (f32[256,1024]{0,1:T(8,128)S(1)}, f32[256,1024]{0,1:T(8,128)S(1)}, u32[]{:S(2)}, u32[]{:S(2)}) collective-permute-start(f32[256,1024]{0,1:T(8,128)S(1)} %bitcast.146), channel_id=1, source_target_pairs={{8,0},{12,4},{16,8},{20,12},{24,16},{28,20},{9,1},{13,5},{17,9},{2... | collective-permute-start | bytes 3145736 | tf_op jit(solution)/shard_map/ppermute | solution.py:18
  126.3 79.4 %collective-permute-start.4 = (f32[256,1024]{0,1:T(8,128)S(1)}, f32[256,1024]{0,1:T(8,128)S(1)}, u32[]{:S(2)}, u32[]{:S(2)}) collective-permute-start(f32[256,1024]{0,1:T(8,128)S(1)} %bitcast.144), channel_id=1, source_target_pairs={{4,0},{8,4},{12,8},{16,12},{20,16},{24,20},{28,24},{5,1},{9,5},{13... | collective-permute-start | bytes 3145736 | tf_op jit(solution)/shard_map/ppermute | solution.py:18
  214.0 182.3 %all-gather.5.cloned.1.call-start = ((), (), s32[]{:S(2)}) async-start(), calls=%async_computation.4 | async-start | bytes 5242880 | tf_op jit(solution)/shard_map/all_gather | solution.py:123
  214.8 217.7 %all-gather.3.cloned.1.call-start = ((), (), s32[]{:S(2)}) async-start(), calls=%async_computation.3 | async-start | bytes 5242880 | tf_op jit(solution)/shard_map/all_gather | solution.py:123
  215.5 288.5 %reduce-scatter.6.cloned.1.call-start = ((), (), s32[]{:S(2)}) async-start(), calls=%async_computation.6 | async-start | bytes 2359296 | tf_op jit(solution)/shard_map/reduce_scatter | solution.py:135
  364.8 1.0 copy-start.6
  364.8 209.9 %reduce-scatter.8.cloned.1.call-start = ((), (), s32[]{:S(2)}) async-start(), calls=%async_computation.7 | async-start | bytes 2359296 | tf_op jit(solution)/shard_map/reduce_scatter | solution.py:136
Sparse Core Ops, SparseCore 0:
  214.2 145.9 reduce-scatter.3
  361.8 34.4 all-gather.4
  398.0 34.4 all-gather.2
  436.3 67.7 reduce-scatter.5
  507.8 66.8 reduce-scatter.7
where the time goes:
time: 585 us; the launch traced here: 583 us
  waiting for transfers between devices  426 us (73%)
  matrix products  83.3 us (14%)
  local copies, waits for them, and re-layouts  30.3 us (5%)
  starting transfers between devices  21.7 us (4%)
  between operations  14.6 us (2%)
  other arithmetic  6.82 us (1%)
    reduce_scatter x1, waiting for transfers between devices, shards(): lax.psum_scatter(jnp.einsum('tr,tc->rc', input_slab, paired_lower_rows, p...  145 us
    ppermute x8, waiting for transfers between devices, from_behind(): lax.ppermute(value, axis, [(source, source + steps) for source in range(l...  83.8 us
    reduce_scatter x1, waiting for transfers between devices, shards(): lax.psum_scatter(weight_grad[:, HD:], 'tm', scatter_dimension=1, tiled=True)  68.9 us
    reduce_scatter x1, waiting for transfers between devices, shards(): lax.psum_scatter(weight_grad[:, :HD], 'tm', scatter_dimension=1, tiled=True)  66.4 us
    all_gather x2, waiting for transfers between devices, shards(): lax.all_gather((key_weight, value_weight), 'fsdp', axis=0, tiled=True)  60.4 us
    ppermute x8, starting transfers between devices, from_behind(): lax.ppermute(value, axis, [(source, source + steps) for source in range(l...  21.3 us
    dot_general x8, matrix products, head_terms(): jnp.einsum('qk,qd->kd', weights_low, cotangent_head, preferred_element_ty...  16.7 us
  transfers between devices with their start and end apart: 13, of which 10 were waited for; matrix products, arithmetic and copies ran while one was open for 4% of the time, Pallas kernels for 0%

commit v1 on v0

v1 whole, which is shorter than its diff:
```python
import functools

import jax
import jax.numpy as jnp
from jax import lax
from jax.experimental import pallas as pl
from jax.experimental.pallas import tpu as pltpu
from jax.sharding import PartitionSpec as P

H = 8
HS = 128
BLK = 128
HD = 1024
QBD = 2
REACH = 2
MAXP = 8
SLOTS = QBD + 3
SPAN = SLOTS * BLK
LOWEST = -1e29
MASKED = -1e30
SCALE = HS ** (-0.5)
GROUPS = ((0, 1, 2, 3, 4, 5, 6, 7),)
VMEM = pl.BlockSpec(memory_space=pltpu.VMEM)
SMEM = pl.BlockSpec(memory_space=pltpu.SMEM)


def kernel_call(body, outs, operands, scalars=0, scratch=(), flops=0):
    moved = sum(x.size * x.dtype.itemsize for x in (*operands, *outs))
    return pl.pallas_call(
        body,
        out_shape=tuple(outs),
        in_specs=[SMEM] * scalars + [VMEM] * (len(operands) - scalars),
        out_specs=tuple([VMEM] * len(outs)),
        scratch_shapes=list(scratch),
        compiler_params=pltpu.CompilerParams(vmem_limit_bytes=40 * 1024 * 1024),
        cost_estimate=pl.CostEstimate(flops=flops, bytes_accessed=moved, transcendentals=0),
    )(*operands)


def shape(dims, kind):
    return jax.ShapeDtypeStruct(dims, kind)


def shifted(value, axis, steps):
    count = lax.axis_size(axis)
    return lax.ppermute(
        value, axis, [(s, s + steps) for s in range(max(0, -steps), min(count, count - steps))]
    )


def rolled_pairs(count, far, flip):
    half = count // 2
    return [(((a + far) % half) * 2 + (b ^ flip), a * 2 + b) for a in range(half) for b in range(2)]


def nt(left, right):
    return lax.dot_general(left, right, (((1,), (1,)), ((), ())), preferred_element_type=jnp.float32)


def tn(left, right):
    return lax.dot_general(left, right, (((0,), (0,)), ((), ())), preferred_element_type=jnp.float32)


def nn(left, right):
    return jnp.dot(left, right, preferred_element_type=jnp.float32)


def fill_bias(tables, bias):
    rows = lax.broadcasted_iota(jnp.int32, (BLK, BLK), 0)
    columns = lax.broadcasted_iota(jnp.int32, (BLK, BLK), 1)
    for key in range(QBD):
        for slot in range(SLOTS):
            place = (pl.ds(key * BLK, BLK), pl.ds(slot * BLK, BLK))
            if not 0 <= slot - key <= 3:
                bias[place] = jnp.full((BLK, BLK), MASKED, jnp.float32)
                continue
            step = slot // QBD
            table = tables[step]
            hit = jnp.int32(0)
            for row in range(MAXP):
                same = (table[2 * row] == slot - QBD * step) & (table[2 * row + 1] == key - QBD * step)
                hit = hit + jnp.where(same & (row < table[2 * MAXP]), 1, 0)
            value = jnp.where(hit > 0, 0.0, MASKED).astype(jnp.float32)
            block = jnp.full((BLK, BLK), value, jnp.float32)
            if slot == key:
                block = jnp.where(rows <= columns, block, MASKED)
            bias[place] = block


def head_of(ref, place):
    return ref[:, place * HS : (place + 1) * HS]


def queries_of(own, near, far, head, place):
    return jnp.concatenate([head_of(own, head), head_of(near, place), head_of(far, place)], axis=0)


def stats_body(heads, t0, t1, t2, q, k, v, g, near, far, own, up1, up2, down1, down2, bias):
    count = len(heads)
    fill_bias((t0, t1, t2), bias)
    for n, h in enumerate(heads):
        query = queries_of(q, near, far, h, n)
        cotangent = queries_of(g, near, far, h, count + n)
        scores = nt(head_of(k, h), query) * SCALE + bias[...]
        products = nt(head_of(v, h), cotangent)
        largest = jnp.maximum(jnp.max(scores, axis=0, keepdims=True), LOWEST)
        weights = jnp.exp(scores - largest)
        own[n : n + 1, :] = largest
        own[count + n : count + n + 1, :] = jnp.sum(weights, axis=0, keepdims=True)
        own[2 * count + n : 2 * count + n + 1, :] = jnp.sum(weights * products, axis=0, keepdims=True)
    up1[...] = own[:, 2 * BLK :]
    up2[...] = own[:, 4 * BLK :]
    down1[...] = own[:, : 3 * BLK]
    down2[...] = own[:, :BLK]


def grads_body(
    heads, t0, t1, t2, q, k, v, g, near, far, own, from1, from2, back1, back2,
    low, dq0, dq1, dq2, bias, total,
):
    count = len(heads)
    fill_bias((t0, t1, t2), bias)

    def terms(ref, first, last):
        part = ref[:, first * BLK : last * BLK]
        large, mass, dot = (part[i * count : (i + 1) * count] for i in range(3))
        return jnp.where(mass > 0, large, LOWEST), mass, dot

    nothing = (
        jnp.full((count, BLK), LOWEST, jnp.float32),
        jnp.zeros((count, BLK), jnp.float32),
        jnp.zeros((count, BLK), jnp.float32),
    )

    def side(*parts):
        return tuple(jnp.concatenate(piece, axis=1) for piece in zip(*parts))

    sets = (
        terms(own, 0, SLOTS),
        side(terms(from1, 0, 3), terms(back1, 1, 3)),
        side(terms(from2, 0, 1), nothing, terms(back1, 0, 1), nothing, terms(back2, 0, 1)),
    )
    largest = jnp.maximum(jnp.maximum(sets[0][0], sets[1][0]), sets[2][0])
    mass = jnp.zeros((count, SPAN), jnp.float32)
    dot = jnp.zeros((count, SPAN), jnp.float32)
    for large, part_mass, part_dot in sets:
        factor = jnp.exp(large - largest)
        mass = mass + factor * part_mass
        dot = dot + factor * part_dot
    inverse = jnp.where(mass > 0, 1.0 / jnp.where(mass > 0, mass, 1.0), 0.0)
    total[0, :count] = largest
    total[1, :count] = inverse
    total[2, :count] = dot * inverse
    for n, h in enumerate(heads):
        query = queries_of(q, near, far, h, n)
        cotangent = queries_of(g, near, far, h, count + n)
        key = head_of(k, h)
        scores = nt(key, query) * SCALE + bias[...]
        products = nt(head_of(v, h), cotangent)
        probs = jnp.exp(scores - total[0, n : n + 1, :]) * total[1, n : n + 1, :]
        grad_scores = (probs * (products - total[2, n : n + 1, :])).astype(jnp.bfloat16)
        columns = slice(n * HS, (n + 1) * HS)
        low[:, columns] = (nn(grad_scores, query) * SCALE).astype(jnp.bfloat16)
        low[:, (count + n) * HS : (count + n + 1) * HS] = nn(
            probs.astype(jnp.bfloat16), cotangent
        ).astype(jnp.bfloat16)
        grad_query = tn(grad_scores, key) * SCALE
        dq0[:, columns] = grad_query[: 2 * BLK]
        dq1[:, columns] = grad_query[2 * BLK : 4 * BLK].astype(jnp.bfloat16)
        dq2[:, columns] = grad_query[4 * BLK :].astype(jnp.bfloat16)


def weight_body(pairs, parts, count, y_ref, turned, *refs):
    lows, (send, keep) = refs[:parts], refs[parts:]
    tokens = lows[0].shape[0]
    mine = y_ref[0]
    for out, side in ((send, 1 - mine), (keep, mine)):
        for pair in range(pairs):
            first = pl.multiple_of((2 * pair + side) * HS, HS)
            second = pl.multiple_of((count + 2 * pair + side) * HS, HS)
            total = None
            for part, low in enumerate(lows):
                right = jnp.concatenate([low[:, pl.ds(first, HS)], low[:, pl.ds(second, HS)]], axis=1)
                term = nn(turned[:, part * tokens : (part + 1) * tokens], right)
                total = term if total is None else total + term
            out[:, pair * 2 * HS : (pair + 1) * 2 * HS] = total.astype(out.dtype)


def plain_weight_body(parts, turned, *refs):
    lows, out = refs[:parts], refs[parts]
    tokens = lows[0].shape[0]
    for first in range(0, lows[0].shape[1], 2 * HS):
        total = None
        for part, low in enumerate(lows):
            term = nn(turned[:, part * tokens : (part + 1) * tokens], low[:, first : first + 2 * HS])
            total = term if total is None else total + term
        out[:, first : first + 2 * HS] = total


def rows_body(heads, parts, has_base, *refs):
    lows, key_weight, value_weight = refs[:parts], refs[parts], refs[parts + 1]
    bases = refs[parts + 2 : 2 * parts + 2] if has_base else ()
    outs = refs[-parts:]
    width = len(heads) * HS
    if width == HD:
        weights = (key_weight[...], value_weight[...])
    else:
        weights = tuple(
            jnp.concatenate([head_of(w, h) for h in heads], axis=1) for w in (key_weight, value_weight)
        )
    for part, low in enumerate(lows):
        total = nt(low[:, :width], weights[0]) + nt(low[:, width:], weights[1])
        if has_base:
            total = total + bases[part][...]
        outs[part][...] = total.astype(outs[part].dtype)


def chunks_body(places, place_ref, keep, heard, *outs):
    width = 2 * HS
    for index in range(places):
        columns = pl.ds(pl.multiple_of(place_ref[index] * width, width), width)
        value = keep[:, columns] + heard[:, columns].astype(jnp.float32)
        outs[index][...] = value.astype(outs[index].dtype)


def shards(
    inputs, query_rows, saved_key_rows, value_rows, grad_out, key_weight, value_weight, block_pairs, pair_counts
):
    tokens = query_rows.shape[1]
    n_tm, n_fsdp = lax.axis_size("tm"), lax.axis_size("fsdp")
    shard, owner = lax.axis_index("tm"), lax.axis_index("fsdp")
    d_model = inputs.shape[2]
    rows = d_model // n_fsdp
    q, k, v, g = query_rows[0], saved_key_rows[0], value_rows[0], grad_out[0]
    bf16, f32 = jnp.bfloat16, jnp.float32

    def columns_of(array, heads):
        return [array[:, h * HS : (h + 1) * HS] for h in heads] if len(heads) < H else [array]

    halos = []
    for heads in GROUPS:
        packed = jnp.concatenate(columns_of(q, heads) + columns_of(g, heads), axis=1)
        halos.append((shifted(packed, "tm", -1), shifted(packed[:BLK], "tm", -2)))
    table = jnp.concatenate([(block_pairs[0] - shard * QBD).reshape(-1), pair_counts])
    tables = (table, shifted(table, "tm", -1), shifted(table, "tm", -2))

    relative = [(far, flip) for far in range(n_fsdp // 2) for flip in range(2)]
    pieces = []
    for far, flip in relative:
        target = ((owner // 2 - far) % (n_fsdp // 2)) * 2 + (owner % 2 ^ flip)
        piece = lax.dynamic_slice_in_dim(inputs[0], target * rows, rows, 1)
        if far or flip:
            piece = lax.ppermute(piece, "fsdp", rolled_pairs(n_fsdp, far, flip))
        pieces.append(piece.T)
    turned = jnp.concatenate(pieces, axis=1)

    gathered, query_terms = [], []
    for heads, (near, far_rows) in zip(GROUPS, halos):
        count = len(heads)
        width = count * HS
        operands = (*tables, q, k, v, g, near, far_rows)
        height = -(-3 * count // 8) * 8
        own, up1, up2, down1, down2 = kernel_call(
            functools.partial(stats_body, heads),
            [shape((height, n * BLK), f32) for n in (SLOTS, 3, 1, 3, 1)],
            operands,
            scalars=3,
            scratch=[pltpu.VMEM((tokens, SPAN), f32)],
            flops=4 * tokens * SPAN * width,
        )
        stats = (
            own, shifted(up1, "tm", 1), shifted(up2, "tm", 2), shifted(down1, "tm", -1), shifted(down2, "tm", -2)
        )
        low, dq0, dq1, dq2 = kernel_call(
            functools.partial(grads_body, heads),
            [
                shape((tokens, 2 * width), bf16),
                shape((tokens, width), f32),
                shape((tokens, width), bf16),
                shape((BLK, width), bf16),
            ],
            (*operands, *stats),
            scalars=3,
            scratch=[pltpu.VMEM((tokens, SPAN), f32), pltpu.VMEM((3, 8, SPAN), f32)],
            flops=10 * tokens * SPAN * width,
        )
        lows = []
        for far in range(n_fsdp // 2):
            there = low if far == 0 else lax.ppermute(low, "fsdp", rolled_pairs(n_fsdp, far, 0))
            lows += [there, lax.ppermute(there, "fsdp", rolled_pairs(n_fsdp, 0, 1))]
        gathered.append(lows)
        query_terms.append((dq0, shifted(dq1, "tm", 1), shifted(dq2, "tm", 2)))

    column_width = HD // n_tm
    half = n_tm // 2
    key_total = value_total = None
    bases = None
    for index, (heads, lows) in enumerate(zip(GROUPS, gathered)):
        count = len(heads)
        parts = len(lows)
        work = 2 * rows * tokens * parts * 2 * count * HS
        if column_width == HS:
            pairs = count // 2
            send, keep = kernel_call(
                functools.partial(weight_body, pairs, parts, count),
                [shape((rows, count * HS), bf16), shape((rows, count * HS), f32)],
                (jnp.reshape(shard % 2, (1,)), turned, *lows),
                scalars=1,
                flops=work,
            )
            heard = lax.ppermute(send, "tm", rolled_pairs(n_tm, 0, 1))
            goal = [[heads[2 * n + y] // 2 for n in range(pairs)] for y in range(2)]
            routes, places = [], []
            for far in range(half):
                routes.append([(((z + far) % half) * 2 + y, z * 2 + y) for y in range(2) for z in goal[y]])
                lookup = [0] * n_tm
                for y in range(2):
                    for n, z in enumerate(goal[y]):
                        lookup[((z + far) % half) * 2 + y] = n
                places.append(jnp.asarray(lookup, jnp.int32)[shard])
            parcels = kernel_call(
                functools.partial(chunks_body, half),
                [shape((rows, 2 * HS), f32 if far == 0 else bf16) for far in range(half)],
                (jnp.stack(places), keep, heard),
                scalars=1,
            )
            total = parcels[0]
            for far in range(1, half):
                total = total + lax.ppermute(parcels[far], "tm", routes[far]).astype(f32)
            if key_total is None:
                key_total, value_total = total[:, :HS], total[:, HS:]
            else:
                mine = jnp.asarray([any(h == j for h in heads) for j in range(n_tm)])[shard]
                key_total = jnp.where(mine, total[:, :HS], key_total)
                value_total = jnp.where(mine, total[:, HS:], value_total)
        else:
            (partial,) = kernel_call(
                functools.partial(plain_weight_body, parts),
                [shape((rows, 2 * count * HS), f32)],
                (turned, *lows),
                flops=work,
            )
            bases_w = partial if index == 0 else jnp.concatenate([bases_w, partial], axis=1)
        last = index == len(GROUPS) - 1
        bases = kernel_call(
            functools.partial(rows_body, heads, parts, index > 0),
            [shape((tokens, rows), bf16 if last else f32)] * parts,
            (*lows, key_weight, value_weight, *(bases or ())),
            flops=work,
        )
    if column_width != HS:
        order = [h for heads in GROUPS for h in heads]
        starts = []
        for side in range(2):
            found = {}
            base = 0
            for heads in GROUPS:
                for n, h in enumerate(heads):
                    found[h] = base + (side * len(heads) + n) * HS
                base += 2 * len(heads) * HS
            starts.append(found)
        key_total, value_total = (
            lax.psum_scatter(
                jnp.concatenate([bases_w[:, found[h] : found[h] + HS] for h in sorted(order)], axis=1),
                "tm",
                scatter_dimension=1,
                tiled=True,
            )
            for found in starts
        )

    result = jnp.zeros((tokens, d_model), bf16)
    for (far, flip), piece in zip(relative, bases):
        if far or flip:
            routes = [(receiver, sender) for sender, receiver in rolled_pairs(n_fsdp, far, flip)]
            piece = lax.ppermute(piece, "fsdp", routes)
        source = ((owner // 2 - far) % (n_fsdp // 2)) * 2 + (owner % 2 ^ flip)
        result = lax.dynamic_update_slice_in_dim(result, piece, source * rows, 1)

    by_head = [None] * H
    for heads, (dq0, near, far_rows) in zip(GROUPS, query_terms):
        full = dq0 + near.astype(f32)
        full = jnp.concatenate([full[:BLK] + far_rows.astype(f32), full[BLK:]], axis=0).astype(bf16)
        for n, h in enumerate(heads):
            by_head[h] = full[:, n * HS : (n + 1) * HS] if len(heads) < H else full
    grad_query = by_head[0] if len(GROUPS) == 1 else jnp.concatenate(by_head, axis=1)
    return (grad_query[None], result[None], key_total, value_total)


def solution(mesh):
    return jax.shard_map(
        shards,
        mesh=mesh,
        in_specs=(
            P("fsdp", "tm", None),
            P("fsdp", "tm", None),
            P("fsdp", "tm", None),
            P("fsdp", "tm", None),
            P("fsdp", "tm", None),
            P("fsdp", None),
            P("fsdp", None),
            P("tm", None, None),
            P("tm"),
        ),
        out_specs=(P("fsdp", "tm", None), P("fsdp", "tm", None), P("fsdp", "tm"), P("fsdp", "tm")),
        check_vma=False,
    )
```

time: 585 us -> 174 us (0.30)
  waiting for transfers between devices: 426 us -> 92.9 us
  matrix products: 83.3 us -> 0 us
  Pallas kernels: 0 us -> 18.1 us
  local copies, waits for them, and re-layouts: 30.3 us -> 15 us
  between operations: 14.6 us -> 1.67 us
  starting transfers between devices: 21.7 us -> 34 us
    reduce_scatter x3 -> x0, waiting for transfers between devices: 280 us -> none  [the longest x1 145 us: shards(): lax.psum_scatter(jnp.einsum('tr,tc->rc', input_slab, paired_lower_rows, p...]
    dot_general x51 -> x0, matrix products: 83.3 us -> none  [the longest x8 16.7 us: head_terms(): jnp.einsum('qk,qd->kd', weights_low, cotangent_head, preferred_element_ty...]
    all_gather x2 -> x0, waiting for transfers between devices: 60.4 us -> none  [shards(): lax.all_gather((key_weight, value_weight), 'fsdp', axis=0, tiled=True)]
    pallas_call x0 -> x5, Pallas kernels: none -> 18.1 us  [kernel_call(): pl.pallas_call(body, out_shape=tuple(outs), in_specs=[SMEM] * scalars + [...]
    ppermute x8 -> x23, starting transfers between devices: 21.3 us -> 34 us  [the longest x10 24.4 us: shifted(): lax.ppermute(value, axis, [(s, s + steps) for s in range(max(0, -steps),...]
    dynamic_slice x0 -> x9, local copies, waits for them, and re-layouts: none -> 11.9 us  [the longest x5 9.39 us: shards(): piece = lax.dynamic_slice_in_dim(inputs[0], target * rows, rows, 1)]
    ppermute x8 -> x23, waiting for transfers between devices: 83.8 us -> 92.9 us  [the longest x10 38 us: shifted(): lax.ppermute(value, axis, [(s, s + steps) for s in range(max(0, -steps),...]
    unnamed x18 -> x30, local copies, waits for them, and re-layouts: 10.5 us -> 1.89 us
  transfers between devices with their start and end apart: 13 -> 23, of which waited for: 10 -> 9; matrix products, arithmetic and copies ran while one was open for 4% -> 11% of each run, Pallas kernels for 0% -> 5%
where the time goes in v1:
time: 174 us; the launch traced here: 171 us
  waiting for transfers between devices  92.9 us (53%)
  starting transfers between devices  34 us (20%)
  Pallas kernels  18.1 us (10%)
  local copies, waits for them, and re-layouts  15 us (9%)
  other arithmetic  9.34 us (5%)
    ppermute x10, waiting for transfers between devices, shifted(): lax.ppermute(value, axis, [(s, s + steps) for s in range(max(0, -steps),...  38 us
    ppermute x10, starting transfers between devices, shifted(): lax.ppermute(value, axis, [(s, s + steps) for s in range(max(0, -steps),...  24.4 us
    ppermute x1, waiting for transfers between devices, shards(): lax.ppermute(low, 'fsdp', rolled_pairs(n_fsdp, far, 0))  20.7 us
    pallas_call x5, Pallas kernels, kernel_call(): pl.pallas_call(body, out_shape=tuple(outs), in_specs=[SMEM] * scalars + [...  18.1 us
    ppermute x1, waiting for transfers between devices, shards(): heard = lax.ppermute(send, 'tm', rolled_pairs(n_tm, 0, 1))  17.7 us
    ppermute x3, waiting for transfers between devices, shards(): total = total + lax.ppermute(parcels[far], 'tm', routes[far]).astype(f32)  16.4 us
    dynamic_slice x5, local copies, waits for them, and re-layouts, shards(): piece = lax.dynamic_slice_in_dim(inputs[0], target * rows, rows, 1)  9.39 us
    ppermute x3, starting transfers between devices, shards(): total = total + lax.ppermute(parcels[far], 'tm', routes[far]).astype(f32)  3.88 us
  transfers between devices with their start and end apart: 23, of which 9 were waited for; matrix products, arithmetic and copies ran while one was open for 11% of the time, Pallas kernels for 5%

profile of v1, /device:TPU:0, one launch (start us, length us, event | category | flops | bytes accessed | tf_op | source)
XLA Modules:
  0.0 171.0 jit_solution(41977421344263895)
XLA Ops:
  0.7 0.0 copy-start.2
  0.7 0.0 copy-start.4
  0.7 2.4 %pad_maximum_fusion = bf16[256,2048]{1,0:T(8,128)(2,1)} fusion(bf16[256,1024]{1,0:T(8,128)(2,1)} %bitcast.30, bf16[256,1024]{1,0:T(8,128)(2,1)} %bitcast.26), kind=kLoop, calls=%fused_computation.1 | loop fusion | flops 2097152 | bytes 2097152 | tf_op jit(solution)/shard_map/concatenate | solution.py:242
  3.1 1.3 collective-permute-start.2
  4.4 0.8 fusion
  5.2 1.3 collective-permute-start.3
  7.2 0.1 copy.22
  7.3 0.1 sub.29
  7.4 0.1 pad_add_fusion.t0
  7.4 1.4 collective-permute-start
  8.9 1.3 collective-permute-start.1
  10.2 21.2 %collective-permute-done.t1 = s32[17]{0:T(128)S(1)} collective-permute-done((s32[17]{0:T(128)S(1)}, s32[17]{0:T(128)S(1)}, u32[]{:S(2)}, u32[]{:S(2)}) %collective-permute-start) | collective-permute-done | bytes 100 | tf_op jit(solution)/shard_map/ppermute | solution.py:46
  31.4 12.5 %collective-permute-done.1.t2 = s32[17]{0:T(128)S(1)} collective-permute-done((s32[17]{0:T(128)S(1)}, s32[17]{0:T(128)S(1)}, u32[]{:S(2)}, u32[]{:S(2)}) %collective-permute-start.1) | collective-permute-done | bytes 100 | tf_op jit(solution)/shard_map/ppermute | solution.py:46
  43.8 0.0 collective-permute-done.3.far
  43.9 3.3 %shard_map.156 = (f32[24,640]{1,0:T(8,128)S(1)}, f32[24,384]{1,0:T(8,128)S(1)}, f32[24,128]{1,0:T(8,128)S(1)}, f32[24,384]{1,0:T(8,128)S(1)}, f32[24,128]{1,0:T(8,128)S(1)}) custom-call(s32[17]{0:T(128)S(1)} %pad_add_fusion.t0, s32[17]{0:T(128)S(1)} %collective-permute-done.t1, s32[17]{0:T(128)S(1)} %collective-permute-done.1.t2, ...), custom_call_target="tpu_custom_call" | custom-call | flops 671088640 | bytes 3829964 | tf_op jit(solution)/shard_map/pallas_call | solution.py:29
  47.2 3.3 %collective-permute-start.4 = (f32[24,384]{1,0:T(8,128)S(1)}, f32[24,384]{1,0:T(8,128)S(1)}, u32[]{:S(2)}, u32[]{:S(2)}) collective-permute-start(f32[24,384]{1,0:T(8,128)S(1)} %get-tuple-element.24), channel_id=1, source_target_pairs={{0,4},{4,8},{8,12},{12,16},{16,20},{20,24},{24,28},{1,5},{5,9},{9,... | collective-permute-start | bytes 110600 | tf_op jit(solution)/shard_map/ppermute | solution.py:46
  50.4 1.3 collective-permute-start.6
  51.7 5.7 %collective-permute-start.5 = (f32[24,128]{1,0:T(8,128)S(1)}, f32[24,128]{1,0:T(8,128)S(1)}, u32[]{:S(2)}, u32[]{:S(2)}) collective-permute-start(f32[24,128]{1,0:T(8,128)S(1)} %get-tuple-element.25), channel_id=1, source_target_pairs={{0,8},{4,12},{8,16},{12,20},{16,24},{20,28},{1,9},{5,13},{9,17},{1... | collective-permute-start | bytes 36872 | tf_op jit(solution)/shard_map/ppermute | solution.py:46
  57.4 1.3 collective-permute-start.7
  58.7 0.1 collective-permute-done.5.from2
  58.8 4.2 %collective-permute-done.7.back2 = f32[24,128]{1,0:T(8,128)S(1)} collective-permute-done((f32[24,128]{1,0:T(8,128)S(1)}, f32[24,128]{1,0:T(8,128)S(1)}, u32[]{:S(2)}, u32[]{:S(2)}) %collective-permute-start.7) | collective-permute-done | bytes 12320 | tf_op jit(solution)/shard_map/ppermute | solution.py:46
  63.0 0.0 copy-start.3
  63.0 1.0 copy-done.3
  64.1 6.0 %shard_map.157 = (bf16[256,2048]{1,0:T(8,128)(2,1)}, f32[256,1024]{1,0:T(8,128)S(1)}, bf16[256,1024]{1,0:T(8,128)(2,1)S(1)}, bf16[128,1024]{1,0:T(8,128)(2,1)S(1)}) custom-call(s32[17]{0:T(128)S(1)} %pad_add_fusion.t0, s32[17]{0:T(128)S(1)} %collective-permute-done.t1, s32[17]{0:T(128)S(1)} %collective-permute-done.1.t2, bf16[256,1024]{1,0:T(8,128)(2,1)S(1)} %bitcast.29, ...), custom_call_target="tpu_custom_call" | custom-call | flops 1677721600 | bytes 6713548 | tf_op jit(solution)/shard_map/pallas_call | solution.py:29
  70.1 0.8 copy-done.8
  70.9 1.6 collective-permute-start.11
  72.4 20.7 %collective-permute-done.11.refs_2_ = bf16[256,2048]{1,0:T(8,128)(2,1)S(1)} collective-permute-done((bf16[256,2048]{1,0:T(8,128)(2,1)}, bf16[256,2048]{1,0:T(8,128)(2,1)S(1)}, u32[]{:S(2)}, u32[]{:S(2)}) %collective-permute-start.11) | collective-permute-done | bytes 1048608 | tf_op jit(solution)/shard_map/ppermute | solution.py:289
  93.2 2.2 %constant_dynamic-slice_fusion.3 = (bf16[1,256,512]{2,1,0:T(8,128)(2,1)}, bf16[1,256,512]{2,1,0:T(8,128)(2,1)}, bf16[1,256,512]{2,1,0:T(8,128)(2,1)}, bf16[1,256,512]{2,1,0:T(8,128)(2,1)}) fusion(bf16[1,256,2048]{2,1,0:T(8,128)(2,1)} %param.13, s32[]{:T(128)S(6)} %select_n.81, s32[]{:T(128)S(6)} %select_n.82, s32[]{:T(128)S(6)} %select_n.85, s32[]{:T(128)S(6)} %select_n.84), kind=kLoop, calls=%fused_computation.20 | loop fusion | bytes 2097168 | tf_op jit(solution)/shard_map/dynamic_slice | solution.py:251
  95.3 1.8 %copy.26 = bf16[1,256,512]{1,2,0:T(8,128)(2,1)} copy(bf16[1,256,512]{2,1,0:T(8,128)(2,1)} %get-tuple-element.44) | data formatting | bytes 524288 | tf_op jit(solution)/shard_map/dynamic_slice | solution.py:251
  97.2 1.6 collective-permute-start.18
  98.8 3.1 %collective-permute-start.8 = (bf16[256,1024]{1,0:T(8,128)(2,1)}, bf16[256,1024]{1,0:T(8,128)(2,1)}, u32[]{:S(2)}, u32[]{:S(2)}) collective-permute-start(bf16[256,1024]{1,0:T(8,128)(2,1)} %copy-done.8), channel_id=1, source_target_pairs={{0,4},{4,8},{8,12},{12,16},{16,20},{20,24},{24,28},{1,5},{5,9},{9,... | collective-permute-start | bytes 1572872 | tf_op jit(solution)/shard_map/ppermute | solution.py:46
  101.9 1.8 %copy.25 = bf16[1,256,512]{1,2,0:T(8,128)(2,1)} copy(bf16[1,256,512]{2,1,0:T(8,128)(2,1)} %get-tuple-element.45) | data formatting | bytes 524288 | tf_op jit(solution)/shard_map/dynamic_slice | solution.py:251
  103.7 0.5 collective-permute-start.17
  104.2 1.8 %copy.24 = bf16[1,256,512]{1,2,0:T(8,128)(2,1)} copy(bf16[1,256,512]{2,1,0:T(8,128)(2,1)} %get-tuple-element.43) | data formatting | bytes 524288 | tf_op jit(solution)/shard_map/dynamic_slice | solution.py:251
  106.0 0.7 dynamic_slice.35
  106.7 0.6 dynamic_slice.34
  107.3 0.7 dynamic_slice.33
  107.9 0.6 dynamic_slice.32
  108.5 1.8 %copy.23 = bf16[1,256,512]{1,2,0:T(8,128)(2,1)} copy(bf16[1,256,512]{2,1,0:T(8,128)(2,1)} %get-tuple-element.42) | data formatting | bytes 524288 | tf_op jit(solution)/shard_map/dynamic_slice | solution.py:251
  110.3 2.5 %pad_add_fusion.1.place_ref = s32[4]{0:T(128)S(1)} fusion(s32[1]{0:T(128)} %dynamic_slice.35, s32[1]{0:T(128)} %dynamic_slice.34, s32[1]{0:T(128)} %dynamic_slice.33, s32[1]{0:T(128)} %dynamic_slice.32), kind=kLoop, calls=%fused_computation.22 | loop fusion | flops 12 | bytes 32 | tf_op jit(solution)/shard_map/stack | solution.py:324
  112.8 1.3 pad_maximum_fusion.1.turned
  114.2 4.5 %collective-permute-start.9 = (bf16[128,1024]{1,0:T(8,128)(2,1)S(1)}, bf16[128,1024]{1,0:T(8,128)(2,1)S(1)}, u32[]{:S(2)}, u32[]{:S(2)}) collective-permute-start(bf16[128,1024]{1,0:T(8,128)(2,1)S(1)} %get-tuple-element.30), channel_id=1, source_target_pairs={{0,8},{4,12},{8,16},{12,20},{16,24},{20,28},{1,9},{5,13},{9,17},{1... | collective-permute-start | bytes 786440 | tf_op jit(solution)/shard_map/ppermute | solution.py:46
  118.7 1.2 convert_add_fusion
  119.9 0.0 copy-start.6
  119.9 0.0 copy-start.7
  119.9 4.1 %shard_map.159 = (bf16[512,1024]{1,0:T(8,128)(2,1)S(1)}, f32[512,1024]{1,0:T(8,128)S(1)}) custom-call(s32[1]{0:T(128)} %bitcast.10.y_ref, bf16[512,1024]{1,0:T(8,128)(2,1)S(1)} %pad_maximum_fusion.1.turned, bf16[256,2048]{1,0:T(8,128)(2,1)} %get-tuple-element.31.refs_0_, bf16[256,2048]{1,0:T(8,128)(2,1)S(1)} %collective-permute-done.10.refs_1_, ...), custom_call_target="tpu_custom_call" | custom-call | flops 2147483648 | bytes 8388612 | tf_op jit(solution)/shard_map/pallas_call | solution.py:29
  124.0 0.1 collective-permute-start.19
  124.1 0.1 collective-permute-done.9
  124.2 0.1 fusion.2
  124.3 3.9 %shard_map.158 = (bf16[256,512]{1,0:T(8,128)(2,1)S(1)}, bf16[256,512]{1,0:T(8,128)(2,1)S(1)}, bf16[256,512]{1,0:T(8,128)(2,1)S(1)}, bf16[256,512]{1,0:T(8,128)(2,1)S(1)}) custom-call(bf16[256,2048]{1,0:T(8,128)(2,1)} %get-tuple-element.31.refs_0_, bf16[256,2048]{1,0:T(8,128)(2,1)S(1)} %collective-permute-done.10.refs_1_, ...), custom_call_target="tpu_custom_call" | custom-call | flops 2147483648 | bytes 7340032 | tf_op jit(solution)/shard_map/pallas_call | solution.py:29
  128.2 0.1 collective-permute-start.13
  128.3 0.8 pad_maximum_fusion.2
  129.1 1.5 collective-permute-start.14
  130.6 0.4 collective-permute-start.15
  131.0 0.1 broadcast_in_dim.13
  131.2 17.7 %collective-permute-done.19.heard = bf16[512,1024]{1,0:T(8,128)(2,1)S(1)} collective-permute-done((bf16[512,1024]{1,0:T(8,128)(2,1)S(1)}, bf16[512,1024]{1,0:T(8,128)(2,1)S(1)}, u32[]{:S(2)}, u32[]{:S(2)}) %collective-permute-start.19) | collective-permute-done | bytes 1048608 | tf_op jit(solution)/shard_map/ppermute | solution.py:311
  148.9 0.8 shard_map.160
  149.7 0.3 collective-permute-start.22
  150.1 3.5 %collective-permute-start.20 = (bf16[512,256]{1,0:T(8,128)(2,1)S(1)}, bf16[512,256]{1,0:T(8,128)(2,1)S(1)}, u32[]{:S(2)}, u32[]{:S(2)}) collective-permute-start(bf16[512,256]{1,0:T(8,128)(2,1)S(1)} %get-tuple-element.39), channel_id=1, source_target_pairs={{8,0},{16,8},{24,16},{0,24},{12,4},{20,12},{28,20},{4,28},{9,1},{1... | collective-permute-start | bytes 786440 | tf_op jit(solution)/shard_map/ppermute | solution.py:329
  153.7 0.0 copy-start.9
  153.7 7.2 %collective-permute-done.22 = bf16[512,256]{1,0:T(8,128)(2,1)S(1)} collective-permute-done((bf16[512,256]{1,0:T(8,128)(2,1)S(1)}, bf16[512,256]{1,0:T(8,128)(2,1)S(1)}, u32[]{:S(2)}, u32[]{:S(2)}) %collective-permute-start.22) | collective-permute-done | bytes 262176 | tf_op jit(solution)/shard_map/ppermute | solution.py:329
  160.9 9.1 %collective-permute-done.21 = bf16[512,256]{1,0:T(8,128)(2,1)S(1)} collective-permute-done((bf16[512,256]{1,0:T(8,128)(2,1)S(1)}, bf16[512,256]{1,0:T(8,128)(2,1)S(1)}, u32[]{:S(2)}, u32[]{:S(2)}) %collective-permute-start.21) | collective-permute-done | bytes 262176 | tf_op jit(solution)/shard_map/ppermute | solution.py:329
  170.1 0.1 convert_add_fusion.1
  170.2 0.8 fusion.4
  (45 shorter events, 0.2 us)
Async XLA Ops:
  0.6 3.8 %copy-start = (bf16[1,256,1024]{2,1,0:T(8,128)(2,1)S(1)}, bf16[1,256,1024]{2,1,0:T(8,128)(2,1)}, u32[]{:S(2)}) copy-start(bf16[1,256,1024]{2,1,0:T(8,128)(2,1)} %param.14) | copy-start | bytes 1572868
  0.6 3.8 %copy-start.1 = (bf16[1,256,1024]{2,1,0:T(8,128)(2,1)S(1)}, bf16[1,256,1024]{2,1,0:T(8,128)(2,1)}, u32[]{:S(2)}) copy-start(bf16[1,256,1024]{2,1,0:T(8,128)(2,1)} %param.17) | copy-start | bytes 1572868
  0.7 6.5 %copy-start.10 = (s32[1,8,2]{1,2,0:T(2,128)S(1)}, s32[1,8,2]{1,2,0:T(2,128)}, u32[]{:S(2)}) copy-start(s32[1,8,2]{1,2,0:T(2,128)} %param.20) | copy-start | bytes 196
  0.7 43.2 %copy-start.2 = (bf16[1,256,1024]{2,1,0:T(8,128)(2,1)S(1)}, bf16[1,256,1024]{2,1,0:T(8,128)(2,1)}, u32[]{:S(2)}) copy-start(bf16[1,256,1024]{2,1,0:T(8,128)(2,1)} %param.15) | copy-start | bytes 1572868
  0.7 43.2 %copy-start.4 = (bf16[1,256,1024]{2,1,0:T(8,128)(2,1)S(1)}, bf16[1,256,1024]{2,1,0:T(8,128)(2,1)}, u32[]{:S(2)}) copy-start(bf16[1,256,1024]{2,1,0:T(8,128)(2,1)} %param.16) | copy-start | bytes 1572868
  3.1 40.8 %collective-permute-start.2 = (bf16[256,2048]{1,0:T(8,128)(2,1)}, bf16[256,2048]{1,0:T(8,128)(2,1)S(1)}, u32[]{:S(2)}, u32[]{:S(2)}) collective-permute-start(bf16[256,2048]{1,0:T(8,128)(2,1)} %pad_maximum_fusion), channel_id=1, source_target_pairs={{4,0},{8,4},{12,8},{16,12},{20,16},{24,20},{28,24},{5,1},{9,5},{13... | collective-permute-start | bytes 3145736 | tf_op jit(solution)/shard_map/ppermute | solution.py:46
  5.2 38.6 %collective-permute-start.3 = (bf16[128,2048]{1,0:T(8,128)(2,1)}, bf16[128,2048]{1,0:T(8,128)(2,1)}, u32[]{:S(2)}, u32[]{:S(2)}) collective-permute-start(bf16[128,2048]{1,0:T(8,128)(2,1)} %fusion), channel_id=1, source_target_pairs={{8,0},{12,4},{16,8},{20,12},{24,16},{28,20},{9,1},{13,5},{17,9},{2... | collective-permute-start | bytes 1572872 | tf_op jit(solution)/shard_map/ppermute | solution.py:46
  7.4 55.6 %copy-start.5 = (bf16[1,256,1024]{2,1,0:T(8,128)(2,1)S(1)}, bf16[1,256,1024]{2,1,0:T(8,128)(2,1)}, u32[]{:S(2)}) copy-start(bf16[1,256,1024]{2,1,0:T(8,128)(2,1)} %param.16) | copy-start | bytes 1572868
  7.4 23.9 %collective-permute-start = (s32[17]{0:T(128)S(1)}, s32[17]{0:T(128)S(1)}, u32[]{:S(2)}, u32[]{:S(2)}) collective-permute-start(s32[17]{0:T(128)S(1)} %pad_add_fusion.t0), channel_id=1, source_target_pairs={{4,0},{8,4},{12,8},{16,12},{20,16},{24,20},{28,24},{5,1},{9,5},{13... | collective-permute-start | bytes 212 | tf_op jit(solution)/shard_map/ppermute | solution.py:46
  8.9 35.0 %collective-permute-start.1 = (s32[17]{0:T(128)S(1)}, s32[17]{0:T(128)S(1)}, u32[]{:S(2)}, u32[]{:S(2)}) collective-permute-start(s32[17]{0:T(128)S(1)} %pad_add_fusion.t0), channel_id=1, source_target_pairs={{8,0},{12,4},{16,8},{20,12},{24,16},{28,20},{9,1},{13,5},{17,9},{2... | collective-permute-start | bytes 212 | tf_op jit(solution)/shard_map/ppermute | solution.py:46
  47.2 15.8 %collective-permute-start.4 = (f32[24,384]{1,0:T(8,128)S(1)}, f32[24,384]{1,0:T(8,128)S(1)}, u32[]{:S(2)}, u32[]{:S(2)}) collective-permute-start(f32[24,384]{1,0:T(8,128)S(1)} %get-tuple-element.24), channel_id=1, source_target_pairs={{0,4},{4,8},{8,12},{12,16},{16,20},{20,24},{24,28},{1,5},{5,9},{9,... | collective-permute-start | bytes 110600 | tf_op jit(solution)/shard_map/ppermute | solution.py:46
  50.4 12.6 %collective-permute-start.6 = (f32[24,384]{1,0:T(8,128)S(1)}, f32[24,384]{1,0:T(8,128)S(1)}, u32[]{:S(2)}, u32[]{:S(2)}) collective-permute-start(f32[24,384]{1,0:T(8,128)S(1)} %get-tuple-element.26), channel_id=1, source_target_pairs={{4,0},{8,4},{12,8},{16,12},{20,16},{24,20},{28,24},{5,1},{9,5},{13... | collective-permute-start | bytes 110600 | tf_op jit(solution)/shard_map/ppermute | solution.py:46
  51.7 7.1 %collective-permute-start.5 = (f32[24,128]{1,0:T(8,128)S(1)}, f32[24,128]{1,0:T(8,128)S(1)}, u32[]{:S(2)}, u32[]{:S(2)}) collective-permute-start(f32[24,128]{1,0:T(8,128)S(1)} %get-tuple-element.25), channel_id=1, source_target_pairs={{0,8},{4,12},{8,16},{12,20},{16,24},{20,28},{1,9},{5,13},{9,17},{1... | collective-permute-start | bytes 36872 | tf_op jit(solution)/shard_map/ppermute | solution.py:46
  57.4 5.6 %collective-permute-start.7 = (f32[24,128]{1,0:T(8,128)S(1)}, f32[24,128]{1,0:T(8,128)S(1)}, u32[]{:S(2)}, u32[]{:S(2)}) collective-permute-start(f32[24,128]{1,0:T(8,128)S(1)} %get-tuple-element.27), channel_id=1, source_target_pairs={{8,0},{12,4},{16,8},{20,12},{24,16},{28,20},{9,1},{13,5},{17,9},{2... | collective-permute-start | bytes 36872 | tf_op jit(solution)/shard_map/ppermute | solution.py:46
  63.0 1.0 copy-start.3
  70.1 0.8 copy-start.8
  70.8 35.2 %copy-start.14 = (s32[8]{0:T(128)S(1)}, s32[8]{0:T(128)}, u32[]{:S(2)}) copy-start(s32[8]{0:T(128)} %constant.115.clone) | copy-start | bytes 100
  70.8 35.8 %copy-start.13 = (s32[8]{0:T(128)S(1)}, s32[8]{0:T(128)}, u32[]{:S(2)}) copy-start(s32[8]{0:T(128)} %constant.114.clone) | copy-start | bytes 100
  70.8 36.4 %copy-start.12 = (s32[8]{0:T(128)S(1)}, s32[8]{0:T(128)}, u32[]{:S(2)}) copy-start(s32[8]{0:T(128)} %constant.113.clone) | copy-start | bytes 100
  70.9 37.1 %copy-start.11 = (s32[8]{0:T(128)S(1)}, s32[8]{0:T(128)}, u32[]{:S(2)}) copy-start(s32[8]{0:T(128)} %constant.112.clone) | copy-start | bytes 100
  70.9 22.3 %collective-permute-start.11 = (bf16[256,2048]{1,0:T(8,128)(2,1)}, bf16[256,2048]{1,0:T(8,128)(2,1)S(1)}, u32[]{:S(2)}, u32[]{:S(2)}) collective-permute-start(bf16[256,2048]{1,0:T(8,128)(2,1)} %get-tuple-element.31.refs_0_), channel_id=1, source_target_pairs={{2,0},{3,1},{0,2},{1,3},{6,4},{7,5},{4,6},{5,7},{10,8},{11,9},{8,1... | collective-permute-start | bytes 3145736 | tf_op jit(solution)/shard_map/ppermute | solution.py:289
  72.4 47.5 %collective-permute-start.10 = (bf16[256,2048]{1,0:T(8,128)(2,1)}, bf16[256,2048]{1,0:T(8,128)(2,1)S(1)}, u32[]{:S(2)}, u32[]{:S(2)}) collective-permute-start(bf16[256,2048]{1,0:T(8,128)(2,1)} %get-tuple-element.31.refs_0_), channel_id=1, source_target_pairs={{1,0},{0,1},{3,2},{2,3},{5,4},{4,5},{7,6},{6,7},{9,8},{8,9},{11,10... | collective-permute-start | bytes 3145736 | tf_op jit(solution)/shard_map/ppermute | solution.py:290
  93.2 26.7 %collective-permute-start.12 = (bf16[256,2048]{1,0:T(8,128)(2,1)S(1)}, bf16[256,2048]{1,0:T(8,128)(2,1)}, u32[]{:S(2)}, u32[]{:S(2)}) collective-permute-start(bf16[256,2048]{1,0:T(8,128)(2,1)S(1)} %collective-permute-done.11.refs_2_), channel_id=1, source_target_pairs={{1,0},{0,1},{3,2},{2,3},{5,4},{4,5},{7,6},{6,7},{9,8},{8,9},{11,10... | collective-permute-start | bytes 3145736 | tf_op jit(solution)/shard_map/ppermute | solution.py:290
  97.2 8.9 %collective-permute-start.18 = (bf16[256,512]{0,1:T(8,128)(2,1)}, bf16[256,512]{0,1:T(8,128)(2,1)}, u32[]{:S(2)}, u32[]{:S(2)}) collective-permute-start(bf16[256,512]{0,1:T(8,128)(2,1)} %bitcast.41), channel_id=1, source_target_pairs={{3,0},{2,1},{1,2},{0,3},{7,4},{6,5},{5,6},{4,7},{11,8},{10,9},{9,1... | collective-permute-start | bytes 786440 | tf_op jit(solution)/shard_map/ppermute | solution.py:253
  98.8 19.9 %collective-permute-start.8 = (bf16[256,1024]{1,0:T(8,128)(2,1)}, bf16[256,1024]{1,0:T(8,128)(2,1)}, u32[]{:S(2)}, u32[]{:S(2)}) collective-permute-start(bf16[256,1024]{1,0:T(8,128)(2,1)} %copy-done.8), channel_id=1, source_target_pairs={{0,4},{4,8},{8,12},{12,16},{16,20},{20,24},{24,28},{1,5},{5,9},{9,... | collective-permute-start | bytes 1572872 | tf_op jit(solution)/shard_map/ppermute | solution.py:46
  103.7 9.1 %collective-permute-start.17 = (bf16[256,512]{0,1:T(8,128)(2,1)}, bf16[256,512]{0,1:T(8,128)(2,1)}, u32[]{:S(2)}, u32[]{:S(2)}) collective-permute-start(bf16[256,512]{0,1:T(8,128)(2,1)} %bitcast.39), channel_id=1, source_target_pairs={{2,0},{3,1},{0,2},{1,3},{6,4},{7,5},{4,6},{5,7},{10,8},{11,9},{8,1... | collective-permute-start | bytes 786440 | tf_op jit(solution)/shard_map/ppermute | solution.py:253
  106.0 6.8 %collective-permute-start.16 = (bf16[256,512]{0,1:T(8,128)(2,1)}, bf16[256,512]{0,1:T(8,128)(2,1)}, u32[]{:S(2)}, u32[]{:S(2)}) collective-permute-start(bf16[256,512]{0,1:T(8,128)(2,1)} %bitcast.40), channel_id=1, source_target_pairs={{1,0},{0,1},{3,2},{2,3},{5,4},{4,5},{7,6},{6,7},{9,8},{8,9},{11,10... | collective-permute-start | bytes 786440 | tf_op jit(solution)/shard_map/ppermute | solution.py:253
  114.2 10.0 %collective-permute-start.9 = (bf16[128,1024]{1,0:T(8,128)(2,1)S(1)}, bf16[128,1024]{1,0:T(8,128)(2,1)S(1)}, u32[]{:S(2)}, u32[]{:S(2)}) collective-permute-start(bf16[128,1024]{1,0:T(8,128)(2,1)S(1)} %get-tuple-element.30), channel_id=1, source_target_pairs={{0,8},{4,12},{8,16},{12,20},{16,24},{20,28},{1,9},{5,13},{9,17},{1... | collective-permute-start | bytes 786440 | tf_op jit(solution)/shard_map/ppermute | solution.py:46
  119.9 4.4 %copy-start.6 = (bf16[512,1024]{1,0:T(8,128)(2,1)S(1)}, bf16[512,1024]{1,0:T(8,128)(2,1)}, u32[]{:S(2)}) copy-start(bf16[512,1024]{1,0:T(8,128)(2,1)} %refs_4_.1) | copy-start | bytes 3145732
  119.9 4.4 %copy-start.7 = (bf16[512,1024]{1,0:T(8,128)(2,1)S(1)}, bf16[512,1024]{1,0:T(8,128)(2,1)}, u32[]{:S(2)}) copy-start(bf16[512,1024]{1,0:T(8,128)(2,1)} %refs_5_.1) | copy-start | bytes 3145732
  124.0 24.9 %collective-permute-start.19 = (bf16[512,1024]{1,0:T(8,128)(2,1)S(1)}, bf16[512,1024]{1,0:T(8,128)(2,1)S(1)}, u32[]{:S(2)}, u32[]{:S(2)}) collective-permute-start(bf16[512,1024]{1,0:T(8,128)(2,1)S(1)} %get-tuple-element.37), channel_id=1, source_target_pairs={{4,0},{0,4},{12,8},{8,12},{20,16},{16,20},{28,24},{24,28},{5,1},{1... | collective-permute-start | bytes 3145736 | tf_op jit(solution)/shard_map/ppermute | solution.py:311
  128.2 2.9 %collective-permute-start.13 = (bf16[256,512]{1,0:T(8,128)(2,1)S(1)}, bf16[256,512]{1,0:T(8,128)(2,1)S(1)}, u32[]{:S(2)}, u32[]{:S(2)}) collective-permute-start(bf16[256,512]{1,0:T(8,128)(2,1)S(1)} %get-tuple-element.33), channel_id=1, source_target_pairs={{0,1},{1,0},{2,3},{3,2},{4,5},{5,4},{6,7},{7,6},{8,9},{9,8},{10,11... | collective-permute-start | bytes 786440 | tf_op jit(solution)/shard_map/ppermute | solution.py:376
  129.1 24.5 %collective-permute-start.14 = (bf16[256,512]{1,0:T(8,128)(2,1)S(1)}, bf16[256,512]{1,0:T(8,128)(2,1)S(1)}, u32[]{:S(2)}, u32[]{:S(2)}) collective-permute-start(bf16[256,512]{1,0:T(8,128)(2,1)S(1)} %get-tuple-element.34), channel_id=1, source_target_pairs={{0,2},{1,3},{2,0},{3,1},{4,6},{5,7},{6,4},{7,5},{8,10},{9,11},{10,... | collective-permute-start | bytes 786440 | tf_op jit(solution)/shard_map/ppermute | solution.py:376
  130.6 23.0 %collective-permute-start.15 = (bf16[256,512]{1,0:T(8,128)(2,1)S(1)}, bf16[256,512]{1,0:T(8,128)(2,1)S(1)}, u32[]{:S(2)}, u32[]{:S(2)}) collective-permute-start(bf16[256,512]{1,0:T(8,128)(2,1)S(1)} %get-tuple-element.35), channel_id=1, source_target_pairs={{0,3},{1,2},{2,1},{3,0},{4,7},{5,6},{6,5},{7,4},{8,11},{9,10},{10,... | collective-permute-start | bytes 786440 | tf_op jit(solution)/shard_map/ppermute | solution.py:376
  149.7 11.2 %collective-permute-start.22 = (bf16[512,256]{1,0:T(8,128)(2,1)S(1)}, bf16[512,256]{1,0:T(8,128)(2,1)S(1)}, u32[]{:S(2)}, u32[]{:S(2)}) collective-permute-start(bf16[512,256]{1,0:T(8,128)(2,1)S(1)} %get-tuple-element.41), channel_id=1, source_target_pairs={{24,0},{0,8},{8,16},{16,24},{28,4},{4,12},{12,20},{20,28},{25,1},{... | collective-permute-start | bytes 786440 | tf_op jit(solution)/shard_map/ppermute | solution.py:329
  150.1 20.0 %collective-permute-start.21 = (bf16[512,256]{1,0:T(8,128)(2,1)S(1)}, bf16[512,256]{1,0:T(8,128)(2,1)S(1)}, u32[]{:S(2)}, u32[]{:S(2)}) collective-permute-start(bf16[512,256]{1,0:T(8,128)(2,1)S(1)} %get-tuple-element.40), channel_id=1, source_target_pairs={{16,0},{24,8},{0,16},{8,24},{20,4},{28,12},{4,20},{12,28},{17,1},{... | collective-permute-start | bytes 786440 | tf_op jit(solution)/shard_map/ppermute | solution.py:329
  150.1 20.0 %collective-permute-start.20 = (bf16[512,256]{1,0:T(8,128)(2,1)S(1)}, bf16[512,256]{1,0:T(8,128)(2,1)S(1)}, u32[]{:S(2)}, u32[]{:S(2)}) collective-permute-start(bf16[512,256]{1,0:T(8,128)(2,1)S(1)} %get-tuple-element.39), channel_id=1, source_target_pairs={{8,0},{16,8},{24,16},{0,24},{12,4},{20,12},{28,20},{4,28},{9,1},{1... | collective-permute-start | bytes 786440 | tf_op jit(solution)/shard_map/ppermute | solution.py:329
  153.7 17.3 %copy-start.9 = (bf16[1,256,2048]{2,1,0:T(8,128)(2,1)}, bf16[1,256,2048]{2,1,0:T(8,128)(2,1)S(1)}, u32[]{:S(2)}) copy-start(bf16[1,256,2048]{2,1,0:T(8,128)(2,1)S(1)} %bitcast_dynamic-update-slice_fusion) | copy-start | bytes 3145732

commit v2 on v0

v2 whole, which is shorter than its diff:
```python
import functools

import jax
import jax.numpy as jnp
from jax import lax
from jax.experimental import pallas as pl
from jax.experimental.pallas import tpu as pltpu
from jax.sharding import PartitionSpec as P

H = 8
HS = 128
BLK = 128
HD = 1024
QBD = 2
REACH = 2
MAXP = 8
WB = 4
SLOTS = QBD + WB - 1
RULES = 16
VMEM_LIMIT = 24 * 1024 * 1024
SPAN = SLOTS * BLK
LOWEST = -1e29
MASKED = -1e30
SCALE = HS ** (-0.5)
VMEM = pl.BlockSpec(memory_space=pltpu.VMEM)
SMEM = pl.BlockSpec(memory_space=pltpu.SMEM)
ANY = pl.BlockSpec(memory_space=pl.ANY)


def kernel_call(body, outs, operands, scalars=0, after=(), scratch=()):
    count = len(operands)

    def run(*refs):
        body(*refs[:count], *refs[count + len(after) :])

    return pl.pallas_call(
        run,
        out_shape=tuple(outs),
        in_specs=[SMEM] * scalars + [VMEM] * (count - scalars) + [ANY] * len(after),
        out_specs=tuple([VMEM] * len(outs)),
        scratch_shapes=list(scratch),
        compiler_params=pltpu.CompilerParams(vmem_limit_bytes=VMEM_LIMIT),
        cost_estimate=pl.CostEstimate(flops=0, bytes_accessed=0, transcendentals=0),
    )(*operands, *after)


def copy_body(value, out):
    out[...] = value[...]


def held(value, *others):
    (copy,) = kernel_call(copy_body, [shape(value.shape, value.dtype)], (value,), after=others)
    return copy


def shape(dims, kind):
    return jax.ShapeDtypeStruct(dims, kind)


def shifted(value, axis, steps):
    count = lax.axis_size(axis)
    return lax.ppermute(
        value, axis, [(s, s + steps) for s in range(max(0, -steps), min(count, count - steps))]
    )


def rolled_pairs(count, far, flip):
    half = count // 2
    return [(((a + far) % half) * 2 + (b ^ flip), a * 2 + b) for a in range(half) for b in range(2)]


def nt(left, right):
    return lax.dot_general(left, right, (((1,), (1,)), ((), ())), preferred_element_type=jnp.float32)


def tn(left, right):
    return lax.dot_general(left, right, (((0,), (0,)), ((), ())), preferred_element_type=jnp.float32)


def nn(left, right):
    return jnp.dot(left, right, preferred_element_type=jnp.float32)


def rules_body(pairs, counts, rules):
    base = lax.axis_index("tm") * QBD
    numbers = lax.broadcasted_iota(jnp.int32, (RULES, BLK), 0)
    values = jnp.zeros((RULES, BLK), jnp.float32)
    for query in range(QBD):
        for back in range(WB):
            hit = jnp.int32(0)
            for row in range(MAXP):
                same = (pairs[row, 0] == base + query) & (pairs[row, 1] == base + query - back)
                hit = hit + jnp.where(same & (row < counts[0]), 1, 0)
            value = jnp.where(hit > 0, 0.0, MASKED).astype(jnp.float32)
            values = jnp.where(numbers == query * WB + back, value, values)
    rules[...] = values


def fill_bias(sets, bias):
    rows = lax.broadcasted_iota(jnp.int32, (BLK, BLK), 0)
    columns = lax.broadcasted_iota(jnp.int32, (BLK, BLK), 1)
    for key in range(QBD):
        for slot in range(SLOTS):
            place = (pl.ds(key * BLK, BLK), pl.ds(slot * BLK, BLK))
            back = slot - key
            if not 0 <= back < WB:
                bias[place] = jnp.full((BLK, BLK), MASKED, jnp.float32)
                continue
            line = (slot % QBD) * WB + back
            block = jnp.broadcast_to(sets[slot // QBD][line : line + 1, :], (BLK, BLK))
            if slot == key:
                block = jnp.where(rows <= columns, block, MASKED)
            bias[place] = block


def head_of(ref, place):
    return ref[:, place * HS : (place + 1) * HS]


def rows_of(own, halo, head, place):
    even, odd, swap, relay, far, flag = halo
    first = head_of(even, place) + head_of(odd, place)
    second = head_of(swap, place) * flag + head_of(relay, place)
    return jnp.concatenate([head_of(own, head), first, second, head_of(far, place)], axis=0)


def halo_of(refs):
    flag = jnp.where(lax.axis_index("tm") % 2 == 0, 1.0, 0.0).astype(jnp.bfloat16)
    return (*refs, flag)


def stats_body(rules, rules1, rules2, q, k, v, g, even, odd, swap, relay, far, own, bias):
    halo = halo_of((even, odd, swap, relay, far))
    fill_bias((rules, rules1, rules2), bias)
    for h in range(H):
        scores = nt(head_of(k, h), rows_of(q, halo, h, h)) * SCALE + bias[...]
        products = nt(head_of(v, h), rows_of(g, halo, h, H + h))
        largest = jnp.maximum(jnp.max(scores, axis=0, keepdims=True), LOWEST)
        weights = jnp.exp(scores - largest)
        own[h : h + 1, :] = largest
        own[H + h : H + h + 1, :] = jnp.sum(weights, axis=0, keepdims=True)
        own[2 * H + h : 2 * H + h + 1, :] = jnp.sum(weights * products, axis=0, keepdims=True)


def spread_body(own, pair, up, down):
    up[:, :BLK] = own[:, 4 * BLK :]
    up[:, BLK:] = pair[:, 2 * BLK :]
    down[:, :BLK] = own[:, :BLK]
    down[:, BLK:] = pair[:, : 3 * BLK]


def merge_stats(own, pair, up, down):
    is_even = lax.axis_index("tm") % 2 == 0

    def terms(ref, first, last):
        part = ref[:, first * BLK : last * BLK]
        large, mass, dot = (part[i * H : (i + 1) * H] for i in range(3))
        return jnp.where(mass > 0, large, LOWEST), mass, dot

    def either(first, second):
        return tuple(jnp.where(is_even, a, b) for a, b in zip(first, second))

    nothing = (
        jnp.full((H, BLK), LOWEST, jnp.float32),
        jnp.zeros((H, BLK), jnp.float32),
        jnp.zeros((H, BLK), jnp.float32),
    )

    def side(*parts):
        return tuple(jnp.concatenate(piece, axis=1) for piece in zip(*parts))

    def cut(part, first, last):
        return tuple(piece[:, first * BLK : last * BLK] for piece in part)

    before = either(terms(up, 1, 4), terms(pair, 2, 5))
    behind = either(terms(pair, 0, 3), terms(down, 1, 4))
    sets = (
        terms(own, 0, SLOTS),
        side(before, cut(behind, 1, 3)),
        side(terms(up, 0, 1), nothing, cut(behind, 0, 1), nothing, terms(down, 0, 1)),
    )
    largest = jnp.maximum(jnp.maximum(sets[0][0], sets[1][0]), sets[2][0])
    mass = jnp.zeros((H, SPAN), jnp.float32)
    dot = jnp.zeros((H, SPAN), jnp.float32)
    for large, part_mass, part_dot in sets:
        factor = jnp.exp(large - largest)
        mass = mass + factor * part_mass
        dot = dot + factor * part_dot
    inverse = jnp.where(mass > 0, 1.0 / jnp.where(mass > 0, mass, 1.0), 0.0)
    return largest, inverse, dot * inverse


def values_body(
    rules, rules1, rules2, q, k, g, even, odd, swap, relay, far, own, pair, up, down, low, total, bias
):
    halo = halo_of((even, odd, swap, relay, far))
    fill_bias((rules, rules1, rules2), bias)
    for index, value in enumerate(merge_stats(own, pair, up, down)):
        total[index * H : (index + 1) * H] = value
    for h in range(H):
        scores = nt(head_of(k, h), rows_of(q, halo, h, h)) * SCALE + bias[...]
        probs = jnp.exp(scores - total[h : h + 1, :]) * total[H + h : H + h + 1, :]
        value_grads = nn(probs.astype(jnp.bfloat16), rows_of(g, halo, h, H + h))
        low[:, h * HS : (h + 1) * HS] = value_grads.astype(jnp.bfloat16)


def keys_body(rules, rules1, rules2, q, k, v, g, even, odd, swap, relay, far, total, low, dq0, dq1, dq2, bias):
    halo = halo_of((even, odd, swap, relay, far))
    fill_bias((rules, rules1, rules2), bias)
    for h in range(H):
        query = rows_of(q, halo, h, h)
        key = head_of(k, h)
        scores = nt(key, query) * SCALE + bias[...]
        products = nt(head_of(v, h), rows_of(g, halo, h, H + h))
        probs = jnp.exp(scores - total[h : h + 1, :]) * total[H + h : H + h + 1, :]
        grad_scores = (probs * (products - total[2 * H + h : 2 * H + h + 1, :])).astype(jnp.bfloat16)
        columns = slice(h * HS, (h + 1) * HS)
        low[:, columns] = (nn(grad_scores, query) * SCALE).astype(jnp.bfloat16)
        grad_query = tn(grad_scores, key) * SCALE
        dq0[:, columns] = grad_query[: 2 * BLK]
        dq1[:, columns] = grad_query[2 * BLK : 4 * BLK].astype(jnp.bfloat16)
        dq2[:, columns] = grad_query[4 * BLK :].astype(jnp.bfloat16)


def cut_body(width, parts, targets, x, *outs):
    for index in range(parts):
        first = pl.multiple_of(targets[index] * width, width)
        outs[index][...] = x[:, pl.ds(first, width)].T


def weight_body(half, parts, y_ref, *refs):
    turned, lows, (send, keep) = refs[:parts], refs[parts : 2 * parts], refs[2 * parts :]
    mine = y_ref[0]
    for out, side in ((send, 1 - mine), (keep, mine)):
        for z in range(0, half, 2):
            places = [pl.ds(pl.multiple_of((2 * place + side) * HS, HS), HS) for place in (z, z + 1)]
            total = None
            for left, low in zip(turned, lows):
                term = nn(left[...], jnp.concatenate([low[:, place] for place in places], axis=1))
                total = term if total is None else total + term
            out[:, z * HS : (z + 2) * HS] = total.astype(out.dtype)


def plain_weight_body(parts, *refs):
    turned, lows, out = refs[:parts], refs[parts : 2 * parts], refs[-1]
    for first in range(0, HD, 2 * HS):
        total = None
        for left, low in zip(turned, lows):
            term = nn(left[...], low[:, first : first + 2 * HS])
            total = term if total is None else total + term
        out[:, first : first + 2 * HS] = total


def rows_body(parts, *refs):
    key_lows, value_lows = refs[:parts], refs[parts : 2 * parts]
    key_weight, value_weight = refs[2 * parts : 2 * parts + 2]
    for key_low, value_low, out in zip(key_lows, value_lows, refs[-parts:]):
        out[...] = (nt(key_low[...], key_weight[...]) + nt(value_low[...], value_weight[...])).astype(out.dtype)


def chunks_body(count, place_ref, keep, heard, *outs):
    for index in range(count):
        columns = pl.ds(pl.multiple_of(place_ref[index] * HS, HS), HS)
        value = keep[:, columns] + heard[:, columns].astype(jnp.float32)
        outs[index][...] = value.astype(outs[index].dtype)


def shards(
    inputs, query_rows, saved_key_rows, value_rows, grad_out, key_weight, value_weight, block_pairs, pair_counts
):
    tokens = query_rows.shape[1]
    n_tm, n_fsdp = lax.axis_size("tm"), lax.axis_size("fsdp")
    shard, owner = lax.axis_index("tm"), lax.axis_index("fsdp")
    d_model = inputs.shape[2]
    rows = d_model // n_fsdp
    half = n_tm // 2
    q, k, v, g = query_rows[0], saved_key_rows[0], value_rows[0], grad_out[0]
    bf16, f32 = jnp.bfloat16, jnp.float32

    first = jnp.concatenate([q[:BLK], g[:BLK]], axis=1)
    latter = jnp.concatenate([q[BLK:], g[BLK:]], axis=1)
    far = shifted(first, "tm", -2)
    swap = lax.ppermute(latter, "tm", rolled_pairs(n_tm, 0, 1))
    even = lax.ppermute(first, "tm", [(2 * z + 1, 2 * z) for z in range(half)])
    (rules,) = kernel_call(rules_body, [shape((RULES, BLK), f32)], (block_pairs[0], pair_counts), scalars=2)
    rules = (rules, shifted(rules, "tm", -1), shifted(rules, "tm", -2))

    relative = [(away, flip) for away in range(n_fsdp // 2) for flip in range(2)]
    parts = len(relative)
    others = [((owner // 2 - away) % (n_fsdp // 2)) * 2 + (owner % 2 ^ flip) for away, flip in relative]
    turned = kernel_call(
        functools.partial(cut_body, rows, parts),
        [shape((rows, tokens), bf16)] * parts,
        (jnp.stack(others), inputs[0]),
        scalars=1,
    )
    turned = [
        lax.ppermute(piece, "fsdp", rolled_pairs(n_fsdp, *place)) if any(place) else piece
        for place, piece in zip(relative, turned)
    ]
    far = held(far, *turned, *rules)
    odd = lax.ppermute(far, "tm", [(2 * z, 2 * z + 1) for z in range(half)])
    relay = lax.ppermute(swap, "tm", [(2 * z + 3, 2 * z + 1) for z in range(half - 1)])

    halo = (even, odd, swap, relay, far)
    bias = pltpu.VMEM((tokens, SPAN), f32)
    (own,) = kernel_call(
        stats_body,
        [shape((3 * H, SPAN), f32)],
        (*rules, q, k, v, g, *halo),
        scratch=[bias],
    )
    pair = lax.ppermute(own, "tm", rolled_pairs(n_tm, 0, 1))
    up, down = kernel_call(spread_body, [shape((3 * H, 4 * BLK), f32)] * 2, (own, pair))
    up, down = shifted(up, "tm", 2), shifted(down, "tm", -2)
    value_low, total = kernel_call(
        values_body,
        [shape((tokens, HD), bf16), shape((3 * H, SPAN), f32)],
        (*rules, q, k, g, *halo, own, pair, up, down),
        scratch=[bias],
    )

    def exchanged(array):
        return lax.ppermute(array, "fsdp", rolled_pairs(n_fsdp, 0, 1))

    def fetched(array):
        return [lax.ppermute(array, "fsdp", rolled_pairs(n_fsdp, away, 0)) for away in range(1, n_fsdp // 2)]

    value_lows = [value_low, exchanged(value_low)]
    value_far = fetched(value_low)
    key_low, dq0, dq1, dq2 = kernel_call(
        keys_body,
        [shape((tokens, HD), kind) for kind in (bf16, f32, bf16)] + [shape((BLK, HD), bf16)],
        (*rules, q, k, v, g, *halo, total),
        scratch=[bias],
    )
    key_lows = [key_low, exchanged(key_low)]
    key_far = fetched(key_low)
    near_terms, far_terms = shifted(dq1, "tm", 1), shifted(dq2, "tm", 2)
    for array in value_far:
        array = held(array, key_low)
        value_lows += [array, exchanged(array)]

    def partial_sums(lows, after=()):
        if HD // n_tm != HS:
            return kernel_call(
                functools.partial(plain_weight_body, parts),
                [shape((rows, HD), f32)],
                (*turned, *lows),
                after=after,
            )
        return kernel_call(
            functools.partial(weight_body, half, parts),
            [shape((rows, HD // 2), bf16), shape((rows, HD // 2), f32)],
            (jnp.reshape(shard % 2, (1,)), *turned, *lows),
            scalars=1,
            after=after,
        )

    def summed(partial):
        if HD // n_tm != HS:
            return lax.psum_scatter(partial[0], "tm", scatter_dimension=1, tiled=True)
        heard = lax.ppermute(partial[0], "tm", rolled_pairs(n_tm, 0, 1))
        places = jnp.stack([(shard // 2 - away) % half for away in range(half)])
        parcels = kernel_call(
            functools.partial(chunks_body, half),
            [shape((rows, HS), f32 if away == 0 else bf16) for away in range(half)],
            (places, partial[1], heard),
            scalars=1,
        )
        result = parcels[0]
        for away in range(1, half):
            result = result + lax.ppermute(parcels[away], "tm", rolled_pairs(n_tm, away, 0)).astype(f32)
        return result

    value_partial = partial_sums(value_lows)
    for array in key_far:
        array = held(array, value_partial[0], near_terms, far_terms)
        key_lows += [array, exchanged(array)]
    key_partial = partial_sums(key_lows)
    value_total, key_total = summed(value_partial), summed(key_partial)
    pieces = kernel_call(
        functools.partial(rows_body, parts),
        [shape((tokens, rows), bf16)] * parts,
        (*key_lows, *value_lows, key_weight, value_weight),
        after=(key_partial[0],),
    )

    result = jnp.zeros((tokens, d_model), bf16)
    for place, source, piece in zip(relative, others, pieces):
        if any(place):
            routes = [(receiver, sender) for sender, receiver in rolled_pairs(n_fsdp, *place)]
            piece = lax.ppermute(piece, "fsdp", routes)
        result = lax.dynamic_update_slice_in_dim(result, piece, source * rows, 1)

    grad_query = dq0 + near_terms.astype(f32)
    grad_query = jnp.concatenate([grad_query[:BLK] + far_terms.astype(f32), grad_query[BLK:]], axis=0).astype(bf16)
    return (grad_query[None], result[None], key_total, value_total)


def solution(mesh):
    return jax.shard_map(
        shards,
        mesh=mesh,
        in_specs=(
            P("fsdp", "tm", None),
            P("fsdp", "tm", None),
            P("fsdp", "tm", None),
            P("fsdp", "tm", None),
            P("fsdp", "tm", None),
            P("fsdp", None),
            P("fsdp", None),
            P("tm", None, None),
            P("tm"),
        ),
        out_specs=(P("fsdp", "tm", None), P("fsdp", "tm", None), P("fsdp", "tm"), P("fsdp", "tm")),
        check_vma=False,
    )
```

time: 585 us -> 141 us (0.24)
  waiting for transfers between devices: 426 us -> 67.8 us
  matrix products: 83.3 us -> 0 us
  local copies, waits for them, and re-layouts: 30.3 us -> 1.65 us
  Pallas kernels: 0 us -> 21 us
  starting transfers between devices: 21.7 us -> 42.5 us
  between operations: 14.6 us -> 1.73 us
    reduce_scatter x3 -> x0, waiting for transfers between devices: 280 us -> none  [the longest x1 145 us: shards(): lax.psum_scatter(jnp.einsum('tr,tc->rc', input_slab, paired_lower_rows, p...]
    dot_general x51 -> x0, matrix products: 83.3 us -> none  [the longest x8 16.7 us: head_terms(): jnp.einsum('qk,qd->kd', weights_low, cotangent_head, preferred_element_ty...]
    all_gather x2 -> x0, waiting for transfers between devices: 60.4 us -> none  [shards(): lax.all_gather((key_weight, value_weight), 'fsdp', axis=0, tiled=True)]
    ppermute x8 -> x32, starting transfers between devices: 21.3 us -> 42.5 us  [the longest x7 17.5 us: shifted(): lax.ppermute(value, axis, [(s, s + steps) for s in range(max(0, -steps),...]
    pallas_call x0 -> x14, Pallas kernels: none -> 21 us  [kernel_call(): pl.pallas_call(run, out_shape=tuple(outs), in_specs=[SMEM] * scalars + [V...]
    ppermute x8 -> x32, waiting for transfers between devices: 83.8 us -> 67.8 us  [the longest x7 16.8 us: shifted(): lax.ppermute(value, axis, [(s, s + steps) for s in range(max(0, -steps),...]
    unnamed x18 -> x20, local copies, waits for them, and re-layouts: 10.5 us -> 0.04 us
    dynamic_update_slice x16 -> x4, local copies, waits for them, and re-layouts: 7.61 us -> 0.1 us  [shards(): result = lax.dynamic_update_slice_in_dim(result, piece, source * rows, 1)]
  transfers between devices with their start and end apart: 13 -> 32, of which waited for: 10 -> 15; matrix products, arithmetic and copies ran while one was open for 4% -> 3% of each run, Pallas kernels for 0% -> 12%
where the time goes in v2:
time: 141 us; the launch traced here: 140 us
  waiting for transfers between devices  67.8 us (48%)
  starting transfers between devices  42.5 us (30%)
  Pallas kernels  21 us (15%)
  other arithmetic  5.6 us (4%)
  between operations  1.73 us (1%)
  local copies, waits for them, and re-layouts  1.65 us (1%)
    pallas_call x14, Pallas kernels, kernel_call(): pl.pallas_call(run, out_shape=tuple(outs), in_specs=[SMEM] * scalars + [V...  21 us
    ppermute x7, starting transfers between devices, shifted(): lax.ppermute(value, axis, [(s, s + steps) for s in range(max(0, -steps),...  17.5 us
    ppermute x7, waiting for transfers between devices, shifted(): lax.ppermute(value, axis, [(s, s + steps) for s in range(max(0, -steps),...  16.8 us
    ppermute x6, waiting for transfers between devices, summed(): lax.ppermute(parcels[away], 'tm', rolled_pairs(n_tm, away, 0)).astype(f32)  10.8 us
    ppermute x1, waiting for transfers between devices, shards(): odd = lax.ppermute(far, 'tm', [(2 * z, 2 * z + 1) for z in range(half)])  9.27 us
    ppermute x3, waiting for transfers between devices, shards(): lax.ppermute(piece, 'fsdp', rolled_pairs(n_fsdp, *place))  9 us
    ppermute x2, waiting for transfers between devices, summed(): heard = lax.ppermute(partial[0], 'tm', rolled_pairs(n_tm, 0, 1))  8.16 us
    ppermute x6, starting transfers between devices, summed(): lax.ppermute(parcels[away], 'tm', rolled_pairs(n_tm, away, 0)).astype(f32)  7.25 us
  transfers between devices with their start and end apart: 32, of which 15 were waited for; matrix products, arithmetic and copies ran while one was open for 3% of the time, Pallas kernels for 12%

profile of v2, /device:TPU:0, one launch (start us, length us, event | category | flops | bytes accessed | tf_op | source)
XLA Modules:
  0.0 140.3 jit_solution(6150408048341216865)
XLA Ops:
  0.6 1.3 slice_bitcast_fusion
  1.9 0.8 pad_maximum_fusion
  2.8 1.3 collective-permute-start.3
  4.0 0.8 pad_maximum_fusion.1
  4.9 3.0 %collective-permute-start.8 = (bf16[128,2048]{1,0:T(8,128)(2,1)}, bf16[128,2048]{1,0:T(8,128)(2,1)S(1)}, u32[]{:S(2)}, u32[]{:S(2)}) collective-permute-start(bf16[128,2048]{1,0:T(8,128)(2,1)} %pad_maximum_fusion.1), channel_id=1, source_target_pairs={{4,0},{0,4},{12,8},{8,12},{20,16},{16,20},{28,24},{24,28},{5,1},{1... | collective-permute-start | bytes 1572872 | tf_op jit(solution)/shard_map/ppermute | solution.py:283
  7.8 0.1 copy.13.refs_0_
  8.6 0.8 shard_map.120.refs_5_.refs_0_
  9.4 1.3 collective-permute-start
  10.7 1.3 collective-permute-start.1
  12.0 0.1 pad_add_fusion.refs_0_
  12.1 0.9 shard_map.121
  13.0 0.1 collective-permute-start.4
  13.1 7.1 %collective-permute-done.refs_6_.refs_1_ = f32[16,128]{1,0:T(8,128)S(1)} collective-permute-done((f32[16,128]{1,0:T(8,128)S(1)}, f32[16,128]{1,0:T(8,128)S(1)}, u32[]{:S(2)}, u32[]{:S(2)}) %collective-permute-start) | collective-permute-done | bytes 8224 | tf_op jit(solution)/shard_map/ppermute | solution.py:62
  20.2 1.7 %collective-permute-start.5 = (bf16[512,256]{1,0:T(8,128)(2,1)S(1)}, bf16[512,256]{1,0:T(8,128)(2,1)S(1)}, u32[]{:S(2)}, u32[]{:S(2)}) collective-permute-start(bf16[512,256]{1,0:T(8,128)(2,1)S(1)} %get-tuple-element.34), channel_id=1, source_target_pairs={{2,0},{3,1},{0,2},{1,3},{6,4},{7,5},{4,6},{5,7},{10,8},{11,9},{8,1... | collective-permute-start | bytes 786440 | tf_op jit(solution)/shard_map/ppermute | solution.py:298
  21.9 1.3 collective-permute-start.2
  23.2 6.2 %collective-permute-done.5.refs_3_ = bf16[512,256]{1,0:T(8,128)(2,1)S(1)} collective-permute-done((bf16[512,256]{1,0:T(8,128)(2,1)S(1)}, bf16[512,256]{1,0:T(8,128)(2,1)S(1)}, u32[]{:S(2)}, u32[]{:S(2)}) %collective-permute-start.5) | collective-permute-done | bytes 262176 | tf_op jit(solution)/shard_map/ppermute | solution.py:298
  29.4 2.8 %collective-permute-done.6.refs_4_ = bf16[512,256]{1,0:T(8,128)(2,1)S(1)} collective-permute-done((bf16[512,256]{1,0:T(8,128)(2,1)S(1)}, bf16[512,256]{1,0:T(8,128)(2,1)S(1)}, u32[]{:S(2)}, u32[]{:S(2)}) %collective-permute-start.6) | collective-permute-done | bytes 262176 | tf_op jit(solution)/shard_map/ppermute | solution.py:298
  32.2 3.0 %collective-permute-start.7 = (bf16[128,2048]{1,0:T(8,128)(2,1)S(1)}, bf16[128,2048]{1,0:T(8,128)(2,1)S(1)}, u32[]{:S(2)}, u32[]{:S(2)}) collective-permute-start(bf16[128,2048]{1,0:T(8,128)(2,1)S(1)} %shard_map.122.refs_11_.refs_10_), channel_id=1, source_target_pairs={{0,4},{8,12},{16,20},{24,28},{1,5},{9,13},{17,21},{25,29},{2,6},{1... | collective-permute-start | bytes 1572872 | tf_op jit(solution)/shard_map/ppermute | solution.py:302
  35.3 0.7 collective-permute-start.9
  36.0 2.3 %collective-permute-done.2.refs_7_.refs_6_ = bf16[128,2048]{1,0:T(8,128)(2,1)S(1)} collective-permute-done((bf16[128,2048]{1,0:T(8,128)(2,1)}, bf16[128,2048]{1,0:T(8,128)(2,1)S(1)}, u32[]{:S(2)}, u32[]{:S(2)}) %collective-permute-start.2) | collective-permute-done | bytes 524320 | tf_op jit(solution)/shard_map/ppermute | solution.py:284
  38.2 9.3 %collective-permute-done.7.refs_8_.refs_7_ = bf16[128,2048]{1,0:T(8,128)(2,1)S(1)} collective-permute-done((bf16[128,2048]{1,0:T(8,128)(2,1)S(1)}, bf16[128,2048]{1,0:T(8,128)(2,1)S(1)}, u32[]{:S(2)}, u32[]{:S(2)}) %collective-permute-start.7) | collective-permute-done | bytes 524320 | tf_op jit(solution)/shard_map/ppermute | solution.py:302
  47.5 2.4 %shard_map.123.refs_0_.refs_11_ = f32[24,640]{1,0:T(8,128)S(1)} custom-call(f32[16,128]{1,0:T(8,128)S(1)} %shard_map.120.refs_5_.refs_0_, f32[16,128]{1,0:T(8,128)S(1)} %collective-permute-done.refs_6_.refs_1_, f32[16,128]{1,0:T(8,128)S(1)} %collective-permute-done.1.refs_7_.refs_2_, bf16[256,1024]{1,0:T(8,128)(2,1)S(1)} %bitcast.35, ...), custom_call_target="tpu_custom_call" | custom-call | tf_op jit(solution)/shard_map/pallas_call | solution.py:36
  49.9 3.8 %collective-permute-start.10 = (f32[24,640]{1,0:T(8,128)S(1)}, f32[24,640]{1,0:T(8,128)S(1)}, u32[]{:S(2)}, u32[]{:S(2)}) collective-permute-start(f32[24,640]{1,0:T(8,128)S(1)} %shard_map.123.refs_0_.refs_11_), channel_id=1, source_target_pairs={{4,0},{0,4},{12,8},{8,12},{20,16},{16,20},{28,24},{24,28},{5,1},{1... | collective-permute-start | bytes 184328 | tf_op jit(solution)/shard_map/ppermute | solution.py:313
  53.8 2.3 %collective-permute-done.10.refs_1_.refs_12_ = f32[24,640]{1,0:T(8,128)S(1)} collective-permute-done((f32[24,640]{1,0:T(8,128)S(1)}, f32[24,640]{1,0:T(8,128)S(1)}, u32[]{:S(2)}, u32[]{:S(2)}) %collective-permute-start.10) | collective-permute-done | bytes 61472 | tf_op jit(solution)/shard_map/ppermute | solution.py:313
  56.1 3.3 %collective-permute-start.11 = (f32[24,512]{1,0:T(8,128)S(1)}, f32[24,512]{1,0:T(8,128)S(1)}, u32[]{:S(2)}, u32[]{:S(2)}) collective-permute-start(f32[24,512]{1,0:T(8,128)S(1)} %get-tuple-element.36), channel_id=1, source_target_pairs={{0,8},{4,12},{8,16},{12,20},{16,24},{20,28},{1,9},{5,13},{9,17},{1... | collective-permute-start | bytes 147464 | tf_op jit(solution)/shard_map/ppermute | solution.py:62
  59.3 1.3 collective-permute-start.12
  60.6 0.4 collective-permute-done.11.refs_13_
  61.1 4.3 %collective-permute-done.12.refs_14_ = f32[24,512]{1,0:T(8,128)S(1)} collective-permute-done((f32[24,512]{1,0:T(8,128)S(1)}, f32[24,512]{1,0:T(8,128)S(1)}, u32[]{:S(2)}, u32[]{:S(2)}) %collective-permute-start.12) | collective-permute-done | bytes 49184 | tf_op jit(solution)/shard_map/ppermute | solution.py:62
  65.3 2.4 %shard_map.125 = (bf16[256,1024]{1,0:T(8,128)(2,1)S(1)}, f32[24,640]{1,0:T(8,128)S(1)}) custom-call(f32[16,128]{1,0:T(8,128)S(1)} %shard_map.120.refs_5_.refs_0_, f32[16,128]{1,0:T(8,128)S(1)} %collective-permute-done.refs_6_.refs_1_, f32[16,128]{1,0:T(8,128)S(1)} %collective-permute-done.1.refs_7_.refs_2_, bf16[256,1024]{1,0:T(8,128)(2,1)S(1)} %bitcast.36, ...), custom_call_target="tpu_custom_call" | custom-call | tf_op jit(solution)/shard_map/pallas_call | solution.py:36
  67.7 0.5 collective-permute-start.18
  68.2 4.5 %shard_map.126 = (bf16[256,1024]{1,0:T(8,128)(2,1)S(1)}, f32[256,1024]{1,0:T(8,128)S(1)}, bf16[256,1024]{1,0:T(8,128)(2,1)}, bf16[128,1024]{1,0:T(8,128)(2,1)S(1)}) custom-call(f32[16,128]{1,0:T(8,128)S(1)} %shard_map.120.refs_5_.refs_0_, f32[16,128]{1,0:T(8,128)S(1)} %collective-permute-done.refs_6_.refs_1_, ...), custom_call_target="tpu_custom_call" | custom-call | tf_op jit(solution)/shard_map/pallas_call | solution.py:36
  72.7 3.7 %collective-permute-start.13 = (bf16[256,1024]{1,0:T(8,128)(2,1)}, bf16[256,1024]{1,0:T(8,128)(2,1)S(1)}, u32[]{:S(2)}, u32[]{:S(2)}) collective-permute-start(bf16[256,1024]{1,0:T(8,128)(2,1)} %get-tuple-element.40), channel_id=1, source_target_pairs={{0,4},{4,8},{8,12},{12,16},{16,20},{20,24},{24,28},{1,5},{5,9},{9,... | collective-permute-start | bytes 1572872 | tf_op jit(solution)/shard_map/ppermute | solution.py:62
  76.4 0.1 collective-permute-start.17
  76.5 2.8 %collective-permute-done.18.refs_0_ = bf16[256,1024]{1,0:T(8,128)(2,1)S(1)} collective-permute-done((bf16[256,1024]{1,0:T(8,128)(2,1)S(1)}, bf16[256,1024]{1,0:T(8,128)(2,1)S(1)}, u32[]{:S(2)}, u32[]{:S(2)}) %collective-permute-start.18) | collective-permute-done | bytes 524320 | tf_op jit(solution)/shard_map/ppermute | solution.py:327
  79.3 0.1 collective-permute-start.19
  79.4 1.5 %collective-permute-start.16 = (bf16[256,1024]{1,0:T(8,128)(2,1)S(1)}, bf16[256,1024]{1,0:T(8,128)(2,1)}, u32[]{:S(2)}, u32[]{:S(2)}) collective-permute-start(bf16[256,1024]{1,0:T(8,128)(2,1)S(1)} %get-tuple-element.42.refs_1_.refs_5_.refs_0_), channel_id=1, source_target_pairs={{2,0},{3,1},{0,2},{1,3},{6,4},{7,5},{4,6},{5,7},{10,8},{11,9},{8,1... | collective-permute-start | bytes 1572872 | tf_op jit(solution)/shard_map/ppermute | solution.py:327
  80.8 0.1 pad_add_fusion.1.refs_0_
  80.9 0.2 collective-permute-start.15
  81.1 5.0 %collective-permute-done.13.refs_2_ = bf16[256,1024]{1,0:T(8,128)(2,1)S(1)} collective-permute-done((bf16[256,1024]{1,0:T(8,128)(2,1)}, bf16[256,1024]{1,0:T(8,128)(2,1)S(1)}, u32[]{:S(2)}, u32[]{:S(2)}) %collective-permute-start.13) | collective-permute-done | bytes 524320 | tf_op jit(solution)/shard_map/ppermute | solution.py:62
  86.1 5.4 %collective-permute-start.14 = (bf16[128,1024]{1,0:T(8,128)(2,1)S(1)}, bf16[128,1024]{1,0:T(8,128)(2,1)S(1)}, u32[]{:S(2)}, u32[]{:S(2)}) collective-permute-start(bf16[128,1024]{1,0:T(8,128)(2,1)S(1)} %get-tuple-element.41), channel_id=1, source_target_pairs={{0,8},{4,12},{8,16},{12,20},{16,24},{20,28},{1,9},{5,13},{9,17},{1... | collective-permute-start | bytes 786440 | tf_op jit(solution)/shard_map/ppermute | solution.py:62
  91.5 1.4 convert_add_fusion
  92.9 2.5 %shard_map.128 = (bf16[512,512]{1,0:T(8,128)(2,1)S(1)}, f32[512,512]{1,0:T(8,128)S(1)}) custom-call(s32[1]{0:T(128)} %bitcast.16.refs_0_, bf16[512,256]{1,0:T(8,128)(2,1)S(1)} %get-tuple-element.32.refs_1_, bf16[512,256]{1,0:T(8,128)(2,1)S(1)} %collective-permute-done.4.refs_2_, bf16[512,256]{1,0:T(8,128)(2,1)S(1)} %collective-permute-done.5.refs_3_, ...), custom_call_target="tpu_custom_call" | custom-call | tf_op jit(solution)/shard_map/pallas_call | solution.py:36
  95.5 0.7 collective-permute-start.28
  96.2 1.1 shard_map.129.refs_7_.refs_2_
  97.5 0.8 pad_maximum_fusion.2
  98.3 8.2 %collective-permute-done.28.refs_2_ = bf16[512,512]{1,0:T(8,128)(2,1)S(1)} collective-permute-done((bf16[512,512]{1,0:T(8,128)(2,1)S(1)}, bf16[512,512]{1,0:T(8,128)(2,1)S(1)}, u32[]{:S(2)}, u32[]{:S(2)}) %collective-permute-start.28) | collective-permute-done | bytes 524320 | tf_op jit(solution)/shard_map/ppermute | solution.py:363
  106.5 0.8 shard_map.133
  107.3 1.9 %collective-permute-start.30 = (bf16[512,128]{1,0:T(8,128)(2,1)S(1)}, bf16[512,128]{1,0:T(8,128)(2,1)S(1)}, u32[]{:S(2)}, u32[]{:S(2)}) collective-permute-start(bf16[512,128]{1,0:T(8,128)(2,1)S(1)} %get-tuple-element.58), channel_id=1, source_target_pairs={{16,0},{20,4},{24,8},{28,12},{0,16},{4,20},{8,24},{12,28},{17,1},{... | collective-permute-start | bytes 393224 | tf_op jit(solution)/shard_map/ppermute | solution.py:373
  109.2 0.6 collective-permute-start.31
  109.8 1.3 shard_map.130
  111.1 0.5 collective-permute-start.24
  111.6 3.6 %shard_map.131 = (bf16[256,512]{1,0:T(8,128)(2,1)S(1)}, bf16[256,512]{1,0:T(8,128)(2,1)S(1)}, bf16[256,512]{1,0:T(8,128)(2,1)S(1)}, bf16[256,512]{1,0:T(8,128)(2,1)S(1)}) custom-call(bf16[256,1024]{1,0:T(8,128)(2,1)S(1)} %get-tuple-element.42.refs_1_.refs_5_.refs_0_, bf16[256,1024]{1,0:T(8,128)(2,1)S(1)} %collective-permute-done.15.refs_6_.refs_1_, ...), custom_call_target="tpu_custom_call" | custom-call | tf_op jit(solution)/shard_map/pallas_call | solution.py:36
  115.2 0.1 broadcast_in_dim.13
  115.4 0.5 collective-permute-start.22
  115.9 1.4 collective-permute-done.30
  117.3 0.1 collective-permute-start.23
  117.3 0.8 convert_add_fusion.1
  118.1 6.4 %collective-permute-done.22 = bf16[256,512]{1,0:T(8,128)(2,1)S(1)} collective-permute-done((bf16[256,512]{1,0:T(8,128)(2,1)S(1)}, bf16[256,512]{1,0:T(8,128)(2,1)S(1)}, u32[]{:S(2)}, u32[]{:S(2)}) %collective-permute-start.22) | collective-permute-done | bytes 262176 | tf_op jit(solution)/shard_map/ppermute | solution.py:393
  124.6 0.8 shard_map.132
  125.4 3.6 %collective-permute-start.25 = (bf16[512,128]{1,0:T(8,128)(2,1)S(1)}, bf16[512,128]{1,0:T(8,128)(2,1)S(1)}, u32[]{:S(2)}, u32[]{:S(2)}) collective-permute-start(bf16[512,128]{1,0:T(8,128)(2,1)S(1)} %get-tuple-element.52), channel_id=1, source_target_pairs={{8,0},{12,4},{16,8},{20,12},{24,16},{28,20},{0,24},{4,28},{9,1},{1... | collective-permute-start | bytes 393224 | tf_op jit(solution)/shard_map/ppermute | solution.py:373
  129.0 1.1 collective-permute-start.27
  130.1 2.8 %collective-permute-done.25 = bf16[512,128]{1,0:T(8,128)(2,1)S(1)} collective-permute-done((bf16[512,128]{1,0:T(8,128)(2,1)S(1)}, bf16[512,128]{1,0:T(8,128)(2,1)S(1)}, u32[]{:S(2)}, u32[]{:S(2)}) %collective-permute-start.25) | collective-permute-done | bytes 131104 | tf_op jit(solution)/shard_map/ppermute | solution.py:373
  132.9 6.6 %collective-permute-done.26 = bf16[512,128]{1,0:T(8,128)(2,1)S(1)} collective-permute-done((bf16[512,128]{1,0:T(8,128)(2,1)S(1)}, bf16[512,128]{1,0:T(8,128)(2,1)S(1)}, u32[]{:S(2)}, u32[]{:S(2)}) %collective-permute-start.26) | collective-permute-done | bytes 131104 | tf_op jit(solution)/shard_map/ppermute | solution.py:373
  139.5 0.8 convert_add_fusion.2
  (51 shorter events, 0.6 us)
Async XLA Ops:
  1.9 10.2 %copy-start.4 = (bf16[1,256,2048]{2,1,0:T(8,128)(2,1)S(1)}, bf16[1,256,2048]{2,1,0:T(8,128)(2,1)}, u32[]{:S(2)}) copy-start(bf16[1,256,2048]{2,1,0:T(8,128)(2,1)} %param.9) | copy-start | bytes 3145732
  2.8 29.4 %collective-permute-start.3 = (bf16[128,2048]{1,0:T(8,128)(2,1)}, bf16[128,2048]{1,0:T(8,128)(2,1)S(1)}, u32[]{:S(2)}, u32[]{:S(2)}) collective-permute-start(bf16[128,2048]{1,0:T(8,128)(2,1)} %pad_maximum_fusion), channel_id=1, source_target_pairs={{8,0},{12,4},{16,8},{20,12},{24,16},{28,20},{9,1},{13,5},{17,9},{2... | collective-permute-start | bytes 1572872 | tf_op jit(solution)/shard_map/ppermute | solution.py:62
  4.9 3.0 %copy-start.9 = (s32[1,8,2]{1,2,0:T(2,128)S(1)}, s32[1,8,2]{1,2,0:T(2,128)}, u32[]{:S(2)}) copy-start(s32[1,8,2]{1,2,0:T(2,128)} %param.16) | copy-start | bytes 196
  4.9 30.4 %collective-permute-start.8 = (bf16[128,2048]{1,0:T(8,128)(2,1)}, bf16[128,2048]{1,0:T(8,128)(2,1)S(1)}, u32[]{:S(2)}, u32[]{:S(2)}) collective-permute-start(bf16[128,2048]{1,0:T(8,128)(2,1)} %pad_maximum_fusion.1), channel_id=1, source_target_pairs={{4,0},{0,4},{12,8},{8,12},{20,16},{16,20},{28,24},{24,28},{5,1},{1... | collective-permute-start | bytes 1572872 | tf_op jit(solution)/shard_map/ppermute | solution.py:283
  9.4 10.8 %collective-permute-start = (f32[16,128]{1,0:T(8,128)S(1)}, f32[16,128]{1,0:T(8,128)S(1)}, u32[]{:S(2)}, u32[]{:S(2)}) collective-permute-start(f32[16,128]{1,0:T(8,128)S(1)} %shard_map.120.refs_5_.refs_0_), channel_id=1, source_target_pairs={{4,0},{8,4},{12,8},{16,12},{20,16},{24,20},{28,24},{5,1},{9,5},{13... | collective-permute-start | bytes 24584 | tf_op jit(solution)/shard_map/ppermute | solution.py:62
  10.7 11.2 %collective-permute-start.1 = (f32[16,128]{1,0:T(8,128)S(1)}, f32[16,128]{1,0:T(8,128)S(1)}, u32[]{:S(2)}, u32[]{:S(2)}) collective-permute-start(f32[16,128]{1,0:T(8,128)S(1)} %shard_map.120.refs_5_.refs_0_), channel_id=1, source_target_pairs={{8,0},{12,4},{16,8},{20,12},{24,16},{28,20},{9,1},{13,5},{17,9},{2... | collective-permute-start | bytes 24584 | tf_op jit(solution)/shard_map/ppermute | solution.py:62
  13.0 8.9 %collective-permute-start.4 = (bf16[512,256]{1,0:T(8,128)(2,1)S(1)}, bf16[512,256]{1,0:T(8,128)(2,1)S(1)}, u32[]{:S(2)}, u32[]{:S(2)}) collective-permute-start(bf16[512,256]{1,0:T(8,128)(2,1)S(1)} %get-tuple-element.33), channel_id=1, source_target_pairs={{1,0},{0,1},{3,2},{2,3},{5,4},{4,5},{7,6},{6,7},{9,8},{8,9},{11,10... | collective-permute-start | bytes 786440 | tf_op jit(solution)/shard_map/ppermute | solution.py:298
  20.2 9.2 %collective-permute-start.5 = (bf16[512,256]{1,0:T(8,128)(2,1)S(1)}, bf16[512,256]{1,0:T(8,128)(2,1)S(1)}, u32[]{:S(2)}, u32[]{:S(2)}) collective-permute-start(bf16[512,256]{1,0:T(8,128)(2,1)S(1)} %get-tuple-element.34), channel_id=1, source_target_pairs={{2,0},{3,1},{0,2},{1,3},{6,4},{7,5},{4,6},{5,7},{10,8},{11,9},{8,1... | collective-permute-start | bytes 786440 | tf_op jit(solution)/shard_map/ppermute | solution.py:298
  21.9 10.3 %collective-permute-start.6 = (bf16[512,256]{1,0:T(8,128)(2,1)S(1)}, bf16[512,256]{1,0:T(8,128)(2,1)S(1)}, u32[]{:S(2)}, u32[]{:S(2)}) collective-permute-start(bf16[512,256]{1,0:T(8,128)(2,1)S(1)} %get-tuple-element.35), channel_id=1, source_target_pairs={{3,0},{2,1},{1,2},{0,3},{7,4},{6,5},{5,6},{4,7},{11,8},{10,9},{9,1... | collective-permute-start | bytes 786440 | tf_op jit(solution)/shard_map/ppermute | solution.py:298
  21.9 16.4 %collective-permute-start.2 = (bf16[128,2048]{1,0:T(8,128)(2,1)}, bf16[128,2048]{1,0:T(8,128)(2,1)S(1)}, u32[]{:S(2)}, u32[]{:S(2)}) collective-permute-start(bf16[128,2048]{1,0:T(8,128)(2,1)} %pad_maximum_fusion), channel_id=1, source_target_pairs={{4,0},{12,8},{20,16},{28,24},{5,1},{13,9},{21,17},{29,25},{6,2},{1... | collective-permute-start | bytes 1572872 | tf_op jit(solution)/shard_map/ppermute | solution.py:284
  32.2 15.3 %copy-start = (bf16[1,256,1024]{2,1,0:T(8,128)(2,1)S(1)}, bf16[1,256,1024]{2,1,0:T(8,128)(2,1)}, u32[]{:S(2)}) copy-start(bf16[1,256,1024]{2,1,0:T(8,128)(2,1)} %param.10) | copy-start | bytes 1572868
  32.2 15.3 %copy-start.1 = (bf16[1,256,1024]{2,1,0:T(8,128)(2,1)S(1)}, bf16[1,256,1024]{2,1,0:T(8,128)(2,1)}, u32[]{:S(2)}) copy-start(bf16[1,256,1024]{2,1,0:T(8,128)(2,1)} %param.13) | copy-start | bytes 1572868
  32.2 15.3 %copy-start.2 = (bf16[1,256,1024]{2,1,0:T(8,128)(2,1)S(1)}, bf16[1,256,1024]{2,1,0:T(8,128)(2,1)}, u32[]{:S(2)}) copy-start(bf16[1,256,1024]{2,1,0:T(8,128)(2,1)} %param.11) | copy-start | bytes 1572868
  32.2 15.3 %copy-start.3 = (bf16[1,256,1024]{2,1,0:T(8,128)(2,1)S(1)}, bf16[1,256,1024]{2,1,0:T(8,128)(2,1)}, u32[]{:S(2)}) copy-start(bf16[1,256,1024]{2,1,0:T(8,128)(2,1)} %param.12) | copy-start | bytes 1572868
  32.2 15.3 %collective-permute-start.7 = (bf16[128,2048]{1,0:T(8,128)(2,1)S(1)}, bf16[128,2048]{1,0:T(8,128)(2,1)S(1)}, u32[]{:S(2)}, u32[]{:S(2)}) collective-permute-start(bf16[128,2048]{1,0:T(8,128)(2,1)S(1)} %shard_map.122.refs_11_.refs_10_), channel_id=1, source_target_pairs={{0,4},{8,12},{16,20},{24,28},{1,5},{9,13},{17,21},{25,29},{2,6},{1... | collective-permute-start | bytes 1572872 | tf_op jit(solution)/shard_map/ppermute | solution.py:302
  35.3 12.2 %collective-permute-start.9 = (bf16[128,2048]{1,0:T(8,128)(2,1)S(1)}, bf16[128,2048]{1,0:T(8,128)(2,1)S(1)}, u32[]{:S(2)}, u32[]{:S(2)}) collective-permute-start(bf16[128,2048]{1,0:T(8,128)(2,1)S(1)} %collective-permute-done.8.refs_9_.refs_8_), channel_id=1, source_target_pairs={{12,4},{20,12},{28,20},{13,5},{21,13},{29,21},{14,6},{22,14},{30,2... | collective-permute-start | bytes 1572872 | tf_op jit(solution)/shard_map/ppermute | solution.py:303
  49.9 6.1 %collective-permute-start.10 = (f32[24,640]{1,0:T(8,128)S(1)}, f32[24,640]{1,0:T(8,128)S(1)}, u32[]{:S(2)}, u32[]{:S(2)}) collective-permute-start(f32[24,640]{1,0:T(8,128)S(1)} %shard_map.123.refs_0_.refs_11_), channel_id=1, source_target_pairs={{4,0},{0,4},{12,8},{8,12},{20,16},{16,20},{28,24},{24,28},{5,1},{1... | collective-permute-start | bytes 184328 | tf_op jit(solution)/shard_map/ppermute | solution.py:313
  56.1 5.0 %collective-permute-start.11 = (f32[24,512]{1,0:T(8,128)S(1)}, f32[24,512]{1,0:T(8,128)S(1)}, u32[]{:S(2)}, u32[]{:S(2)}) collective-permute-start(f32[24,512]{1,0:T(8,128)S(1)} %get-tuple-element.36), channel_id=1, source_target_pairs={{0,8},{4,12},{8,16},{12,20},{16,24},{20,28},{1,9},{5,13},{9,17},{1... | collective-permute-start | bytes 147464 | tf_op jit(solution)/shard_map/ppermute | solution.py:62
  59.3 6.0 %collective-permute-start.12 = (f32[24,512]{1,0:T(8,128)S(1)}, f32[24,512]{1,0:T(8,128)S(1)}, u32[]{:S(2)}, u32[]{:S(2)}) collective-permute-start(f32[24,512]{1,0:T(8,128)S(1)} %get-tuple-element.37), channel_id=1, source_target_pairs={{8,0},{12,4},{16,8},{20,12},{24,16},{28,20},{9,1},{13,5},{17,9},{2... | collective-permute-start | bytes 147464 | tf_op jit(solution)/shard_map/ppermute | solution.py:62
  67.7 11.6 %collective-permute-start.18 = (bf16[256,1024]{1,0:T(8,128)(2,1)S(1)}, bf16[256,1024]{1,0:T(8,128)(2,1)S(1)}, u32[]{:S(2)}, u32[]{:S(2)}) collective-permute-start(bf16[256,1024]{1,0:T(8,128)(2,1)S(1)} %get-tuple-element.43.refs_5_.refs_4_), channel_id=1, source_target_pairs={{2,0},{3,1},{0,2},{1,3},{6,4},{7,5},{4,6},{5,7},{10,8},{11,9},{8,1... | collective-permute-start | bytes 1572872 | tf_op jit(solution)/shard_map/ppermute | solution.py:327
  72.7 6.6 %copy-start.5 = (f32[256,1024]{1,0:T(8,128)}, f32[256,1024]{1,0:T(8,128)S(1)}, u32[]{:S(2)}) copy-start(f32[256,1024]{1,0:T(8,128)S(1)} %get-tuple-element.39) | copy-start | bytes 3145732
  72.7 13.4 %collective-permute-start.13 = (bf16[256,1024]{1,0:T(8,128)(2,1)}, bf16[256,1024]{1,0:T(8,128)(2,1)S(1)}, u32[]{:S(2)}, u32[]{:S(2)}) collective-permute-start(bf16[256,1024]{1,0:T(8,128)(2,1)} %get-tuple-element.40), channel_id=1, source_target_pairs={{0,4},{4,8},{8,12},{12,16},{16,20},{20,24},{24,28},{1,5},{5,9},{9,... | collective-permute-start | bytes 1572872 | tf_op jit(solution)/shard_map/ppermute | solution.py:62
  76.4 16.5 %collective-permute-start.17 = (bf16[256,1024]{1,0:T(8,128)(2,1)S(1)}, bf16[256,1024]{1,0:T(8,128)(2,1)}, u32[]{:S(2)}, u32[]{:S(2)}) collective-permute-start(bf16[256,1024]{1,0:T(8,128)(2,1)S(1)} %get-tuple-element.43.refs_5_.refs_4_), channel_id=1, source_target_pairs={{1,0},{0,1},{3,2},{2,3},{5,4},{4,5},{7,6},{6,7},{9,8},{8,9},{11,10... | collective-permute-start | bytes 1572872 | tf_op jit(solution)/shard_map/ppermute | solution.py:324
  79.3 13.6 %collective-permute-start.19 = (bf16[256,1024]{1,0:T(8,128)(2,1)S(1)}, bf16[256,1024]{1,0:T(8,128)(2,1)}, u32[]{:S(2)}, u32[]{:S(2)}) collective-permute-start(bf16[256,1024]{1,0:T(8,128)(2,1)S(1)} %shard_map.127.refs_7_.refs_6_), channel_id=1, source_target_pairs={{1,0},{0,1},{3,2},{2,3},{5,4},{4,5},{7,6},{6,7},{9,8},{8,9},{11,10... | collective-permute-start | bytes 1572872 | tf_op jit(solution)/shard_map/ppermute | solution.py:324
  79.4 16.8 %collective-permute-start.16 = (bf16[256,1024]{1,0:T(8,128)(2,1)S(1)}, bf16[256,1024]{1,0:T(8,128)(2,1)}, u32[]{:S(2)}, u32[]{:S(2)}) collective-permute-start(bf16[256,1024]{1,0:T(8,128)(2,1)S(1)} %get-tuple-element.42.refs_1_.refs_5_.refs_0_), channel_id=1, source_target_pairs={{2,0},{3,1},{0,2},{1,3},{6,4},{7,5},{4,6},{5,7},{10,8},{11,9},{8,1... | collective-permute-start | bytes 1572872 | tf_op jit(solution)/shard_map/ppermute | solution.py:327
  80.9 28.8 %collective-permute-start.15 = (bf16[256,1024]{1,0:T(8,128)(2,1)S(1)}, bf16[256,1024]{1,0:T(8,128)(2,1)S(1)}, u32[]{:S(2)}, u32[]{:S(2)}) collective-permute-start(bf16[256,1024]{1,0:T(8,128)(2,1)S(1)} %get-tuple-element.42.refs_1_.refs_5_.refs_0_), channel_id=1, source_target_pairs={{1,0},{0,1},{3,2},{2,3},{5,4},{4,5},{7,6},{6,7},{9,8},{8,9},{11,10... | collective-permute-start | bytes 1572872 | tf_op jit(solution)/shard_map/ppermute | solution.py:324
  86.1 10.1 %collective-permute-start.14 = (bf16[128,1024]{1,0:T(8,128)(2,1)S(1)}, bf16[128,1024]{1,0:T(8,128)(2,1)S(1)}, u32[]{:S(2)}, u32[]{:S(2)}) collective-permute-start(bf16[128,1024]{1,0:T(8,128)(2,1)S(1)} %get-tuple-element.41), channel_id=1, source_target_pairs={{0,8},{4,12},{8,16},{12,20},{16,24},{20,28},{1,9},{5,13},{9,17},{1... | collective-permute-start | bytes 786440 | tf_op jit(solution)/shard_map/ppermute | solution.py:62
  95.5 11.0 %collective-permute-start.28 = (bf16[512,512]{1,0:T(8,128)(2,1)S(1)}, bf16[512,512]{1,0:T(8,128)(2,1)S(1)}, u32[]{:S(2)}, u32[]{:S(2)}) collective-permute-start(bf16[512,512]{1,0:T(8,128)(2,1)S(1)} %get-tuple-element.44.refs_1_), channel_id=1, source_target_pairs={{4,0},{0,4},{12,8},{8,12},{20,16},{16,20},{28,24},{24,28},{5,1},{1... | collective-permute-start | bytes 1572872 | tf_op jit(solution)/shard_map/ppermute | solution.py:363
  97.3 12.5 %collective-permute-start.20 = (bf16[256,1024]{1,0:T(8,128)(2,1)S(1)}, bf16[256,1024]{1,0:T(8,128)(2,1)S(1)}, u32[]{:S(2)}, u32[]{:S(2)}) collective-permute-start(bf16[256,1024]{1,0:T(8,128)(2,1)S(1)} %shard_map.129.refs_7_.refs_2_), channel_id=1, source_target_pairs={{1,0},{0,1},{3,2},{2,3},{5,4},{4,5},{7,6},{6,7},{9,8},{8,9},{11,10... | collective-permute-start | bytes 1572872 | tf_op jit(solution)/shard_map/ppermute | solution.py:324
  107.2 8.2 %collective-permute-start.29 = (bf16[512,128]{1,0:T(8,128)(2,1)S(1)}, bf16[512,128]{1,0:T(8,128)(2,1)S(1)}, u32[]{:S(2)}, u32[]{:S(2)}) collective-permute-start(bf16[512,128]{1,0:T(8,128)(2,1)S(1)} %get-tuple-element.57), channel_id=1, source_target_pairs={{8,0},{12,4},{16,8},{20,12},{24,16},{28,20},{0,24},{4,28},{9,1},{1... | collective-permute-start | bytes 393224 | tf_op jit(solution)/shard_map/ppermute | solution.py:373
  107.3 10.0 %collective-permute-start.30 = (bf16[512,128]{1,0:T(8,128)(2,1)S(1)}, bf16[512,128]{1,0:T(8,128)(2,1)S(1)}, u32[]{:S(2)}, u32[]{:S(2)}) collective-permute-start(bf16[512,128]{1,0:T(8,128)(2,1)S(1)} %get-tuple-element.58), channel_id=1, source_target_pairs={{16,0},{20,4},{24,8},{28,12},{0,16},{4,20},{8,24},{12,28},{17,1},{... | collective-permute-start | bytes 393224 | tf_op jit(solution)/shard_map/ppermute | solution.py:373
  109.2 2.4 %copy-start.6 = (bf16[512,1024]{1,0:T(8,128)(2,1)S(1)}, bf16[512,1024]{1,0:T(8,128)(2,1)}, u32[]{:S(2)}) copy-start(bf16[512,1024]{1,0:T(8,128)(2,1)} %refs_8_.1) | copy-start | bytes 3145732
  109.2 2.4 %copy-start.7 = (bf16[512,1024]{1,0:T(8,128)(2,1)S(1)}, bf16[512,1024]{1,0:T(8,128)(2,1)}, u32[]{:S(2)}) copy-start(bf16[512,1024]{1,0:T(8,128)(2,1)} %refs_9_.1) | copy-start | bytes 3145732
  109.2 8.1 %collective-permute-start.31 = (bf16[512,128]{1,0:T(8,128)(2,1)S(1)}, bf16[512,128]{1,0:T(8,128)(2,1)S(1)}, u32[]{:S(2)}, u32[]{:S(2)}) collective-permute-start(bf16[512,128]{1,0:T(8,128)(2,1)S(1)} %get-tuple-element.59), channel_id=1, source_target_pairs={{24,0},{28,4},{0,8},{4,12},{8,16},{12,20},{16,24},{20,28},{25,1},{... | collective-permute-start | bytes 393224 | tf_op jit(solution)/shard_map/ppermute | solution.py:373
  111.1 13.5 %collective-permute-start.24 = (bf16[512,512]{1,0:T(8,128)(2,1)S(1)}, bf16[512,512]{1,0:T(8,128)(2,1)S(1)}, u32[]{:S(2)}, u32[]{:S(2)}) collective-permute-start(bf16[512,512]{1,0:T(8,128)(2,1)S(1)} %get-tuple-element.45.refs_10_), channel_id=1, source_target_pairs={{4,0},{0,4},{12,8},{8,12},{20,16},{16,20},{28,24},{24,28},{5,1},{1... | collective-permute-start | bytes 1572872 | tf_op jit(solution)/shard_map/ppermute | solution.py:363
  115.2 2.9 %collective-permute-start.21 = (bf16[256,512]{1,0:T(8,128)(2,1)S(1)}, bf16[256,512]{1,0:T(8,128)(2,1)S(1)}, u32[]{:S(2)}, u32[]{:S(2)}) collective-permute-start(bf16[256,512]{1,0:T(8,128)(2,1)S(1)} %get-tuple-element.47), channel_id=1, source_target_pairs={{0,1},{1,0},{2,3},{3,2},{4,5},{5,4},{6,7},{7,6},{8,9},{9,8},{10,11... | collective-permute-start | bytes 786440 | tf_op jit(solution)/shard_map/ppermute | solution.py:393
  115.4 9.2 %collective-permute-start.22 = (bf16[256,512]{1,0:T(8,128)(2,1)S(1)}, bf16[256,512]{1,0:T(8,128)(2,1)S(1)}, u32[]{:S(2)}, u32[]{:S(2)}) collective-permute-start(bf16[256,512]{1,0:T(8,128)(2,1)S(1)} %get-tuple-element.48), channel_id=1, source_target_pairs={{0,2},{1,3},{2,0},{3,1},{4,6},{5,7},{6,4},{7,5},{8,10},{9,11},{10,... | collective-permute-start | bytes 786440 | tf_op jit(solution)/shard_map/ppermute | solution.py:393
  117.3 12.8 %collective-permute-start.23 = (bf16[256,512]{1,0:T(8,128)(2,1)S(1)}, bf16[256,512]{1,0:T(8,128)(2,1)S(1)}, u32[]{:S(2)}, u32[]{:S(2)}) collective-permute-start(bf16[256,512]{1,0:T(8,128)(2,1)S(1)} %get-tuple-element.49), channel_id=1, source_target_pairs={{0,3},{1,2},{2,1},{3,0},{4,7},{5,6},{6,5},{7,4},{8,11},{9,10},{10,... | collective-permute-start | bytes 786440 | tf_op jit(solution)/shard_map/ppermute | solution.py:393
  125.4 7.5 %collective-permute-start.25 = (bf16[512,128]{1,0:T(8,128)(2,1)S(1)}, bf16[512,128]{1,0:T(8,128)(2,1)S(1)}, u32[]{:S(2)}, u32[]{:S(2)}) collective-permute-start(bf16[512,128]{1,0:T(8,128)(2,1)S(1)} %get-tuple-element.52), channel_id=1, source_target_pairs={{8,0},{12,4},{16,8},{20,12},{24,16},{28,20},{0,24},{4,28},{9,1},{1... | collective-permute-start | bytes 393224 | tf_op jit(solution)/shard_map/ppermute | solution.py:373
  129.0 10.6 %collective-permute-start.26 = (bf16[512,128]{1,0:T(8,128)(2,1)S(1)}, bf16[512,128]{1,0:T(8,128)(2,1)S(1)}, u32[]{:S(2)}, u32[]{:S(2)}) collective-permute-start(bf16[512,128]{1,0:T(8,128)(2,1)S(1)} %get-tuple-element.53), channel_id=1, source_target_pairs={{16,0},{20,4},{24,8},{28,12},{0,16},{4,20},{8,24},{12,28},{17,1},{... | collective-permute-start | bytes 393224 | tf_op jit(solution)/shard_map/ppermute | solution.py:373
  129.0 10.6 %collective-permute-start.27 = (bf16[512,128]{1,0:T(8,128)(2,1)S(1)}, bf16[512,128]{1,0:T(8,128)(2,1)S(1)}, u32[]{:S(2)}, u32[]{:S(2)}) collective-permute-start(bf16[512,128]{1,0:T(8,128)(2,1)S(1)} %get-tuple-element.54), channel_id=1, source_target_pairs={{24,0},{28,4},{0,8},{4,12},{8,16},{12,20},{16,24},{20,28},{25,1},{... | collective-permute-start | bytes 393224 | tf_op jit(solution)/shard_map/ppermute | solution.py:373
  130.1 10.2 %copy-start.8 = (bf16[1,256,2048]{2,1,0:T(8,128)(2,1)}, bf16[1,256,2048]{2,1,0:T(8,128)(2,1)S(1)}, u32[]{:S(2)}) copy-start(bf16[1,256,2048]{2,1,0:T(8,128)(2,1)S(1)} %bitcast_dynamic-update-slice_fusion) | copy-start | bytes 3145732

commit v3 on v2

v3 whole, which is shorter than its diff:
```python
import functools

import jax
import jax.numpy as jnp
from jax import lax
from jax.experimental import pallas as pl
from jax.experimental.pallas import tpu as pltpu
from jax.sharding import PartitionSpec as P

H = 8
HS = 128
BLK = 128
HD = 1024
QBD = 2
REACH = 2
MAXP = 8
WB = 4
SLOTS = QBD + WB - 1
UNUSED = 100
CHUNK_FLOPS = 20_000_000_000
VMEM_LIMIT = 16 * 1024 * 1024
SPAN = SLOTS * BLK
LOWEST = -1e29
MASKED = -1e30
SCALE = HS ** (-0.5)
SETS = ((0, 3, 4, 7), (2, 1, 6, 5))
VMEM = pl.BlockSpec(memory_space=pltpu.VMEM)
ANY = pl.BlockSpec(memory_space=pl.ANY)


def kernel_call(body, outs, operands, after=(), scratch=(), flops=1):
    count = len(operands)

    def run(*refs):
        body(*refs[:count], *refs[count + len(after) :])

    return pl.pallas_call(
        run,
        out_shape=tuple(outs),
        in_specs=[VMEM] * count + [ANY] * len(after),
        out_specs=tuple([VMEM] * len(outs)),
        scratch_shapes=list(scratch),
        compiler_params=pltpu.CompilerParams(vmem_limit_bytes=VMEM_LIMIT),
        cost_estimate=pl.CostEstimate(flops=flops, bytes_accessed=1, transcendentals=0),
    )(*operands, *after)


def copy_body(value, out):
    out[...] = value[...]


def held(value, *others):
    (copy,) = kernel_call(copy_body, [shape(value.shape, value.dtype)], (value,), after=others)
    return copy


def shape(dims, kind):
    return jax.ShapeDtypeStruct(dims, kind)


def shifted(value, axis, steps):
    count = lax.axis_size(axis)
    return lax.ppermute(
        value, axis, [(s, s + steps) for s in range(max(0, -steps), min(count, count - steps))]
    )


def rolled_pairs(count, far, flip):
    half = count // 2
    return [(((a + far) % half) * 2 + (b ^ flip), a * 2 + b) for a in range(half) for b in range(2)]


def nt(left, right):
    return lax.dot_general(left, right, (((1,), (1,)), ((), ())), preferred_element_type=jnp.float32)


def tn(left, right):
    return lax.dot_general(left, right, (((0,), (0,)), ((), ())), preferred_element_type=jnp.float32)


def nn(left, right):
    return jnp.dot(left, right, preferred_element_type=jnp.float32)


def rules_of(lines):
    lines = lines.astype(jnp.float32)
    queries, keys = lines[:MAXP], lines[MAXP:]
    found = {}
    for query in range(QBD):
        for back in range(WB):
            hit = jnp.where((queries == query) & (keys == query - back), 0.0, MASKED)
            found[query, back] = jnp.max(hit, axis=0, keepdims=True)
    return found


def fill_bias(own, even, odd, far, bias):
    sets = [rules_of(part) for part in (own[BLK:, :BLK], even[BLK:, :BLK] + odd[BLK:, :BLK], far[BLK:, :BLK])]
    rows = lax.broadcasted_iota(jnp.int32, (BLK, BLK), 0)
    columns = lax.broadcasted_iota(jnp.int32, (BLK, BLK), 1)
    for key in range(QBD):
        for slot in range(SLOTS):
            place = (pl.ds(key * BLK, BLK), pl.ds(slot * BLK, BLK))
            back = slot - key
            if not 0 <= back < WB:
                bias[place] = jnp.full((BLK, BLK), MASKED, jnp.float32)
                continue
            block = jnp.broadcast_to(sets[slot // QBD][slot % QBD, back], (BLK, BLK))
            if slot == key:
                block = jnp.where(rows <= columns, block, MASKED)
            bias[place] = block


def head_of(ref, place):
    return ref[:, place * HS : (place + 1) * HS]


def rows_of(own, halo, head, place):
    even, odd, swap, relay, far, flag = halo
    columns = slice(place * HS, (place + 1) * HS)
    first = even[:BLK, columns] + odd[:BLK, columns]
    second = head_of(swap, place) * flag + head_of(relay, place)
    return jnp.concatenate([head_of(own, head), first, second, far[:BLK, columns]], axis=0)


def halo_of(refs):
    flag = jnp.where(lax.axis_index("tm") % 2 == 0, 1.0, 0.0).astype(jnp.bfloat16)
    return (*refs, flag)


def stats_body(mine, q, k, v, g, even, odd, swap, relay, far, own, bias):
    halo = halo_of((even, odd, swap, relay, far))
    fill_bias(mine, even, odd, far, bias)
    for h in range(H):
        scores = nt(head_of(k, h), rows_of(q, halo, h, h)) * SCALE + bias[...]
        products = nt(head_of(v, h), rows_of(g, halo, h, H + h))
        largest = jnp.maximum(jnp.max(scores, axis=0, keepdims=True), LOWEST)
        weights = jnp.exp(scores - largest)
        own[h : h + 1, :] = largest
        own[H + h : H + h + 1, :] = jnp.sum(weights, axis=0, keepdims=True)
        own[2 * H + h : 2 * H + h + 1, :] = jnp.sum(weights * products, axis=0, keepdims=True)


def spread_body(own, pair, up, down):
    up[:, :BLK] = own[:, 4 * BLK :]
    up[:, BLK:] = pair[:, 2 * BLK :]
    down[:, :BLK] = own[:, :BLK]
    down[:, BLK:] = pair[:, : 3 * BLK]


def merge_stats(own, pair, up, down):
    is_even = lax.axis_index("tm") % 2 == 0

    def terms(ref, first, last):
        part = ref[:, first * BLK : last * BLK]
        large, mass, dot = (part[i * H : (i + 1) * H] for i in range(3))
        return jnp.where(mass > 0, large, LOWEST), mass, dot

    def either(first, second):
        return tuple(jnp.where(is_even, a, b) for a, b in zip(first, second))

    nothing = (
        jnp.full((H, BLK), LOWEST, jnp.float32),
        jnp.zeros((H, BLK), jnp.float32),
        jnp.zeros((H, BLK), jnp.float32),
    )

    def side(*parts):
        return tuple(jnp.concatenate(piece, axis=1) for piece in zip(*parts))

    def cut(part, first, last):
        return tuple(piece[:, first * BLK : last * BLK] for piece in part)

    before = either(terms(up, 1, 4), terms(pair, 2, 5))
    behind = either(terms(pair, 0, 3), terms(down, 1, 4))
    sets = (
        terms(own, 0, SLOTS),
        side(before, cut(behind, 1, 3)),
        side(terms(up, 0, 1), nothing, cut(behind, 0, 1), nothing, terms(down, 0, 1)),
    )
    largest = jnp.maximum(jnp.maximum(sets[0][0], sets[1][0]), sets[2][0])
    mass = jnp.zeros((H, SPAN), jnp.float32)
    dot = jnp.zeros((H, SPAN), jnp.float32)
    for large, part_mass, part_dot in sets:
        factor = jnp.exp(large - largest)
        mass = mass + factor * part_mass
        dot = dot + factor * part_dot
    inverse = jnp.where(mass > 0, 1.0 / jnp.where(mass > 0, mass, 1.0), 0.0)
    return largest, inverse, dot * inverse


def probs_of(h, bias, q, k, halo, total):
    query = rows_of(q, halo, h, h)
    scores = nt(head_of(k, h), query) * SCALE + bias[...]
    return query, jnp.exp(scores - total[h : h + 1, :]) * total[H + h : H + h + 1, :]


def grad_scores_of(h, probs, v, cotangent, total):
    products = nt(head_of(v, h), cotangent)
    return (probs * (products - total[2 * H + h : 2 * H + h + 1, :])).astype(jnp.bfloat16)


def lows_body(bias, q, k, v, g, even, odd, swap, relay, far, own, pair, up, down, mine, other, total):
    halo = halo_of((even, odd, swap, relay, far))
    for index, value in enumerate(merge_stats(own, pair, up, down)):
        total[index * H : (index + 1) * H] = value
    keeps_key = lax.axis_index("fsdp") % 2 == 0
    for place, h in enumerate([h for heads in SETS for h in heads]):
        query, probs = probs_of(h, bias, q, k, halo, total)
        cotangent = rows_of(g, halo, h, H + h)
        value_grads = nn(probs.astype(jnp.bfloat16), cotangent)
        key_grads = nn(grad_scores_of(h, probs, v, cotangent, total), query) * SCALE
        columns = slice(place * HS, (place + 1) * HS)
        mine[:, columns] = jnp.where(keeps_key, key_grads, value_grads).astype(jnp.bfloat16)
        other[:, columns] = jnp.where(keeps_key, value_grads, key_grads).astype(jnp.bfloat16)


def queries_body(bias, q, k, v, g, even, odd, swap, relay, far, total, dq0, dq1, dq2):
    halo = halo_of((even, odd, swap, relay, far))
    for h in range(H):
        _, probs = probs_of(h, bias, q, k, halo, total)
        grad_scores = grad_scores_of(h, probs, v, rows_of(g, halo, h, H + h), total)
        columns = slice(h * HS, (h + 1) * HS)
        grad_query = tn(grad_scores, head_of(k, h)) * SCALE
        dq0[:, columns] = grad_query[: 2 * BLK]
        dq1[:, columns] = grad_query[2 * BLK : 4 * BLK].astype(jnp.bfloat16)
        dq2[:, columns] = grad_query[4 * BLK :].astype(jnp.bfloat16)


def query_body(own, near, far, out):
    total = own[...] + near[...].astype(jnp.float32)
    out[:BLK, :] = (total[:BLK] + far[...].astype(jnp.float32)).astype(jnp.bfloat16)
    out[BLK:, :] = total[BLK:].astype(jnp.bfloat16)


def position(axis):
    index = lax.axis_index(axis)
    return index // 2, index % 2


def turned_back(value, away, count):
    return lax.rem(value + (count - away), count)


def looked_up(table):
    shard = lax.axis_index("tm")
    entry = jnp.int32(table[0])
    for index, value in enumerate(table):
        entry = jnp.where(shard == index, jnp.int32(value), entry)
    return entry


def cut_body(width, x, *outs):
    for away, out in enumerate(outs):
        place = turned_back(position("fsdp")[0], away, len(outs))
        first = pl.multiple_of(place * width, width)
        out[...] = x[:, pl.ds(first, width)].T


def join_body(mine, heard, *outs):
    tokens, width = mine.shape[0], outs[0].shape[1]
    for n, out in enumerate(outs):
        out[:tokens, :] = mine[:, n * width : (n + 1) * width]
        out[tokens:, :] = heard[:, n * width : (n + 1) * width]


def weight_body(pairs, *refs):
    parts = (len(refs) - 2) // 3
    turned, lows, (send, keep) = refs[: 2 * parts], refs[2 * parts : 3 * parts], refs[3 * parts :]
    tokens = turned[0].shape[1]
    mine = position("tm")[1]
    for out, side in ((send, 1 - mine), (keep, mine)):
        for pair in range(0, pairs, 2):
            places = [pl.ds(pl.multiple_of((2 * place + side) * HS, HS), HS) for place in (pair, pair + 1)]
            total = None
            for n, left in enumerate(turned):
                rows = pl.ds(n % 2 * tokens, tokens)
                term = nn(left[...], jnp.concatenate([lows[n // 2][rows, place] for place in places], axis=1))
                total = term if total is None else total + term
            out[:, pair * HS : (pair + 2) * HS] = total.astype(out.dtype)


def plain_weight_body(*refs):
    parts = (len(refs) - 1) // 3
    turned, lows, out = refs[: 2 * parts], refs[2 * parts : 3 * parts], refs[-1]
    tokens = turned[0].shape[1]
    for first in range(0, out.shape[1], 2 * HS):
        total = None
        for n, left in enumerate(turned):
            right = lows[n // 2][n % 2 * tokens : (n % 2 + 1) * tokens, first : first + 2 * HS]
            term = nn(left[...], right)
            total = term if total is None else total + term
        out[:, first : first + 2 * HS] = total


def rows_body(weight, pair_weight, *refs):
    parts = (len(refs) - 2) // len(SETS)
    lows, (keep, send) = refs[:-2], refs[-2:]
    tokens, width = lows[0].shape[0] // 2, weight.shape[0]
    core = position("fsdp")[1]
    order = [h for heads in SETS for h in heads]
    for side, source in ((core, weight), (1 - core, pair_weight)):
        columns = pl.ds(pl.multiple_of(side * width, width), width)
        turned = jnp.concatenate([head_of(source, h) for h in order], axis=1)
        for part in range(parts):
            for flip, out in enumerate((keep, send)):
                rows = pl.ds(flip * tokens, tokens)
                low = jnp.concatenate([lows[n * parts + part][rows, :] for n in range(len(SETS))], axis=1)
                out[part * tokens : (part + 1) * tokens, columns] = nt(low, turned).astype(out.dtype)


def sums_body(keep, heard, *outs):
    tokens = outs[0].shape[0]
    for n, out in enumerate(outs):
        rows = pl.ds(n * tokens, tokens)
        out[...] = (keep[rows, :] + heard[rows, :].astype(jnp.float32)).astype(out.dtype)


def place_body(*refs):
    out = refs[-1]
    for away, piece in enumerate(refs[:-1]):
        width = piece.shape[1]
        place = turned_back(position("fsdp")[0], away, len(refs) - 1)
        out[:, pl.ds(pl.multiple_of(place * width, width), width)] = piece[...]


def chunks_body(tables, keep, heard, *outs):
    for index, table in enumerate(tables):
        columns = pl.ds(pl.multiple_of(looked_up(table) * HS, HS), HS)
        value = keep[:, columns] + heard[:, columns].astype(jnp.float32)
        outs[index][...] = value.astype(outs[index].dtype)


def choose_body(first, second, kept, sent):
    for core, (a, b) in enumerate(((first, second), (second, first))):

        @pl.when(position("fsdp")[1] == core)
        def _():
            kept[...] = a[...]
            sent[...] = b[...]


def total_body(*refs):
    total = None
    for part in refs[:-1]:
        term = part[...].astype(jnp.float32)
        total = term if total is None else total + term
    refs[-1][...] = total


def grouped(refs, sizes):
    groups, start = [], 0
    for size in sizes:
        groups.append(refs[start : start + size])
        start += size
    return groups


def final_body(belongs, sizes, *refs):
    mine, send = refs[-2:]
    height = mine.shape[0]
    core = position("fsdp")[1]
    for n, parts in enumerate(grouped(refs[:-2], sizes)):

        @pl.when(looked_up(belongs) == n)
        def _():
            for out, side in ((mine, core), (send, 1 - core)):
                rows = pl.ds(pl.multiple_of(side * height, height), height)
                total = None
                for part in parts:
                    term = part[rows, :].astype(jnp.float32)
                    total = term if total is None else total + term
                out[...] = total


def shards(
    inputs, query_rows, saved_key_rows, value_rows, grad_out, key_weight, value_weight, block_pairs, pair_counts
):
    tokens = query_rows.shape[1]
    n_tm, n_fsdp = lax.axis_size("tm"), lax.axis_size("fsdp")
    shard, owner = lax.axis_index("tm"), lax.axis_index("fsdp")
    core = owner % 2
    d_model = inputs.shape[2]
    rows = d_model // n_fsdp
    half, chips = n_tm // 2, n_fsdp // 2
    q, k, v, g = query_rows[0], saved_key_rows[0], value_rows[0], grad_out[0]
    bf16, f32 = jnp.bfloat16, jnp.float32

    def exchanged(array):
        return lax.ppermute(array, "fsdp", rolled_pairs(n_fsdp, 0, 1))

    pairs = jnp.where(jnp.arange(MAXP)[:, None] < pair_counts[0], block_pairs[0] - shard * QBD, UNUSED)
    lines = jnp.broadcast_to(pairs.T.reshape(2 * MAXP, 1), (2 * MAXP, 2 * HD)).astype(bf16)
    first = jnp.concatenate([jnp.concatenate([q[:BLK], g[:BLK]], axis=1), lines], axis=0)
    latter = jnp.concatenate([q[BLK:], g[BLK:]], axis=1)
    far = shifted(first, "tm", -2)
    swap = lax.ppermute(latter, "tm", rolled_pairs(n_tm, 0, 1))
    even = lax.ppermute(first, "tm", [(2 * z + 1, 2 * z) for z in range(half)])
    odd = lax.ppermute(far, "tm", [(2 * z, 2 * z + 1) for z in range(half)])
    relay = lax.ppermute(swap, "tm", [(2 * z + 3, 2 * z + 1) for z in range(half - 1)])

    cuts = kernel_call(
        functools.partial(cut_body, 2 * rows),
        [shape((2 * rows, tokens), bf16)] * chips,
        (inputs[0],),
    )
    turned = []
    for away, piece in enumerate(cuts):
        if away:
            piece = lax.ppermute(piece, "fsdp", rolled_pairs(n_fsdp, away, 0))
        turned += [piece, exchanged(piece)]

    halo = (even, odd, swap, relay, far)
    own, bias = kernel_call(
        stats_body,
        [shape((3 * H, SPAN), f32), shape((tokens, SPAN), f32)],
        (first, q, k, v, g, *halo),
        after=turned,
    )
    pair = lax.ppermute(own, "tm", rolled_pairs(n_tm, 0, 1))
    up, down = kernel_call(spread_body, [shape((3 * H, 4 * BLK), f32)] * 2, (own, pair))
    up, down = shifted(up, "tm", 2), shifted(down, "tm", -2)
    mine, other, total = kernel_call(
        lows_body,
        [shape((tokens, HD), bf16), shape((tokens, HD), bf16), shape((3 * H, SPAN), f32)],
        (bias, q, k, v, g, *halo, own, pair, up, down),
    )
    heard = exchanged(other)
    widths = [len(heads) * HS for heads in SETS]
    lows = kernel_call(join_body, [shape((2 * tokens, width), bf16) for width in widths], (mine, heard))
    far_lows = [
        [lax.ppermute(low, "fsdp", rolled_pairs(n_fsdp, away, 0)) for away in range(1, chips)] for low in lows
    ]
    dq0, dq1, dq2 = kernel_call(
        queries_body,
        [shape((tokens, HD), f32), shape((tokens, HD), bf16), shape((BLK, HD), bf16)],
        (bias, q, k, v, g, *halo, total),
        after=lows,
    )
    near_terms, far_terms = shifted(dq1, "tm", 1), shifted(dq2, "tm", 2)

    aligned = HD // n_tm == HS
    groups, partials = [], []
    for heads, low, arrays, width in zip(SETS, lows, far_lows, widths):
        if partials:
            arrays = [held(array, partials[-1][0], near_terms, far_terms) for array in arrays]
        group = (low, *arrays)
        groups.append(group)
        if aligned:
            partials.append(
                kernel_call(
                    functools.partial(weight_body, len(heads) // 2),
                    [shape((2 * rows, width // 2), bf16), shape((2 * rows, width // 2), f32)],
                    (*turned, *group),
                )
            )
        else:
            partials.append(kernel_call(plain_weight_body, [shape((2 * rows, width), f32)], (*turned, *group)))
    weight, pair_weight = kernel_call(
        choose_body, [shape(key_weight.shape, bf16)] * 2, (key_weight, value_weight)
    )
    pair_weight = exchanged(pair_weight)
    keep, send = kernel_call(
        rows_body,
        [shape((chips * tokens, 2 * rows), kind) for kind in (f32, bf16)],
        (weight, pair_weight, *(array for group in groups for array in group)),
        after=(partials[-1][0],),
    )
    pieces = kernel_call(sums_body, [shape((tokens, 2 * rows), bf16)] * chips, (keep, exchanged(send)))
    arrived = []
    for away, piece in enumerate(pieces):
        if away:
            routes = [(receiver, sender) for sender, receiver in rolled_pairs(n_fsdp, away, 0)]
            piece = lax.ppermute(piece, "fsdp", routes)
        arrived.append(piece)
    (result,) = kernel_call(place_body, [shape((tokens, d_model), bf16)], arrived)
    (grad_query,) = kernel_call(query_body, [shape((tokens, HD), bf16)], (dq0, near_terms, far_terms))

    if aligned:
        sums, earlier = [], ()
        for index, (heads, (send, keep)) in enumerate(zip(SETS, partials)):
            pairs_here = len(heads) // 2
            partner = lax.ppermute(send, "tm", rolled_pairs(n_tm, 0, 1))
            goal = [[heads[2 * n + y] // 2 for n in range(pairs_here)] for y in range(2)]
            tables = []
            for away in range(half):
                tables.append([0] * n_tm)
                for y in range(2):
                    for n, z in enumerate(goal[y]):
                        tables[-1][((z + away) % half) * 2 + y] = n
            chunks = kernel_call(
                functools.partial(chunks_body, tables),
                [shape((2 * rows, HS), f32 if away == 0 else bf16) for away in range(half)],
                (keep, partner),
                after=earlier,
                flops=CHUNK_FLOPS if index == 0 else 1,
            )
            parcels = [chunks[0]]
            for away in range(1, half):
                routes = [(((z + away) % half) * 2 + y, z * 2 + y) for y in range(2) for z in goal[y]]
                parcels.append(lax.ppermute(chunks[away], "tm", routes))
            if index < len(SETS) - 1:
                parcels = kernel_call(total_body, [shape((2 * rows, HS), f32)], parcels)
            earlier = (*parcels, *pieces)
            sums.append(parcels)
    if aligned:
        belongs = [[j in heads for heads in SETS].index(True) for j in range(n_tm)]
        ours, theirs = kernel_call(
            functools.partial(final_body, belongs, [len(parcels) for parcels in sums]),
            [shape((rows, HS), f32)] * 2,
            [parcel for parcels in sums for parcel in parcels],
            after=(result, grad_query),
        )
    else:
        order = [h for heads in SETS for h in heads]
        partial = jnp.concatenate([part[0] for part in partials], axis=1)
        partial = jnp.concatenate([partial[:, order.index(h) * HS : (order.index(h) + 1) * HS] for h in range(H)], axis=1)
        whole = lax.psum_scatter(partial, "tm", scatter_dimension=1, tiled=True)
        ours, theirs = (lax.dynamic_slice_in_dim(whole, side * rows, rows, 0) for side in (core, 1 - core))
    key_total, value_total = kernel_call(
        choose_body, [shape(ours.shape, f32)] * 2, (ours, exchanged(theirs))
    )

    return (grad_query[None], result[None], key_total, value_total)


def solution(mesh):
    return jax.shard_map(
        shards,
        mesh=mesh,
        in_specs=(
            P("fsdp", "tm", None),
            P("fsdp", "tm", None),
            P("fsdp", "tm", None),
            P("fsdp", "tm", None),
            P("fsdp", "tm", None),
            P("fsdp", None),
            P("fsdp", None),
            P("tm", None, None),
            P("tm"),
        ),
        out_specs=(P("fsdp", "tm", None), P("fsdp", "tm", None), P("fsdp", "tm"), P("fsdp", "tm")),
        check_vma=False,
    )
```

time: 141 us -> 137 us (0.972)
  the two profiles are of different devices: /device:TPU:0 before, /device:TPU:25 now
where the time goes in v3:
time: 137 us
  starting transfers between devices  59 us (43%)
  waiting for transfers between devices  52.4 us (38%)
  Pallas kernels  20 us (15%)
  local copies, waits for them, and re-layouts  2.62 us (2%)
  between operations  1.6 us (1%)
    pallas_call x19, Pallas kernels, kernel_call(): pl.pallas_call(run, out_shape=tuple(outs), in_specs=[VMEM] * count + [ANY...  20 us
    ppermute x6, waiting for transfers between devices, shards(): parcels.append(lax.ppermute(chunks[away], 'tm', routes))  19.5 us
    ppermute x6, starting transfers between devices, shards(): parcels.append(lax.ppermute(chunks[away], 'tm', routes))  18.5 us
    ppermute x5, waiting for transfers between devices, shifted(): lax.ppermute(value, axis, [(s, s + steps) for s in range(max(0, -steps),...  15.8 us
    ppermute x5, starting transfers between devices, shifted(): lax.ppermute(value, axis, [(s, s + steps) for s in range(max(0, -steps),...  13.2 us
    ppermute x6, starting transfers between devices, exchanged(): return lax.ppermute(array, 'fsdp', rolled_pairs(n_fsdp, 0, 1))  6.81 us
    ppermute x1, waiting for transfers between devices, shards(): even = lax.ppermute(first, 'tm', [(2 * z + 1, 2 * z) for z in range(half)])  6.68 us
    ppermute x1, starting transfers between devices, shards(): pair = lax.ppermute(own, 'tm', rolled_pairs(n_tm, 0, 1))  5.45 us
  transfers between devices with their start and end apart: 28, of which 15 were waited for; matrix products, arithmetic and copies ran while one was open for 0% of the time, Pallas kernels for 9%

profile of v3, /device:TPU:25, one launch (start us, length us, event | category | flops | bytes accessed | tf_op | source)
XLA Modules:
  0.0 136.6 jit_solution(4723976567585356394)
XLA Ops:
  1.3 0.7 fusion.1
  2.0 0.1 reshape.22
  2.1 1.3 slice_bitcast_fusion
  3.4 0.2 maximum_maximum_fusion.refs_0_
  3.6 2.2 %collective-permute-start.1 = (bf16[144,2048]{1,0:T(8,128)(2,1)S(1)}, bf16[144,2048]{1,0:T(8,128)(2,1)S(1)}, u32[]{:S(2)}, u32[]{:S(2)}) collective-permute-start(bf16[144,2048]{1,0:T(8,128)(2,1)S(1)} %maximum_maximum_fusion.refs_0_), channel_id=1, source_target_pairs={{8,0},{12,4},{16,8},{20,12},{24,16},{28,20},{9,1},{13,5},{17,9},{2... | collective-permute-start | bytes 1769480 | tf_op jit(solution)/shard_map/ppermute | solution.py:63
  5.9 1.3 collective-permute-start.3
  7.2 0.3 shard_map.120
  7.5 1.3 collective-permute-start.6
  8.8 1.3 collective-permute-start
  10.1 7.7 %collective-permute-done.1.refs_9_ = bf16[144,2048]{1,0:T(8,128)(2,1)S(1)} collective-permute-done((bf16[144,2048]{1,0:T(8,128)(2,1)S(1)}, bf16[144,2048]{1,0:T(8,128)(2,1)S(1)}, u32[]{:S(2)}, u32[]{:S(2)}) %collective-permute-start.1) | collective-permute-done | bytes 589856 | tf_op jit(solution)/shard_map/ppermute | solution.py:63
  17.8 3.2 %collective-permute-start.2 = (bf16[144,2048]{1,0:T(8,128)(2,1)S(1)}, bf16[144,2048]{1,0:T(8,128)(2,1)S(1)}, u32[]{:S(2)}, u32[]{:S(2)}) collective-permute-start(bf16[144,2048]{1,0:T(8,128)(2,1)S(1)} %collective-permute-done.1.refs_9_), channel_id=1, source_target_pairs={{0,4},{8,12},{16,20},{24,28},{1,5},{9,13},{17,21},{25,29},{2,6},{1... | collective-permute-start | bytes 1769480 | tf_op jit(solution)/shard_map/ppermute | solution.py:398
  20.9 1.9 %collective-permute-start.5 = (bf16[1024,256]{1,0:T(8,128)(2,1)S(1)}, bf16[1024,256]{1,0:T(8,128)(2,1)S(1)}, u32[]{:S(2)}, u32[]{:S(2)}) collective-permute-start(bf16[1024,256]{1,0:T(8,128)(2,1)S(1)} %get-tuple-element.40.refs_10_.refs_0_), channel_id=1, source_target_pairs={{1,0},{0,1},{3,2},{2,3},{5,4},{4,5},{7,6},{6,7},{9,8},{8,9},{11,10... | collective-permute-start | bytes 1572872 | tf_op jit(solution)/shard_map/ppermute | solution.py:389
  22.8 0.7 collective-permute-start.4
  23.5 0.1 collective-permute-start.7
  23.6 0.7 collective-permute-done.5.refs_11_.refs_1_
  24.4 6.7 %collective-permute-done.refs_5_ = bf16[144,2048]{1,0:T(8,128)(2,1)S(1)} collective-permute-done((bf16[144,2048]{1,0:T(8,128)(2,1)S(1)}, bf16[144,2048]{1,0:T(8,128)(2,1)S(1)}, u32[]{:S(2)}, u32[]{:S(2)}) %collective-permute-start) | collective-permute-done | bytes 589856 | tf_op jit(solution)/shard_map/ppermute | solution.py:397
  31.0 0.9 collective-permute-done.2.refs_6_
  32.0 2.6 %shard_map.121 = (f32[24,640]{1,0:T(8,128)S(1)}, f32[256,640]{1,0:T(8,128)S(1)}) custom-call(bf16[144,2048]{1,0:T(8,128)(2,1)S(1)} %maximum_maximum_fusion.refs_0_, bf16[256,1024]{1,0:T(8,128)(2,1)S(1)} %bitcast.28, bf16[256,1024]{1,0:T(8,128)(2,1)S(1)} %bitcast.31, bf16[256,1024]{1,0:T(8,128)(2,1)S(1)} %bitcast.34, bf16[256,1024]{1,0:T(8,128)(2,1)S(1)} %bitcast.25, ...), custom_call_target="tpu_custom_call" | custom-call | flops 1 | bytes 1 | tf_op jit(solution)/shard_map/pallas_call | solution.py:37
  34.6 5.4 %collective-permute-start.8 = (f32[24,640]{1,0:T(8,128)S(1)}, f32[24,640]{1,0:T(8,128)S(1)}, u32[]{:S(2)}, u32[]{:S(2)}) collective-permute-start(f32[24,640]{1,0:T(8,128)S(1)} %get-tuple-element.43.refs_0_.refs_10_), channel_id=1, source_target_pairs={{4,0},{0,4},{12,8},{8,12},{20,16},{16,20},{28,24},{24,28},{5,1},{1... | collective-permute-start | bytes 184328 | tf_op jit(solution)/shard_map/ppermute | solution.py:419
  40.0 1.6 %collective-permute-done.8.refs_1_.refs_11_ = f32[24,640]{1,0:T(8,128)S(1)} collective-permute-done((f32[24,640]{1,0:T(8,128)S(1)}, f32[24,640]{1,0:T(8,128)S(1)}, u32[]{:S(2)}, u32[]{:S(2)}) %collective-permute-start.8) | collective-permute-done | bytes 61472 | tf_op jit(solution)/shard_map/ppermute | solution.py:419
  41.7 1.3 collective-permute-start.9
  43.0 4.7 %collective-permute-start.10 = (f32[24,512]{1,0:T(8,128)S(1)}, f32[24,512]{1,0:T(8,128)S(1)}, u32[]{:S(2)}, u32[]{:S(2)}) collective-permute-start(f32[24,512]{1,0:T(8,128)S(1)} %get-tuple-element.45), channel_id=1, source_target_pairs={{8,0},{12,4},{16,8},{20,12},{24,16},{28,20},{9,1},{13,5},{17,9},{2... | collective-permute-start | bytes 147464 | tf_op jit(solution)/shard_map/ppermute | solution.py:63
  47.7 1.1 collective-permute-done.10.refs_13_
  48.9 4.4 %shard_map.123 = (bf16[256,1024]{1,0:T(8,128)(2,1)S(1)}, bf16[256,1024]{1,0:T(8,128)(2,1)S(1)}, f32[24,640]{1,0:T(8,128)S(1)}) custom-call(f32[256,640]{1,0:T(8,128)S(1)} %get-tuple-element.42.refs_0_, bf16[256,1024]{1,0:T(8,128)(2,1)S(1)} %bitcast.29, bf16[256,1024]{1,0:T(8,128)(2,1)S(1)} %bitcast.32, bf16[256,1024]{1,0:T(8,128)(2,1)S(1)} %bitcast.35, ...), custom_call_target="tpu_custom_call" | custom-call | flops 1 | bytes 1 | tf_op jit(solution)/shard_map/pallas_call | solution.py:37
  53.2 2.6 %collective-permute-start.11 = (bf16[256,1024]{1,0:T(8,128)(2,1)S(1)}, bf16[256,1024]{1,0:T(8,128)(2,1)S(1)}, u32[]{:S(2)}, u32[]{:S(2)}) collective-permute-start(bf16[256,1024]{1,0:T(8,128)(2,1)S(1)} %get-tuple-element.48), channel_id=1, source_target_pairs={{1,0},{0,1},{3,2},{2,3},{5,4},{4,5},{7,6},{6,7},{9,8},{8,9},{11,10... | collective-permute-start | bytes 1572872 | tf_op jit(solution)/shard_map/ppermute | solution.py:389
  55.8 0.3 shard_map.127
  56.1 0.1 collective-permute-start.14
  56.3 1.1 collective-permute-done.11.refs_1_
  57.4 1.3 collective-permute-start.15
  58.7 3.8 %shard_map.125 = (f32[256,1024]{1,0:T(8,128)S(1)}, bf16[256,1024]{1,0:T(8,128)(2,1)S(1)}, bf16[128,1024]{1,0:T(8,128)(2,1)S(1)}) custom-call(f32[256,640]{1,0:T(8,128)S(1)} %get-tuple-element.42.refs_0_, bf16[256,1024]{1,0:T(8,128)(2,1)S(1)} %bitcast.30, bf16[256,1024]{1,0:T(8,128)(2,1)S(1)} %bitcast.33, bf16[256,1024]{1,0:T(8,128)(2,1)S(1)} %bitcast.36, ...), custom_call_target="tpu_custom_call" | custom-call | flops 1 | bytes 1 | tf_op jit(solution)/shard_map/pallas_call | solution.py:37
  62.5 3.7 %collective-permute-start.12 = (bf16[256,1024]{1,0:T(8,128)(2,1)S(1)}, bf16[256,1024]{1,0:T(8,128)(2,1)S(1)}, u32[]{:S(2)}, u32[]{:S(2)}) collective-permute-start(bf16[256,1024]{1,0:T(8,128)(2,1)S(1)} %get-tuple-element.52), channel_id=1, source_target_pairs={{0,4},{4,8},{8,12},{12,16},{16,20},{20,24},{24,28},{1,5},{5,9},{9,... | collective-permute-start | bytes 1572872 | tf_op jit(solution)/shard_map/ppermute | solution.py:63
  66.1 0.3 collective-permute-start.16
  66.4 4.2 %collective-permute-done.15.refs_5_.refs_3_ = bf16[512,512]{1,0:T(8,128)(2,1)S(1)} collective-permute-done((bf16[512,512]{1,0:T(8,128)(2,1)S(1)}, bf16[512,512]{1,0:T(8,128)(2,1)S(1)}, u32[]{:S(2)}, u32[]{:S(2)}) %collective-permute-start.15) | collective-permute-done | bytes 524320 | tf_op jit(solution)/shard_map/ppermute | solution.py:431
  70.6 1.3 shard_map.128
  71.9 1.8 %collective-permute-start.19 = (bf16[1024,256]{1,0:T(8,128)(2,1)S(1)}, bf16[1024,256]{1,0:T(8,128)(2,1)S(1)}, u32[]{:S(2)}, u32[]{:S(2)}) collective-permute-start(bf16[1024,256]{1,0:T(8,128)(2,1)S(1)} %get-tuple-element.56.refs_1_), channel_id=1, source_target_pairs={{4,0},{0,4},{12,8},{8,12},{20,16},{16,20},{28,24},{24,28},{5,1},{1... | collective-permute-start | bytes 1572872 | tf_op jit(solution)/shard_map/ppermute | solution.py:482
  73.7 1.3 collective-permute-start.13
  75.0 7.0 %collective-permute-done.13.refs_2_.refs_3_ = bf16[128,1024]{1,0:T(8,128)(2,1)S(1)} collective-permute-done((bf16[128,1024]{1,0:T(8,128)(2,1)S(1)}, bf16[128,1024]{1,0:T(8,128)(2,1)S(1)}, u32[]{:S(2)}, u32[]{:S(2)}) %collective-permute-start.13) | collective-permute-done | bytes 262176 | tf_op jit(solution)/shard_map/ppermute | solution.py:63
  82.0 1.3 shard_map.130
  83.3 3.6 %collective-permute-start.23 = (bf16[1024,256]{1,0:T(8,128)(2,1)S(1)}, bf16[1024,256]{1,0:T(8,128)(2,1)S(1)}, u32[]{:S(2)}, u32[]{:S(2)}) collective-permute-start(bf16[1024,256]{1,0:T(8,128)(2,1)S(1)} %get-tuple-element.57.refs_6_), channel_id=1, source_target_pairs={{4,0},{0,4},{12,8},{8,12},{20,16},{16,20},{28,24},{24,28},{5,1},{1... | collective-permute-start | bytes 1572872 | tf_op jit(solution)/shard_map/ppermute | solution.py:482
  86.9 2.4 %shard_map.131 = (f32[512,1024]{1,0:T(8,128)S(1)}, bf16[512,1024]{1,0:T(8,128)(2,1)S(1)}) custom-call(bf16[512,1024]{1,0:T(8,128)(2,1)S(1)} %get-tuple-element.54.refs_0_, bf16[512,1024]{1,0:T(8,128)(2,1)S(1)} %collective-permute-done.14.refs_1_, bf16[512,512]{1,0:T(8,128)(2,1)S(1)} %get-tuple-element.49.refs_11_.refs_4_.refs_2_, ...), custom_call_target="tpu_custom_call" | custom-call | flops 1 | bytes 1 | tf_op jit(solution)/shard_map/pallas_call | solution.py:37
  89.3 1.6 %collective-permute-start.17 = (bf16[512,1024]{1,0:T(8,128)(2,1)S(1)}, bf16[512,1024]{1,0:T(8,128)(2,1)S(1)}, u32[]{:S(2)}, u32[]{:S(2)}) collective-permute-start(bf16[512,1024]{1,0:T(8,128)(2,1)S(1)} %get-tuple-element.59), channel_id=1, source_target_pairs={{1,0},{0,1},{3,2},{2,3},{5,4},{4,5},{7,6},{6,7},{9,8},{8,9},{11,10... | collective-permute-start | bytes 3145736 | tf_op jit(solution)/shard_map/ppermute | solution.py:389
  90.8 0.7 collective-permute-done.19.refs_1_
  91.5 0.2 shard_map.134
  91.7 3.6 %collective-permute-start.20 = (bf16[1024,128]{1,0:T(8,128)(2,1)S(1)}, bf16[1024,128]{1,0:T(8,128)(2,1)S(1)}, u32[]{:S(2)}, u32[]{:S(2)}) collective-permute-start(bf16[1024,128]{1,0:T(8,128)(2,1)S(1)} %get-tuple-element.64), channel_id=1, source_target_pairs={{8,0},{24,16},{20,12},{4,28},{9,1},{25,17},{21,13},{5,29},{10,2},{... | collective-permute-start | bytes 786440 | tf_op jit(solution)/shard_map/ppermute | solution.py:500
  95.4 0.7 collective-permute-start.21
  96.1 4.6 %collective-permute-start.22 = (bf16[1024,128]{1,0:T(8,128)(2,1)S(1)}, bf16[1024,128]{1,0:T(8,128)(2,1)S(1)}, u32[]{:S(2)}, u32[]{:S(2)}) collective-permute-start(bf16[1024,128]{1,0:T(8,128)(2,1)S(1)} %get-tuple-element.66), channel_id=1, source_target_pairs={{24,0},{8,16},{4,12},{20,28},{25,1},{9,17},{5,13},{21,29},{26,2},{... | collective-permute-start | bytes 786440 | tf_op jit(solution)/shard_map/ppermute | solution.py:500
  100.7 0.2 shard_map.132
  100.9 0.3 collective-permute-start.18
  101.2 4.8 %collective-permute-done.22.refs_3_ = bf16[1024,128]{1,0:T(8,128)(2,1)S(1)} collective-permute-done((bf16[1024,128]{1,0:T(8,128)(2,1)S(1)}, bf16[1024,128]{1,0:T(8,128)(2,1)S(1)}, u32[]{:S(2)}, u32[]{:S(2)}) %collective-permute-start.22) | collective-permute-done | bytes 262176 | tf_op jit(solution)/shard_map/ppermute | solution.py:500
  106.1 0.1 shard_map.135.refs_2_.refs_0_
  106.2 0.2 shard_map.136
  106.4 1.3 collective-permute-start.24
  107.7 7.0 %collective-permute-start.25 = (bf16[1024,128]{1,0:T(8,128)(2,1)S(1)}, bf16[1024,128]{1,0:T(8,128)(2,1)S(1)}, u32[]{:S(2)}, u32[]{:S(2)}) collective-permute-start(bf16[1024,128]{1,0:T(8,128)(2,1)S(1)} %get-tuple-element.70), channel_id=1, source_target_pairs={{24,8},{8,24},{20,4},{4,20},{25,9},{9,25},{21,5},{5,21},{26,10},{1... | collective-permute-start | bytes 786440 | tf_op jit(solution)/shard_map/ppermute | solution.py:500
  114.7 1.3 collective-permute-start.26
  116.0 0.9 shard_map.126.refs_6_
  117.0 1.1 shard_map.133.refs_5_
  118.0 1.4 %collective-permute-done.24.refs_2_ = bf16[1024,128]{1,0:T(8,128)(2,1)S(1)} collective-permute-done((bf16[1024,128]{1,0:T(8,128)(2,1)S(1)}, bf16[1024,128]{1,0:T(8,128)(2,1)S(1)}, u32[]{:S(2)}, u32[]{:S(2)}) %collective-permute-start.24) | collective-permute-done | bytes 262176 | tf_op jit(solution)/shard_map/ppermute | solution.py:500
  119.4 7.7 %collective-permute-done.25.refs_3_ = bf16[1024,128]{1,0:T(8,128)(2,1)S(1)} collective-permute-done((bf16[1024,128]{1,0:T(8,128)(2,1)S(1)}, bf16[1024,128]{1,0:T(8,128)(2,1)S(1)}, u32[]{:S(2)}, u32[]{:S(2)}) %collective-permute-start.25) | collective-permute-done | bytes 262176 | tf_op jit(solution)/shard_map/ppermute | solution.py:500
  127.1 5.6 %collective-permute-done.26.refs_4_ = bf16[1024,128]{1,0:T(8,128)(2,1)S(1)} collective-permute-done((bf16[1024,128]{1,0:T(8,128)(2,1)S(1)}, bf16[1024,128]{1,0:T(8,128)(2,1)S(1)}, u32[]{:S(2)}, u32[]{:S(2)}) %collective-permute-start.26) | collective-permute-done | bytes 262176 | tf_op jit(solution)/shard_map/ppermute | solution.py:500
  132.7 1.2 copy-done.4
  133.9 0.1 shard_map.137
  134.0 0.6 collective-permute-start.27
  134.6 1.2 collective-permute-done.27.refs_1_
  135.7 0.8 shard_map.138
  (36 shorter events, 0.2 us)
Async XLA Ops:
  3.3 3.8 %copy-start.6 = (bf16[1,256,2048]{2,1,0:T(8,128)(2,1)S(1)}, bf16[1,256,2048]{2,1,0:T(8,128)(2,1)}, u32[]{:S(2)}) copy-start(bf16[1,256,2048]{2,1,0:T(8,128)(2,1)} %param.9) | copy-start | bytes 3145732
  3.5 28.4 %copy-start = (bf16[1,256,1024]{2,1,0:T(8,128)(2,1)S(1)}, bf16[1,256,1024]{2,1,0:T(8,128)(2,1)}, u32[]{:S(2)}) copy-start(bf16[1,256,1024]{2,1,0:T(8,128)(2,1)} %param.13) | copy-start | bytes 1572868
  3.5 28.4 %copy-start.1 = (bf16[1,256,1024]{2,1,0:T(8,128)(2,1)S(1)}, bf16[1,256,1024]{2,1,0:T(8,128)(2,1)}, u32[]{:S(2)}) copy-start(bf16[1,256,1024]{2,1,0:T(8,128)(2,1)} %param.10) | copy-start | bytes 1572868
  3.5 28.4 %copy-start.2 = (bf16[1,256,1024]{2,1,0:T(8,128)(2,1)S(1)}, bf16[1,256,1024]{2,1,0:T(8,128)(2,1)}, u32[]{:S(2)}) copy-start(bf16[1,256,1024]{2,1,0:T(8,128)(2,1)} %param.11) | copy-start | bytes 1572868
  3.6 28.4 %copy-start.3 = (bf16[1,256,1024]{2,1,0:T(8,128)(2,1)S(1)}, bf16[1,256,1024]{2,1,0:T(8,128)(2,1)}, u32[]{:S(2)}) copy-start(bf16[1,256,1024]{2,1,0:T(8,128)(2,1)} %param.12) | copy-start | bytes 1572868
  3.6 14.2 %collective-permute-start.1 = (bf16[144,2048]{1,0:T(8,128)(2,1)S(1)}, bf16[144,2048]{1,0:T(8,128)(2,1)S(1)}, u32[]{:S(2)}, u32[]{:S(2)}) collective-permute-start(bf16[144,2048]{1,0:T(8,128)(2,1)S(1)} %maximum_maximum_fusion.refs_0_), channel_id=1, source_target_pairs={{8,0},{12,4},{16,8},{20,12},{24,16},{28,20},{9,1},{13,5},{17,9},{2... | collective-permute-start | bytes 1769480 | tf_op jit(solution)/shard_map/ppermute | solution.py:63
  5.9 17.0 %collective-permute-start.3 = (bf16[128,2048]{1,0:T(8,128)(2,1)S(1)}, bf16[128,2048]{1,0:T(8,128)(2,1)S(1)}, u32[]{:S(2)}, u32[]{:S(2)}) collective-permute-start(bf16[128,2048]{1,0:T(8,128)(2,1)S(1)} %pad_maximum_fusion), channel_id=1, source_target_pairs={{4,0},{0,4},{12,8},{8,12},{20,16},{16,20},{28,24},{24,28},{5,1},{1... | collective-permute-start | bytes 1572872 | tf_op jit(solution)/shard_map/ppermute | solution.py:396
  7.5 16.0 %collective-permute-start.6 = (bf16[1024,256]{1,0:T(8,128)(2,1)S(1)}, bf16[1024,256]{1,0:T(8,128)(2,1)S(1)}, u32[]{:S(2)}, u32[]{:S(2)}) collective-permute-start(bf16[1024,256]{1,0:T(8,128)(2,1)S(1)} %get-tuple-element.41), channel_id=1, source_target_pairs={{2,0},{3,1},{0,2},{1,3},{6,4},{7,5},{4,6},{5,7},{10,8},{11,9},{8,1... | collective-permute-start | bytes 1572872 | tf_op jit(solution)/shard_map/ppermute | solution.py:409
  8.8 22.3 %collective-permute-start = (bf16[144,2048]{1,0:T(8,128)(2,1)S(1)}, bf16[144,2048]{1,0:T(8,128)(2,1)S(1)}, u32[]{:S(2)}, u32[]{:S(2)}) collective-permute-start(bf16[144,2048]{1,0:T(8,128)(2,1)S(1)} %maximum_maximum_fusion.refs_0_), channel_id=1, source_target_pairs={{4,0},{12,8},{20,16},{28,24},{5,1},{13,9},{21,17},{29,25},{6,2},{1... | collective-permute-start | bytes 1769480 | tf_op jit(solution)/shard_map/ppermute | solution.py:397
  17.8 14.2 %collective-permute-start.2 = (bf16[144,2048]{1,0:T(8,128)(2,1)S(1)}, bf16[144,2048]{1,0:T(8,128)(2,1)S(1)}, u32[]{:S(2)}, u32[]{:S(2)}) collective-permute-start(bf16[144,2048]{1,0:T(8,128)(2,1)S(1)} %collective-permute-done.1.refs_9_), channel_id=1, source_target_pairs={{0,4},{8,12},{16,20},{24,28},{1,5},{9,13},{17,21},{25,29},{2,6},{1... | collective-permute-start | bytes 1769480 | tf_op jit(solution)/shard_map/ppermute | solution.py:398
  20.9 3.4 %collective-permute-start.5 = (bf16[1024,256]{1,0:T(8,128)(2,1)S(1)}, bf16[1024,256]{1,0:T(8,128)(2,1)S(1)}, u32[]{:S(2)}, u32[]{:S(2)}) collective-permute-start(bf16[1024,256]{1,0:T(8,128)(2,1)S(1)} %get-tuple-element.40.refs_10_.refs_0_), channel_id=1, source_target_pairs={{1,0},{0,1},{3,2},{2,3},{5,4},{4,5},{7,6},{6,7},{9,8},{8,9},{11,10... | collective-permute-start | bytes 1572872 | tf_op jit(solution)/shard_map/ppermute | solution.py:389
  22.8 8.2 %collective-permute-start.4 = (bf16[128,2048]{1,0:T(8,128)(2,1)S(1)}, bf16[128,2048]{1,0:T(8,128)(2,1)S(1)}, u32[]{:S(2)}, u32[]{:S(2)}) collective-permute-start(bf16[128,2048]{1,0:T(8,128)(2,1)S(1)} %collective-permute-done.3.refs_7_), channel_id=1, source_target_pairs={{12,4},{20,12},{28,20},{13,5},{21,13},{29,21},{14,6},{22,14},{30,2... | collective-permute-start | bytes 1572872 | tf_op jit(solution)/shard_map/ppermute | solution.py:399
  23.5 7.5 %collective-permute-start.7 = (bf16[1024,256]{1,0:T(8,128)(2,1)S(1)}, bf16[1024,256]{1,0:T(8,128)(2,1)S(1)}, u32[]{:S(2)}, u32[]{:S(2)}) collective-permute-start(bf16[1024,256]{1,0:T(8,128)(2,1)S(1)} %collective-permute-done.6.refs_12_.refs_2_), channel_id=1, source_target_pairs={{1,0},{0,1},{3,2},{2,3},{5,4},{4,5},{7,6},{6,7},{9,8},{8,9},{11,10... | collective-permute-start | bytes 1572872 | tf_op jit(solution)/shard_map/ppermute | solution.py:389
  34.6 7.1 %collective-permute-start.8 = (f32[24,640]{1,0:T(8,128)S(1)}, f32[24,640]{1,0:T(8,128)S(1)}, u32[]{:S(2)}, u32[]{:S(2)}) collective-permute-start(f32[24,640]{1,0:T(8,128)S(1)} %get-tuple-element.43.refs_0_.refs_10_), channel_id=1, source_target_pairs={{4,0},{0,4},{12,8},{8,12},{20,16},{16,20},{28,24},{24,28},{5,1},{1... | collective-permute-start | bytes 184328 | tf_op jit(solution)/shard_map/ppermute | solution.py:419
  41.7 6.0 %collective-permute-start.9 = (f32[24,512]{1,0:T(8,128)S(1)}, f32[24,512]{1,0:T(8,128)S(1)}, u32[]{:S(2)}, u32[]{:S(2)}) collective-permute-start(f32[24,512]{1,0:T(8,128)S(1)} %get-tuple-element.44), channel_id=1, source_target_pairs={{0,8},{4,12},{8,16},{12,20},{16,24},{20,28},{1,9},{5,13},{9,17},{1... | collective-permute-start | bytes 147464 | tf_op jit(solution)/shard_map/ppermute | solution.py:63
  43.0 5.9 %collective-permute-start.10 = (f32[24,512]{1,0:T(8,128)S(1)}, f32[24,512]{1,0:T(8,128)S(1)}, u32[]{:S(2)}, u32[]{:S(2)}) collective-permute-start(f32[24,512]{1,0:T(8,128)S(1)} %get-tuple-element.45), channel_id=1, source_target_pairs={{8,0},{12,4},{16,8},{20,12},{24,16},{28,20},{9,1},{13,5},{17,9},{2... | collective-permute-start | bytes 147464 | tf_op jit(solution)/shard_map/ppermute | solution.py:63
  48.9 7.0 %copy-start.7 = (bf16[512,1024]{1,0:T(8,128)(2,1)S(1)}, bf16[512,1024]{1,0:T(8,128)(2,1)}, u32[]{:S(2)}) copy-start(bf16[512,1024]{1,0:T(8,128)(2,1)} %refs_0_.1) | copy-start | bytes 3145732
  48.9 7.0 %copy-start.8 = (bf16[512,1024]{1,0:T(8,128)(2,1)S(1)}, bf16[512,1024]{1,0:T(8,128)(2,1)}, u32[]{:S(2)}) copy-start(bf16[512,1024]{1,0:T(8,128)(2,1)} %refs_1_.1) | copy-start | bytes 3145732
  53.2 4.1 %collective-permute-start.11 = (bf16[256,1024]{1,0:T(8,128)(2,1)S(1)}, bf16[256,1024]{1,0:T(8,128)(2,1)S(1)}, u32[]{:S(2)}, u32[]{:S(2)}) collective-permute-start(bf16[256,1024]{1,0:T(8,128)(2,1)S(1)} %get-tuple-element.48), channel_id=1, source_target_pairs={{1,0},{0,1},{3,2},{2,3},{5,4},{4,5},{7,6},{6,7},{9,8},{8,9},{11,10... | collective-permute-start | bytes 1572872 | tf_op jit(solution)/shard_map/ppermute | solution.py:389
  56.1 30.8 %collective-permute-start.14 = (bf16[512,1024]{1,0:T(8,128)(2,1)S(1)}, bf16[512,1024]{1,0:T(8,128)(2,1)S(1)}, u32[]{:S(2)}, u32[]{:S(2)}) collective-permute-start(bf16[512,1024]{1,0:T(8,128)(2,1)S(1)} %get-tuple-element.55), channel_id=1, source_target_pairs={{1,0},{0,1},{3,2},{2,3},{5,4},{4,5},{7,6},{6,7},{9,8},{8,9},{11,10... | collective-permute-start | bytes 3145736 | tf_op jit(solution)/shard_map/ppermute | solution.py:389
  57.4 13.2 %collective-permute-start.15 = (bf16[512,512]{1,0:T(8,128)(2,1)S(1)}, bf16[512,512]{1,0:T(8,128)(2,1)S(1)}, u32[]{:S(2)}, u32[]{:S(2)}) collective-permute-start(bf16[512,512]{1,0:T(8,128)(2,1)S(1)} %get-tuple-element.49.refs_11_.refs_4_.refs_2_), channel_id=1, source_target_pairs={{2,0},{3,1},{0,2},{1,3},{6,4},{7,5},{4,6},{5,7},{10,8},{11,9},{8,1... | collective-permute-start | bytes 1572872 | tf_op jit(solution)/shard_map/ppermute | solution.py:431
  62.5 19.5 %collective-permute-start.12 = (bf16[256,1024]{1,0:T(8,128)(2,1)S(1)}, bf16[256,1024]{1,0:T(8,128)(2,1)S(1)}, u32[]{:S(2)}, u32[]{:S(2)}) collective-permute-start(bf16[256,1024]{1,0:T(8,128)(2,1)S(1)} %get-tuple-element.52), channel_id=1, source_target_pairs={{0,4},{4,8},{8,12},{12,16},{16,20},{20,24},{24,28},{1,5},{5,9},{9,... | collective-permute-start | bytes 1572872 | tf_op jit(solution)/shard_map/ppermute | solution.py:63
  66.1 15.9 %collective-permute-start.16 = (bf16[512,512]{1,0:T(8,128)(2,1)S(1)}, bf16[512,512]{1,0:T(8,128)(2,1)S(1)}, u32[]{:S(2)}, u32[]{:S(2)}) collective-permute-start(bf16[512,512]{1,0:T(8,128)(2,1)S(1)} %get-tuple-element.50.refs_12_.refs_4_), channel_id=1, source_target_pairs={{2,0},{3,1},{0,2},{1,3},{6,4},{7,5},{4,6},{5,7},{10,8},{11,9},{8,1... | collective-permute-start | bytes 1572872 | tf_op jit(solution)/shard_map/ppermute | solution.py:431
  71.9 19.6 %collective-permute-start.19 = (bf16[1024,256]{1,0:T(8,128)(2,1)S(1)}, bf16[1024,256]{1,0:T(8,128)(2,1)S(1)}, u32[]{:S(2)}, u32[]{:S(2)}) collective-permute-start(bf16[1024,256]{1,0:T(8,128)(2,1)S(1)} %get-tuple-element.56.refs_1_), channel_id=1, source_target_pairs={{4,0},{0,4},{12,8},{8,12},{20,16},{16,20},{28,24},{24,28},{5,1},{1... | collective-permute-start | bytes 1572872 | tf_op jit(solution)/shard_map/ppermute | solution.py:482
  73.7 8.3 %collective-permute-start.13 = (bf16[128,1024]{1,0:T(8,128)(2,1)S(1)}, bf16[128,1024]{1,0:T(8,128)(2,1)S(1)}, u32[]{:S(2)}, u32[]{:S(2)}) collective-permute-start(bf16[128,1024]{1,0:T(8,128)(2,1)S(1)} %get-tuple-element.53), channel_id=1, source_target_pairs={{0,8},{4,12},{8,16},{12,20},{16,24},{20,28},{1,9},{5,13},{9,17},{1... | collective-permute-start | bytes 786440 | tf_op jit(solution)/shard_map/ppermute | solution.py:63
  83.3 22.9 %collective-permute-start.23 = (bf16[1024,256]{1,0:T(8,128)(2,1)S(1)}, bf16[1024,256]{1,0:T(8,128)(2,1)S(1)}, u32[]{:S(2)}, u32[]{:S(2)}) collective-permute-start(bf16[1024,256]{1,0:T(8,128)(2,1)S(1)} %get-tuple-element.57.refs_6_), channel_id=1, source_target_pairs={{4,0},{0,4},{12,8},{8,12},{20,16},{16,20},{28,24},{24,28},{5,1},{1... | collective-permute-start | bytes 1572872 | tf_op jit(solution)/shard_map/ppermute | solution.py:482
  89.3 11.4 %collective-permute-start.17 = (bf16[512,1024]{1,0:T(8,128)(2,1)S(1)}, bf16[512,1024]{1,0:T(8,128)(2,1)S(1)}, u32[]{:S(2)}, u32[]{:S(2)}) collective-permute-start(bf16[512,1024]{1,0:T(8,128)(2,1)S(1)} %get-tuple-element.59), channel_id=1, source_target_pairs={{1,0},{0,1},{3,2},{2,3},{5,4},{4,5},{7,6},{6,7},{9,8},{8,9},{11,10... | collective-permute-start | bytes 3145736 | tf_op jit(solution)/shard_map/ppermute | solution.py:389
  91.7 9.5 %collective-permute-start.20 = (bf16[1024,128]{1,0:T(8,128)(2,1)S(1)}, bf16[1024,128]{1,0:T(8,128)(2,1)S(1)}, u32[]{:S(2)}, u32[]{:S(2)}) collective-permute-start(bf16[1024,128]{1,0:T(8,128)(2,1)S(1)} %get-tuple-element.64), channel_id=1, source_target_pairs={{8,0},{24,16},{20,12},{4,28},{9,1},{25,17},{21,13},{5,29},{10,2},{... | collective-permute-start | bytes 786440 | tf_op jit(solution)/shard_map/ppermute | solution.py:500
  95.4 5.9 %collective-permute-start.21 = (bf16[1024,128]{1,0:T(8,128)(2,1)S(1)}, bf16[1024,128]{1,0:T(8,128)(2,1)S(1)}, u32[]{:S(2)}, u32[]{:S(2)}) collective-permute-start(bf16[1024,128]{1,0:T(8,128)(2,1)S(1)} %get-tuple-element.65), channel_id=1, source_target_pairs={{16,0},{0,16},{28,12},{12,28},{17,1},{1,17},{29,13},{13,29},{18,2}... | collective-permute-start | bytes 786440 | tf_op jit(solution)/shard_map/ppermute | solution.py:500
  96.1 10.0 %collective-permute-start.22 = (bf16[1024,128]{1,0:T(8,128)(2,1)S(1)}, bf16[1024,128]{1,0:T(8,128)(2,1)S(1)}, u32[]{:S(2)}, u32[]{:S(2)}) collective-permute-start(bf16[1024,128]{1,0:T(8,128)(2,1)S(1)} %get-tuple-element.66), channel_id=1, source_target_pairs={{24,0},{8,16},{4,12},{20,28},{25,1},{9,17},{5,13},{21,29},{26,2},{... | collective-permute-start | bytes 786440 | tf_op jit(solution)/shard_map/ppermute | solution.py:500
  100.9 16.1 %collective-permute-start.18 = (bf16[256,1024]{1,0:T(8,128)(2,1)S(1)}, bf16[256,1024]{1,0:T(8,128)(2,1)S(1)}, u32[]{:S(2)}, u32[]{:S(2)}) collective-permute-start(bf16[256,1024]{1,0:T(8,128)(2,1)S(1)} %get-tuple-element.61.refs_4_), channel_id=1, source_target_pairs={{0,2},{1,3},{2,0},{3,1},{4,6},{5,7},{6,4},{7,5},{8,10},{9,11},{10,... | collective-permute-start | bytes 1572872 | tf_op jit(solution)/shard_map/ppermute | solution.py:473
  106.4 13.0 %collective-permute-start.24 = (bf16[1024,128]{1,0:T(8,128)(2,1)S(1)}, bf16[1024,128]{1,0:T(8,128)(2,1)S(1)}, u32[]{:S(2)}, u32[]{:S(2)}) collective-permute-start(bf16[1024,128]{1,0:T(8,128)(2,1)S(1)} %get-tuple-element.69), channel_id=1, source_target_pairs={{16,8},{0,24},{12,4},{28,20},{17,9},{1,25},{13,5},{29,21},{18,10},... | collective-permute-start | bytes 786440 | tf_op jit(solution)/shard_map/ppermute | solution.py:500
  107.7 19.4 %collective-permute-start.25 = (bf16[1024,128]{1,0:T(8,128)(2,1)S(1)}, bf16[1024,128]{1,0:T(8,128)(2,1)S(1)}, u32[]{:S(2)}, u32[]{:S(2)}) collective-permute-start(bf16[1024,128]{1,0:T(8,128)(2,1)S(1)} %get-tuple-element.70), channel_id=1, source_target_pairs={{24,8},{8,24},{20,4},{4,20},{25,9},{9,25},{21,5},{5,21},{26,10},{1... | collective-permute-start | bytes 786440 | tf_op jit(solution)/shard_map/ppermute | solution.py:500
  114.7 18.0 %collective-permute-start.26 = (bf16[1024,128]{1,0:T(8,128)(2,1)S(1)}, bf16[1024,128]{1,0:T(8,128)(2,1)S(1)}, u32[]{:S(2)}, u32[]{:S(2)}) collective-permute-start(bf16[1024,128]{1,0:T(8,128)(2,1)S(1)} %get-tuple-element.71), channel_id=1, source_target_pairs={{0,8},{16,24},{28,4},{12,20},{1,9},{17,25},{29,5},{13,21},{2,10},{... | collective-permute-start | bytes 786440 | tf_op jit(solution)/shard_map/ppermute | solution.py:500
  116.9 15.7 %copy-start.5 = (bf16[256,1024]{1,0:T(8,128)(2,1)S(1)}, bf16[256,1024]{1,0:T(8,128)(2,1)}, u32[]{:S(2)}) copy-start(bf16[256,1024]{1,0:T(8,128)(2,1)} %shard_map.126.refs_6_) | copy-start | bytes 1572868
  132.7 1.2 copy-start.4
  134.0 1.7 %collective-permute-start.27 = (f32[512,128]{1,0:T(8,128)S(1)}, f32[512,128]{1,0:T(8,128)S(1)}, u32[]{:S(2)}, u32[]{:S(2)}) collective-permute-start(f32[512,128]{1,0:T(8,128)S(1)} %get-tuple-element.73), channel_id=1, source_target_pairs={{1,0},{0,1},{3,2},{2,3},{5,4},{4,5},{7,6},{6,7},{9,8},{8,9},{11,10... | collective-permute-start | bytes 786440 | tf_op jit(solution)/shard_map/ppermute | solution.py:389

commit v4 on v3

--- a/solution.py
+++ b/solution.py
@@ -339,14 +339,6 @@
             sent[...] = b[...]
 
 
-def total_body(*refs):
-    total = None
-    for part in refs[:-1]:
-        term = part[...].astype(jnp.float32)
-        total = term if total is None else total + term
-    refs[-1][...] = total
-
-
 def grouped(refs, sizes):
     groups, start = [], 0
     for size in sizes:
@@ -476,7 +468,7 @@
     (grad_query,) = kernel_call(query_body, [shape((tokens, HD), bf16)], (dq0, near_terms, far_terms))
 
     if aligned:
-        sums, earlier = [], ()
+        sums = []
         for index, (heads, (send, keep)) in enumerate(zip(SETS, partials)):
             pairs_here = len(heads) // 2
             partner = lax.ppermute(send, "tm", rolled_pairs(n_tm, 0, 1))
@@ -491,16 +483,13 @@
                 functools.partial(chunks_body, tables),
                 [shape((2 * rows, HS), f32 if away == 0 else bf16) for away in range(half)],
                 (keep, partner),
-                after=earlier,
-                flops=CHUNK_FLOPS if index == 0 else 1,
+                after=pieces if index else (),
+                flops=CHUNK_FLOPS,
             )
             parcels = [chunks[0]]
             for away in range(1, half):
                 routes = [(((z + away) % half) * 2 + y, z * 2 + y) for y in range(2) for z in goal[y]]
                 parcels.append(lax.ppermute(chunks[away], "tm", routes))
-            if index < len(SETS) - 1:
-                parcels = kernel_call(total_body, [shape((2 * rows, HS), f32)], parcels)
-            earlier = (*parcels, *pieces)
             sums.append(parcels)
     if aligned:
         belongs = [[j in heads for heads in SETS].index(True) for j in range(n_tm)]

time: 137 us -> 132 us (0.964)
  waiting for transfers between devices: 52.4 us -> 46.1 us
  starting transfers between devices: 59 us -> 60.7 us
    ppermute x6, waiting for transfers between devices: 19.5 us -> 11.5 us  [shards(): parcels.append(lax.ppermute(chunks[away], 'tm', routes))]
    ppermute x6, starting transfers between devices: 18.5 us -> 20.3 us  [shards(): parcels.append(lax.ppermute(chunks[away], 'tm', routes))]
    ppermute x2, waiting for transfers between devices: 0.67 us -> 2.23 us  [shards(): partner = lax.ppermute(send, 'tm', rolled_pairs(n_tm, 0, 1))]
    pallas_call x19 -> x18, Pallas kernels: 20 us -> 19.9 us  [kernel_call(): pl.pallas_call(run, out_shape=tuple(outs), in_specs=[VMEM] * count + [ANY...]
where the time goes in v4:
time: 132 us
  starting transfers between devices  60.7 us (46%)
  waiting for transfers between devices  46.1 us (35%)
  Pallas kernels  19.9 us (15%)
  local copies, waits for them, and re-layouts  2.62 us (2%)
  between operations  1.61 us (1%)
    ppermute x6, starting transfers between devices, shards(): parcels.append(lax.ppermute(chunks[away], 'tm', routes))  20.3 us
    pallas_call x18, Pallas kernels, kernel_call(): pl.pallas_call(run, out_shape=tuple(outs), in_specs=[VMEM] * count + [ANY...  19.9 us
    ppermute x5, waiting for transfers between devices, shifted(): lax.ppermute(value, axis, [(s, s + steps) for s in range(max(0, -steps),...  15.9 us
    ppermute x5, starting transfers between devices, shifted(): lax.ppermute(value, axis, [(s, s + steps) for s in range(max(0, -steps),...  13.2 us
    ppermute x6, waiting for transfers between devices, shards(): parcels.append(lax.ppermute(chunks[away], 'tm', routes))  11.5 us
    ppermute x6, starting transfers between devices, exchanged(): return lax.ppermute(array, 'fsdp', rolled_pairs(n_fsdp, 0, 1))  6.82 us
    ppermute x1, waiting for transfers between devices, shards(): even = lax.ppermute(first, 'tm', [(2 * z + 1, 2 * z) for z in range(half)])  6.68 us
    ppermute x1, starting transfers between devices, shards(): pair = lax.ppermute(own, 'tm', rolled_pairs(n_tm, 0, 1))  5.45 us
  transfers between devices with their start and end apart: 28, of which 15 were waited for; matrix products, arithmetic and copies ran while one was open for 0% of the time, Pallas kernels for 9%

profile of v4, /device:TPU:25, one launch (start us, length us, event | category | flops | bytes accessed | tf_op | source)
XLA Modules:
  0.0 131.9 jit_solution(6556732427506430562)
XLA Ops:
  1.3 0.7 fusion.1
  2.0 0.1 reshape.22
  2.1 1.3 slice_bitcast_fusion
  3.4 0.2 maximum_maximum_fusion.refs_0_
  3.6 2.2 %collective-permute-start.1 = (bf16[144,2048]{1,0:T(8,128)(2,1)S(1)}, bf16[144,2048]{1,0:T(8,128)(2,1)S(1)}, u32[]{:S(2)}, u32[]{:S(2)}) collective-permute-start(bf16[144,2048]{1,0:T(8,128)(2,1)S(1)} %maximum_maximum_fusion.refs_0_), channel_id=1, source_target_pairs={{8,0},{12,4},{16,8},{20,12},{24,16},{28,20},{9,1},{13,5},{17,9},{2... | collective-permute-start | bytes 1769480 | tf_op jit(solution)/shard_map/ppermute | solution.py:63
  5.9 1.3 collective-permute-start.3
  7.2 0.3 shard_map.120
  7.5 1.3 collective-permute-start.6
  8.8 1.3 collective-permute-start
  10.1 7.7 %collective-permute-done.1.refs_9_ = bf16[144,2048]{1,0:T(8,128)(2,1)S(1)} collective-permute-done((bf16[144,2048]{1,0:T(8,128)(2,1)S(1)}, bf16[144,2048]{1,0:T(8,128)(2,1)S(1)}, u32[]{:S(2)}, u32[]{:S(2)}) %collective-permute-start.1) | collective-permute-done | bytes 589856 | tf_op jit(solution)/shard_map/ppermute | solution.py:63
  17.8 3.2 %collective-permute-start.2 = (bf16[144,2048]{1,0:T(8,128)(2,1)S(1)}, bf16[144,2048]{1,0:T(8,128)(2,1)S(1)}, u32[]{:S(2)}, u32[]{:S(2)}) collective-permute-start(bf16[144,2048]{1,0:T(8,128)(2,1)S(1)} %collective-permute-done.1.refs_9_), channel_id=1, source_target_pairs={{0,4},{8,12},{16,20},{24,28},{1,5},{9,13},{17,21},{25,29},{2,6},{1... | collective-permute-start | bytes 1769480 | tf_op jit(solution)/shard_map/ppermute | solution.py:390
  20.9 1.9 %collective-permute-start.5 = (bf16[1024,256]{1,0:T(8,128)(2,1)S(1)}, bf16[1024,256]{1,0:T(8,128)(2,1)S(1)}, u32[]{:S(2)}, u32[]{:S(2)}) collective-permute-start(bf16[1024,256]{1,0:T(8,128)(2,1)S(1)} %get-tuple-element.40.refs_10_.refs_0_), channel_id=1, source_target_pairs={{1,0},{0,1},{3,2},{2,3},{5,4},{4,5},{7,6},{6,7},{9,8},{8,9},{11,10... | collective-permute-start | bytes 1572872 | tf_op jit(solution)/shard_map/ppermute | solution.py:381
  22.8 0.7 collective-permute-start.4
  23.5 0.1 collective-permute-start.7
  23.6 0.7 collective-permute-done.5.refs_11_.refs_1_
  24.4 6.7 %collective-permute-done.refs_5_ = bf16[144,2048]{1,0:T(8,128)(2,1)S(1)} collective-permute-done((bf16[144,2048]{1,0:T(8,128)(2,1)S(1)}, bf16[144,2048]{1,0:T(8,128)(2,1)S(1)}, u32[]{:S(2)}, u32[]{:S(2)}) %collective-permute-start) | collective-permute-done | bytes 589856 | tf_op jit(solution)/shard_map/ppermute | solution.py:389
  31.0 0.9 collective-permute-done.2.refs_6_
  32.0 2.6 %shard_map.121 = (f32[24,640]{1,0:T(8,128)S(1)}, f32[256,640]{1,0:T(8,128)S(1)}) custom-call(bf16[144,2048]{1,0:T(8,128)(2,1)S(1)} %maximum_maximum_fusion.refs_0_, bf16[256,1024]{1,0:T(8,128)(2,1)S(1)} %bitcast.28, bf16[256,1024]{1,0:T(8,128)(2,1)S(1)} %bitcast.31, bf16[256,1024]{1,0:T(8,128)(2,1)S(1)} %bitcast.34, bf16[256,1024]{1,0:T(8,128)(2,1)S(1)} %bitcast.25, ...), custom_call_target="tpu_custom_call" | custom-call | flops 1 | bytes 1 | tf_op jit(solution)/shard_map/pallas_call | solution.py:37
  34.6 5.4 %collective-permute-start.8 = (f32[24,640]{1,0:T(8,128)S(1)}, f32[24,640]{1,0:T(8,128)S(1)}, u32[]{:S(2)}, u32[]{:S(2)}) collective-permute-start(f32[24,640]{1,0:T(8,128)S(1)} %get-tuple-element.43.refs_0_.refs_10_), channel_id=1, source_target_pairs={{4,0},{0,4},{12,8},{8,12},{20,16},{16,20},{28,24},{24,28},{5,1},{1... | collective-permute-start | bytes 184328 | tf_op jit(solution)/shard_map/ppermute | solution.py:411
  40.0 1.6 %collective-permute-done.8.refs_1_.refs_11_ = f32[24,640]{1,0:T(8,128)S(1)} collective-permute-done((f32[24,640]{1,0:T(8,128)S(1)}, f32[24,640]{1,0:T(8,128)S(1)}, u32[]{:S(2)}, u32[]{:S(2)}) %collective-permute-start.8) | collective-permute-done | bytes 61472 | tf_op jit(solution)/shard_map/ppermute | solution.py:411
  41.7 1.3 collective-permute-start.9
  43.0 4.7 %collective-permute-start.10 = (f32[24,512]{1,0:T(8,128)S(1)}, f32[24,512]{1,0:T(8,128)S(1)}, u32[]{:S(2)}, u32[]{:S(2)}) collective-permute-start(f32[24,512]{1,0:T(8,128)S(1)} %get-tuple-element.45), channel_id=1, source_target_pairs={{8,0},{12,4},{16,8},{20,12},{24,16},{28,20},{9,1},{13,5},{17,9},{2... | collective-permute-start | bytes 147464 | tf_op jit(solution)/shard_map/ppermute | solution.py:63
  47.7 1.1 collective-permute-done.10.refs_13_
  48.9 4.4 %shard_map.123 = (bf16[256,1024]{1,0:T(8,128)(2,1)S(1)}, bf16[256,1024]{1,0:T(8,128)(2,1)S(1)}, f32[24,640]{1,0:T(8,128)S(1)}) custom-call(f32[256,640]{1,0:T(8,128)S(1)} %get-tuple-element.42.refs_0_, bf16[256,1024]{1,0:T(8,128)(2,1)S(1)} %bitcast.29, bf16[256,1024]{1,0:T(8,128)(2,1)S(1)} %bitcast.32, bf16[256,1024]{1,0:T(8,128)(2,1)S(1)} %bitcast.35, ...), custom_call_target="tpu_custom_call" | custom-call | flops 1 | bytes 1 | tf_op jit(solution)/shard_map/pallas_call | solution.py:37
  53.2 2.6 %collective-permute-start.11 = (bf16[256,1024]{1,0:T(8,128)(2,1)S(1)}, bf16[256,1024]{1,0:T(8,128)(2,1)S(1)}, u32[]{:S(2)}, u32[]{:S(2)}) collective-permute-start(bf16[256,1024]{1,0:T(8,128)(2,1)S(1)} %get-tuple-element.48), channel_id=1, source_target_pairs={{1,0},{0,1},{3,2},{2,3},{5,4},{4,5},{7,6},{6,7},{9,8},{8,9},{11,10... | collective-permute-start | bytes 1572872 | tf_op jit(solution)/shard_map/ppermute | solution.py:381
  55.8 0.3 shard_map.127
  56.2 0.1 collective-permute-start.14
  56.3 1.1 collective-permute-done.11.refs_1_
  57.4 0.1 shard_map.124
  57.4 1.3 collective-permute-start.15
  58.7 3.8 %shard_map.125 = (f32[256,1024]{1,0:T(8,128)S(1)}, bf16[256,1024]{1,0:T(8,128)(2,1)S(1)}, bf16[128,1024]{1,0:T(8,128)(2,1)S(1)}) custom-call(f32[256,640]{1,0:T(8,128)S(1)} %get-tuple-element.42.refs_0_, bf16[256,1024]{1,0:T(8,128)(2,1)S(1)} %bitcast.30, bf16[256,1024]{1,0:T(8,128)(2,1)S(1)} %bitcast.33, bf16[256,1024]{1,0:T(8,128)(2,1)S(1)} %bitcast.36, ...), custom_call_target="tpu_custom_call" | custom-call | flops 1 | bytes 1 | tf_op jit(solution)/shard_map/pallas_call | solution.py:37
  62.5 3.7 %collective-permute-start.12 = (bf16[256,1024]{1,0:T(8,128)(2,1)S(1)}, bf16[256,1024]{1,0:T(8,128)(2,1)S(1)}, u32[]{:S(2)}, u32[]{:S(2)}) collective-permute-start(bf16[256,1024]{1,0:T(8,128)(2,1)S(1)} %get-tuple-element.52), channel_id=1, source_target_pairs={{0,4},{4,8},{8,12},{12,16},{16,20},{20,24},{24,28},{1,5},{5,9},{9,... | collective-permute-start | bytes 1572872 | tf_op jit(solution)/shard_map/ppermute | solution.py:63
  66.2 0.3 collective-permute-start.16
  66.4 4.2 %collective-permute-done.15.refs_5_.refs_3_ = bf16[512,512]{1,0:T(8,128)(2,1)S(1)} collective-permute-done((bf16[512,512]{1,0:T(8,128)(2,1)S(1)}, bf16[512,512]{1,0:T(8,128)(2,1)S(1)}, u32[]{:S(2)}, u32[]{:S(2)}) %collective-permute-start.15) | collective-permute-done | bytes 524320 | tf_op jit(solution)/shard_map/ppermute | solution.py:423
  70.6 1.3 shard_map.128
  71.9 1.8 %collective-permute-start.19 = (bf16[1024,256]{1,0:T(8,128)(2,1)S(1)}, bf16[1024,256]{1,0:T(8,128)(2,1)S(1)}, u32[]{:S(2)}, u32[]{:S(2)}) collective-permute-start(bf16[1024,256]{1,0:T(8,128)(2,1)S(1)} %get-tuple-element.56.refs_1_), channel_id=1, source_target_pairs={{4,0},{0,4},{12,8},{8,12},{20,16},{16,20},{28,24},{24,28},{5,1},{1... | collective-permute-start | bytes 1572872 | tf_op jit(solution)/shard_map/ppermute | solution.py:474
  73.7 1.3 collective-permute-start.13
  75.0 7.0 %collective-permute-done.13.refs_2_.refs_3_ = bf16[128,1024]{1,0:T(8,128)(2,1)S(1)} collective-permute-done((bf16[128,1024]{1,0:T(8,128)(2,1)S(1)}, bf16[128,1024]{1,0:T(8,128)(2,1)S(1)}, u32[]{:S(2)}, u32[]{:S(2)}) %collective-permute-start.13) | collective-permute-done | bytes 262176 | tf_op jit(solution)/shard_map/ppermute | solution.py:63
  82.0 1.3 shard_map.130
  83.3 3.6 %collective-permute-start.23 = (bf16[1024,256]{1,0:T(8,128)(2,1)S(1)}, bf16[1024,256]{1,0:T(8,128)(2,1)S(1)}, u32[]{:S(2)}, u32[]{:S(2)}) collective-permute-start(bf16[1024,256]{1,0:T(8,128)(2,1)S(1)} %get-tuple-element.57.refs_6_), channel_id=1, source_target_pairs={{4,0},{0,4},{12,8},{8,12},{20,16},{16,20},{28,24},{24,28},{5,1},{1... | collective-permute-start | bytes 1572872 | tf_op jit(solution)/shard_map/ppermute | solution.py:474
  86.9 2.4 %shard_map.131 = (f32[512,1024]{1,0:T(8,128)S(1)}, bf16[512,1024]{1,0:T(8,128)(2,1)S(1)}) custom-call(bf16[512,1024]{1,0:T(8,128)(2,1)S(1)} %get-tuple-element.54.refs_0_, bf16[512,1024]{1,0:T(8,128)(2,1)S(1)} %collective-permute-done.14.refs_1_, bf16[512,512]{1,0:T(8,128)(2,1)S(1)} %get-tuple-element.49.refs_11_.refs_4_.refs_2_, ...), custom_call_target="tpu_custom_call" | custom-call | flops 1 | bytes 1 | tf_op jit(solution)/shard_map/pallas_call | solution.py:37
  89.3 1.5 %collective-permute-start.17 = (bf16[512,1024]{1,0:T(8,128)(2,1)S(1)}, bf16[512,1024]{1,0:T(8,128)(2,1)S(1)}, u32[]{:S(2)}, u32[]{:S(2)}) collective-permute-start(bf16[512,1024]{1,0:T(8,128)(2,1)S(1)} %get-tuple-element.59), channel_id=1, source_target_pairs={{1,0},{0,1},{3,2},{2,3},{5,4},{4,5},{7,6},{6,7},{9,8},{8,9},{11,10... | collective-permute-start | bytes 3145736 | tf_op jit(solution)/shard_map/ppermute | solution.py:381
  90.8 0.7 collective-permute-done.19.refs_1_
  91.5 0.2 shard_map.134
  91.7 3.6 %collective-permute-start.20 = (bf16[1024,128]{1,0:T(8,128)(2,1)S(1)}, bf16[1024,128]{1,0:T(8,128)(2,1)S(1)}, u32[]{:S(2)}, u32[]{:S(2)}) collective-permute-start(bf16[1024,128]{1,0:T(8,128)(2,1)S(1)} %get-tuple-element.64), channel_id=1, source_target_pairs={{8,0},{24,16},{20,12},{4,28},{9,1},{25,17},{21,13},{5,29},{10,2},{... | collective-permute-start | bytes 786440 | tf_op jit(solution)/shard_map/ppermute | solution.py:492
  95.4 0.7 collective-permute-start.21
  96.1 4.6 %collective-permute-start.22 = (bf16[1024,128]{1,0:T(8,128)(2,1)S(1)}, bf16[1024,128]{1,0:T(8,128)(2,1)S(1)}, u32[]{:S(2)}, u32[]{:S(2)}) collective-permute-start(bf16[1024,128]{1,0:T(8,128)(2,1)S(1)} %get-tuple-element.66), channel_id=1, source_target_pairs={{24,0},{8,16},{4,12},{20,28},{25,1},{9,17},{5,13},{21,29},{26,2},{... | collective-permute-start | bytes 786440 | tf_op jit(solution)/shard_map/ppermute | solution.py:492
  100.7 0.2 shard_map.132
  100.9 0.3 collective-permute-start.18
  101.2 1.6 %collective-permute-done.23.refs_1_ = bf16[1024,256]{1,0:T(8,128)(2,1)S(1)} collective-permute-done((bf16[1024,256]{1,0:T(8,128)(2,1)S(1)}, bf16[1024,256]{1,0:T(8,128)(2,1)S(1)}, u32[]{:S(2)}, u32[]{:S(2)}) %collective-permute-start.23) | collective-permute-done | bytes 524320 | tf_op jit(solution)/shard_map/ppermute | solution.py:474
  102.8 0.2 shard_map.135
  103.0 1.3 collective-permute-start.24
  104.3 8.8 %collective-permute-start.25 = (bf16[1024,128]{1,0:T(8,128)(2,1)S(1)}, bf16[1024,128]{1,0:T(8,128)(2,1)S(1)}, u32[]{:S(2)}, u32[]{:S(2)}) collective-permute-start(bf16[1024,128]{1,0:T(8,128)(2,1)S(1)} %get-tuple-element.70), channel_id=1, source_target_pairs={{24,8},{8,24},{20,4},{4,20},{25,9},{9,25},{21,5},{5,21},{26,10},{1... | collective-permute-start | bytes 786440 | tf_op jit(solution)/shard_map/ppermute | solution.py:492
  113.1 0.1 collective-permute-done.18.refs_1_
  113.2 1.3 collective-permute-start.26
  114.5 0.9 shard_map.126.refs_9_
  115.4 1.1 shard_map.133.refs_8_
  116.5 5.9 %collective-permute-done.25.refs_6_ = bf16[1024,128]{1,0:T(8,128)(2,1)S(1)} collective-permute-done((bf16[1024,128]{1,0:T(8,128)(2,1)S(1)}, bf16[1024,128]{1,0:T(8,128)(2,1)S(1)}, u32[]{:S(2)}, u32[]{:S(2)}) %collective-permute-start.25) | collective-permute-done | bytes 262176 | tf_op jit(solution)/shard_map/ppermute | solution.py:492
  122.4 5.6 %collective-permute-done.26.refs_7_ = bf16[1024,128]{1,0:T(8,128)(2,1)S(1)} collective-permute-done((bf16[1024,128]{1,0:T(8,128)(2,1)S(1)}, bf16[1024,128]{1,0:T(8,128)(2,1)S(1)}, u32[]{:S(2)}, u32[]{:S(2)}) %collective-permute-start.26) | collective-permute-done | bytes 262176 | tf_op jit(solution)/shard_map/ppermute | solution.py:492
  128.0 1.2 copy-done.4
  129.2 0.1 shard_map.136
  129.3 0.6 collective-permute-start.27
  129.9 1.2 collective-permute-done.27.refs_1_
  131.0 0.8 shard_map.137
  (35 shorter events, 0.2 us)
Async XLA Ops:
  3.3 3.8 %copy-start.6 = (bf16[1,256,2048]{2,1,0:T(8,128)(2,1)S(1)}, bf16[1,256,2048]{2,1,0:T(8,128)(2,1)}, u32[]{:S(2)}) copy-start(bf16[1,256,2048]{2,1,0:T(8,128)(2,1)} %param.9) | copy-start | bytes 3145732
  3.5 28.4 %copy-start = (bf16[1,256,1024]{2,1,0:T(8,128)(2,1)S(1)}, bf16[1,256,1024]{2,1,0:T(8,128)(2,1)}, u32[]{:S(2)}) copy-start(bf16[1,256,1024]{2,1,0:T(8,128)(2,1)} %param.13) | copy-start | bytes 1572868
  3.5 28.4 %copy-start.1 = (bf16[1,256,1024]{2,1,0:T(8,128)(2,1)S(1)}, bf16[1,256,1024]{2,1,0:T(8,128)(2,1)}, u32[]{:S(2)}) copy-start(bf16[1,256,1024]{2,1,0:T(8,128)(2,1)} %param.10) | copy-start | bytes 1572868
  3.5 28.4 %copy-start.2 = (bf16[1,256,1024]{2,1,0:T(8,128)(2,1)S(1)}, bf16[1,256,1024]{2,1,0:T(8,128)(2,1)}, u32[]{:S(2)}) copy-start(bf16[1,256,1024]{2,1,0:T(8,128)(2,1)} %param.11) | copy-start | bytes 1572868
  3.6 28.4 %copy-start.3 = (bf16[1,256,1024]{2,1,0:T(8,128)(2,1)S(1)}, bf16[1,256,1024]{2,1,0:T(8,128)(2,1)}, u32[]{:S(2)}) copy-start(bf16[1,256,1024]{2,1,0:T(8,128)(2,1)} %param.12) | copy-start | bytes 1572868
  3.6 14.2 %collective-permute-start.1 = (bf16[144,2048]{1,0:T(8,128)(2,1)S(1)}, bf16[144,2048]{1,0:T(8,128)(2,1)S(1)}, u32[]{:S(2)}, u32[]{:S(2)}) collective-permute-start(bf16[144,2048]{1,0:T(8,128)(2,1)S(1)} %maximum_maximum_fusion.refs_0_), channel_id=1, source_target_pairs={{8,0},{12,4},{16,8},{20,12},{24,16},{28,20},{9,1},{13,5},{17,9},{2... | collective-permute-start | bytes 1769480 | tf_op jit(solution)/shard_map/ppermute | solution.py:63
  5.9 17.0 %collective-permute-start.3 = (bf16[128,2048]{1,0:T(8,128)(2,1)S(1)}, bf16[128,2048]{1,0:T(8,128)(2,1)S(1)}, u32[]{:S(2)}, u32[]{:S(2)}) collective-permute-start(bf16[128,2048]{1,0:T(8,128)(2,1)S(1)} %pad_maximum_fusion), channel_id=1, source_target_pairs={{4,0},{0,4},{12,8},{8,12},{20,16},{16,20},{28,24},{24,28},{5,1},{1... | collective-permute-start | bytes 1572872 | tf_op jit(solution)/shard_map/ppermute | solution.py:388
  7.5 16.0 %collective-permute-start.6 = (bf16[1024,256]{1,0:T(8,128)(2,1)S(1)}, bf16[1024,256]{1,0:T(8,128)(2,1)S(1)}, u32[]{:S(2)}, u32[]{:S(2)}) collective-permute-start(bf16[1024,256]{1,0:T(8,128)(2,1)S(1)} %get-tuple-element.41), channel_id=1, source_target_pairs={{2,0},{3,1},{0,2},{1,3},{6,4},{7,5},{4,6},{5,7},{10,8},{11,9},{8,1... | collective-permute-start | bytes 1572872 | tf_op jit(solution)/shard_map/ppermute | solution.py:401
  8.8 22.3 %collective-permute-start = (bf16[144,2048]{1,0:T(8,128)(2,1)S(1)}, bf16[144,2048]{1,0:T(8,128)(2,1)S(1)}, u32[]{:S(2)}, u32[]{:S(2)}) collective-permute-start(bf16[144,2048]{1,0:T(8,128)(2,1)S(1)} %maximum_maximum_fusion.refs_0_), channel_id=1, source_target_pairs={{4,0},{12,8},{20,16},{28,24},{5,1},{13,9},{21,17},{29,25},{6,2},{1... | collective-permute-start | bytes 1769480 | tf_op jit(solution)/shard_map/ppermute | solution.py:389
  17.8 14.2 %collective-permute-start.2 = (bf16[144,2048]{1,0:T(8,128)(2,1)S(1)}, bf16[144,2048]{1,0:T(8,128)(2,1)S(1)}, u32[]{:S(2)}, u32[]{:S(2)}) collective-permute-start(bf16[144,2048]{1,0:T(8,128)(2,1)S(1)} %collective-permute-done.1.refs_9_), channel_id=1, source_target_pairs={{0,4},{8,12},{16,20},{24,28},{1,5},{9,13},{17,21},{25,29},{2,6},{1... | collective-permute-start | bytes 1769480 | tf_op jit(solution)/shard_map/ppermute | solution.py:390
  20.9 3.4 %collective-permute-start.5 = (bf16[1024,256]{1,0:T(8,128)(2,1)S(1)}, bf16[1024,256]{1,0:T(8,128)(2,1)S(1)}, u32[]{:S(2)}, u32[]{:S(2)}) collective-permute-start(bf16[1024,256]{1,0:T(8,128)(2,1)S(1)} %get-tuple-element.40.refs_10_.refs_0_), channel_id=1, source_target_pairs={{1,0},{0,1},{3,2},{2,3},{5,4},{4,5},{7,6},{6,7},{9,8},{8,9},{11,10... | collective-permute-start | bytes 1572872 | tf_op jit(solution)/shard_map/ppermute | solution.py:381
  22.8 8.2 %collective-permute-start.4 = (bf16[128,2048]{1,0:T(8,128)(2,1)S(1)}, bf16[128,2048]{1,0:T(8,128)(2,1)S(1)}, u32[]{:S(2)}, u32[]{:S(2)}) collective-permute-start(bf16[128,2048]{1,0:T(8,128)(2,1)S(1)} %collective-permute-done.3.refs_7_), channel_id=1, source_target_pairs={{12,4},{20,12},{28,20},{13,5},{21,13},{29,21},{14,6},{22,14},{30,2... | collective-permute-start | bytes 1572872 | tf_op jit(solution)/shard_map/ppermute | solution.py:391
  23.5 7.5 %collective-permute-start.7 = (bf16[1024,256]{1,0:T(8,128)(2,1)S(1)}, bf16[1024,256]{1,0:T(8,128)(2,1)S(1)}, u32[]{:S(2)}, u32[]{:S(2)}) collective-permute-start(bf16[1024,256]{1,0:T(8,128)(2,1)S(1)} %collective-permute-done.6.refs_12_.refs_2_), channel_id=1, source_target_pairs={{1,0},{0,1},{3,2},{2,3},{5,4},{4,5},{7,6},{6,7},{9,8},{8,9},{11,10... | collective-permute-start | bytes 1572872 | tf_op jit(solution)/shard_map/ppermute | solution.py:381
  34.6 7.1 %collective-permute-start.8 = (f32[24,640]{1,0:T(8,128)S(1)}, f32[24,640]{1,0:T(8,128)S(1)}, u32[]{:S(2)}, u32[]{:S(2)}) collective-permute-start(f32[24,640]{1,0:T(8,128)S(1)} %get-tuple-element.43.refs_0_.refs_10_), channel_id=1, source_target_pairs={{4,0},{0,4},{12,8},{8,12},{20,16},{16,20},{28,24},{24,28},{5,1},{1... | collective-permute-start | bytes 184328 | tf_op jit(solution)/shard_map/ppermute | solution.py:411
  41.7 6.0 %collective-permute-start.9 = (f32[24,512]{1,0:T(8,128)S(1)}, f32[24,512]{1,0:T(8,128)S(1)}, u32[]{:S(2)}, u32[]{:S(2)}) collective-permute-start(f32[24,512]{1,0:T(8,128)S(1)} %get-tuple-element.44), channel_id=1, source_target_pairs={{0,8},{4,12},{8,16},{12,20},{16,24},{20,28},{1,9},{5,13},{9,17},{1... | collective-permute-start | bytes 147464 | tf_op jit(solution)/shard_map/ppermute | solution.py:63
  43.0 5.9 %collective-permute-start.10 = (f32[24,512]{1,0:T(8,128)S(1)}, f32[24,512]{1,0:T(8,128)S(1)}, u32[]{:S(2)}, u32[]{:S(2)}) collective-permute-start(f32[24,512]{1,0:T(8,128)S(1)} %get-tuple-element.45), channel_id=1, source_target_pairs={{8,0},{12,4},{16,8},{20,12},{24,16},{28,20},{9,1},{13,5},{17,9},{2... | collective-permute-start | bytes 147464 | tf_op jit(solution)/shard_map/ppermute | solution.py:63
  48.9 7.0 %copy-start.7 = (bf16[512,1024]{1,0:T(8,128)(2,1)S(1)}, bf16[512,1024]{1,0:T(8,128)(2,1)}, u32[]{:S(2)}) copy-start(bf16[512,1024]{1,0:T(8,128)(2,1)} %refs_0_.1) | copy-start | bytes 3145732
  48.9 7.0 %copy-start.8 = (bf16[512,1024]{1,0:T(8,128)(2,1)S(1)}, bf16[512,1024]{1,0:T(8,128)(2,1)}, u32[]{:S(2)}) copy-start(bf16[512,1024]{1,0:T(8,128)(2,1)} %refs_1_.1) | copy-start | bytes 3145732
  53.2 4.1 %collective-permute-start.11 = (bf16[256,1024]{1,0:T(8,128)(2,1)S(1)}, bf16[256,1024]{1,0:T(8,128)(2,1)S(1)}, u32[]{:S(2)}, u32[]{:S(2)}) collective-permute-start(bf16[256,1024]{1,0:T(8,128)(2,1)S(1)} %get-tuple-element.48), channel_id=1, source_target_pairs={{1,0},{0,1},{3,2},{2,3},{5,4},{4,5},{7,6},{6,7},{9,8},{8,9},{11,10... | collective-permute-start | bytes 1572872 | tf_op jit(solution)/shard_map/ppermute | solution.py:381
  56.2 30.8 %collective-permute-start.14 = (bf16[512,1024]{1,0:T(8,128)(2,1)S(1)}, bf16[512,1024]{1,0:T(8,128)(2,1)S(1)}, u32[]{:S(2)}, u32[]{:S(2)}) collective-permute-start(bf16[512,1024]{1,0:T(8,128)(2,1)S(1)} %get-tuple-element.55), channel_id=1, source_target_pairs={{1,0},{0,1},{3,2},{2,3},{5,4},{4,5},{7,6},{6,7},{9,8},{8,9},{11,10... | collective-permute-start | bytes 3145736 | tf_op jit(solution)/shard_map/ppermute | solution.py:381
  57.4 13.2 %collective-permute-start.15 = (bf16[512,512]{1,0:T(8,128)(2,1)S(1)}, bf16[512,512]{1,0:T(8,128)(2,1)S(1)}, u32[]{:S(2)}, u32[]{:S(2)}) collective-permute-start(bf16[512,512]{1,0:T(8,128)(2,1)S(1)} %get-tuple-element.49.refs_11_.refs_4_.refs_2_), channel_id=1, source_target_pairs={{2,0},{3,1},{0,2},{1,3},{6,4},{7,5},{4,6},{5,7},{10,8},{11,9},{8,1... | collective-permute-start | bytes 1572872 | tf_op jit(solution)/shard_map/ppermute | solution.py:423
  62.5 19.5 %collective-permute-start.12 = (bf16[256,1024]{1,0:T(8,128)(2,1)S(1)}, bf16[256,1024]{1,0:T(8,128)(2,1)S(1)}, u32[]{:S(2)}, u32[]{:S(2)}) collective-permute-start(bf16[256,1024]{1,0:T(8,128)(2,1)S(1)} %get-tuple-element.52), channel_id=1, source_target_pairs={{0,4},{4,8},{8,12},{12,16},{16,20},{20,24},{24,28},{1,5},{5,9},{9,... | collective-permute-start | bytes 1572872 | tf_op jit(solution)/shard_map/ppermute | solution.py:63
  66.2 15.9 %collective-permute-start.16 = (bf16[512,512]{1,0:T(8,128)(2,1)S(1)}, bf16[512,512]{1,0:T(8,128)(2,1)S(1)}, u32[]{:S(2)}, u32[]{:S(2)}) collective-permute-start(bf16[512,512]{1,0:T(8,128)(2,1)S(1)} %get-tuple-element.50.refs_12_.refs_4_), channel_id=1, source_target_pairs={{2,0},{3,1},{0,2},{1,3},{6,4},{7,5},{4,6},{5,7},{10,8},{11,9},{8,1... | collective-permute-start | bytes 1572872 | tf_op jit(solution)/shard_map/ppermute | solution.py:423
  71.9 19.6 %collective-permute-start.19 = (bf16[1024,256]{1,0:T(8,128)(2,1)S(1)}, bf16[1024,256]{1,0:T(8,128)(2,1)S(1)}, u32[]{:S(2)}, u32[]{:S(2)}) collective-permute-start(bf16[1024,256]{1,0:T(8,128)(2,1)S(1)} %get-tuple-element.56.refs_1_), channel_id=1, source_target_pairs={{4,0},{0,4},{12,8},{8,12},{20,16},{16,20},{28,24},{24,28},{5,1},{1... | collective-permute-start | bytes 1572872 | tf_op jit(solution)/shard_map/ppermute | solution.py:474
  73.7 8.3 %collective-permute-start.13 = (bf16[128,1024]{1,0:T(8,128)(2,1)S(1)}, bf16[128,1024]{1,0:T(8,128)(2,1)S(1)}, u32[]{:S(2)}, u32[]{:S(2)}) collective-permute-start(bf16[128,1024]{1,0:T(8,128)(2,1)S(1)} %get-tuple-element.53), channel_id=1, source_target_pairs={{0,8},{4,12},{8,16},{12,20},{16,24},{20,28},{1,9},{5,13},{9,17},{1... | collective-permute-start | bytes 786440 | tf_op jit(solution)/shard_map/ppermute | solution.py:63
  83.3 19.4 %collective-permute-start.23 = (bf16[1024,256]{1,0:T(8,128)(2,1)S(1)}, bf16[1024,256]{1,0:T(8,128)(2,1)S(1)}, u32[]{:S(2)}, u32[]{:S(2)}) collective-permute-start(bf16[1024,256]{1,0:T(8,128)(2,1)S(1)} %get-tuple-element.57.refs_6_), channel_id=1, source_target_pairs={{4,0},{0,4},{12,8},{8,12},{20,16},{16,20},{28,24},{24,28},{5,1},{1... | collective-permute-start | bytes 1572872 | tf_op jit(solution)/shard_map/ppermute | solution.py:474
  89.3 11.4 %collective-permute-start.17 = (bf16[512,1024]{1,0:T(8,128)(2,1)S(1)}, bf16[512,1024]{1,0:T(8,128)(2,1)S(1)}, u32[]{:S(2)}, u32[]{:S(2)}) collective-permute-start(bf16[512,1024]{1,0:T(8,128)(2,1)S(1)} %get-tuple-element.59), channel_id=1, source_target_pairs={{1,0},{0,1},{3,2},{2,3},{5,4},{4,5},{7,6},{6,7},{9,8},{8,9},{11,10... | collective-permute-start | bytes 3145736 | tf_op jit(solution)/shard_map/ppermute | solution.py:381
  91.7 12.5 %collective-permute-start.20 = (bf16[1024,128]{1,0:T(8,128)(2,1)S(1)}, bf16[1024,128]{1,0:T(8,128)(2,1)S(1)}, u32[]{:S(2)}, u32[]{:S(2)}) collective-permute-start(bf16[1024,128]{1,0:T(8,128)(2,1)S(1)} %get-tuple-element.64), channel_id=1, source_target_pairs={{8,0},{24,16},{20,12},{4,28},{9,1},{25,17},{21,13},{5,29},{10,2},{... | collective-permute-start | bytes 786440 | tf_op jit(solution)/shard_map/ppermute | solution.py:492
  95.4 21.1 %collective-permute-start.21 = (bf16[1024,128]{1,0:T(8,128)(2,1)S(1)}, bf16[1024,128]{1,0:T(8,128)(2,1)S(1)}, u32[]{:S(2)}, u32[]{:S(2)}) collective-permute-start(bf16[1024,128]{1,0:T(8,128)(2,1)S(1)} %get-tuple-element.65), channel_id=1, source_target_pairs={{16,0},{0,16},{28,12},{12,28},{17,1},{1,17},{29,13},{13,29},{18,2}... | collective-permute-start | bytes 786440 | tf_op jit(solution)/shard_map/ppermute | solution.py:492
  96.1 20.4 %collective-permute-start.22 = (bf16[1024,128]{1,0:T(8,128)(2,1)S(1)}, bf16[1024,128]{1,0:T(8,128)(2,1)S(1)}, u32[]{:S(2)}, u32[]{:S(2)}) collective-permute-start(bf16[1024,128]{1,0:T(8,128)(2,1)S(1)} %get-tuple-element.66), channel_id=1, source_target_pairs={{24,0},{8,16},{4,12},{20,28},{25,1},{9,17},{5,13},{21,29},{26,2},{... | collective-permute-start | bytes 786440 | tf_op jit(solution)/shard_map/ppermute | solution.py:492
  100.9 12.3 %collective-permute-start.18 = (bf16[256,1024]{1,0:T(8,128)(2,1)S(1)}, bf16[256,1024]{1,0:T(8,128)(2,1)S(1)}, u32[]{:S(2)}, u32[]{:S(2)}) collective-permute-start(bf16[256,1024]{1,0:T(8,128)(2,1)S(1)} %get-tuple-element.61.refs_3_), channel_id=1, source_target_pairs={{0,2},{1,3},{2,0},{3,1},{4,6},{5,7},{6,4},{7,5},{8,10},{9,11},{10,... | collective-permute-start | bytes 1572872 | tf_op jit(solution)/shard_map/ppermute | solution.py:465
  103.0 13.5 %collective-permute-start.24 = (bf16[1024,128]{1,0:T(8,128)(2,1)S(1)}, bf16[1024,128]{1,0:T(8,128)(2,1)S(1)}, u32[]{:S(2)}, u32[]{:S(2)}) collective-permute-start(bf16[1024,128]{1,0:T(8,128)(2,1)S(1)} %get-tuple-element.69), channel_id=1, source_target_pairs={{16,8},{0,24},{12,4},{28,20},{17,9},{1,25},{13,5},{29,21},{18,10},... | collective-permute-start | bytes 786440 | tf_op jit(solution)/shard_map/ppermute | solution.py:492
  104.3 18.1 %collective-permute-start.25 = (bf16[1024,128]{1,0:T(8,128)(2,1)S(1)}, bf16[1024,128]{1,0:T(8,128)(2,1)S(1)}, u32[]{:S(2)}, u32[]{:S(2)}) collective-permute-start(bf16[1024,128]{1,0:T(8,128)(2,1)S(1)} %get-tuple-element.70), channel_id=1, source_target_pairs={{24,8},{8,24},{20,4},{4,20},{25,9},{9,25},{21,5},{5,21},{26,10},{1... | collective-permute-start | bytes 786440 | tf_op jit(solution)/shard_map/ppermute | solution.py:492
  113.2 14.8 %collective-permute-start.26 = (bf16[1024,128]{1,0:T(8,128)(2,1)S(1)}, bf16[1024,128]{1,0:T(8,128)(2,1)S(1)}, u32[]{:S(2)}, u32[]{:S(2)}) collective-permute-start(bf16[1024,128]{1,0:T(8,128)(2,1)S(1)} %get-tuple-element.71), channel_id=1, source_target_pairs={{0,8},{16,24},{28,4},{12,20},{1,9},{17,25},{29,5},{13,21},{2,10},{... | collective-permute-start | bytes 786440 | tf_op jit(solution)/shard_map/ppermute | solution.py:492
  115.4 12.6 %copy-start.5 = (bf16[256,1024]{1,0:T(8,128)(2,1)S(1)}, bf16[256,1024]{1,0:T(8,128)(2,1)}, u32[]{:S(2)}) copy-start(bf16[256,1024]{1,0:T(8,128)(2,1)} %shard_map.126.refs_9_) | copy-start | bytes 1572868
  128.0 1.2 copy-start.4
  129.3 1.7 %collective-permute-start.27 = (f32[512,128]{1,0:T(8,128)S(1)}, f32[512,128]{1,0:T(8,128)S(1)}, u32[]{:S(2)}, u32[]{:S(2)}) collective-permute-start(f32[512,128]{1,0:T(8,128)S(1)} %get-tuple-element.73), channel_id=1, source_target_pairs={{1,0},{0,1},{3,2},{2,3},{5,4},{4,5},{7,6},{6,7},{9,8},{8,9},{11,10... | collective-permute-start | bytes 786440 | tf_op jit(solution)/shard_map/ppermute | solution.py:381

commit v5 on v0

v5 whole, which is shorter than its diff:
```python
import functools

import jax
import jax.numpy as jnp
from jax import lax
from jax.experimental import pallas as pl
from jax.experimental.pallas import tpu as pltpu
from jax.sharding import PartitionSpec as P

H = 8
HS = 128
BLK = 128
HD = 1024
QBD = 2
REACH = 2
MAXP = 8
WB = 4
SLOTS = QBD + WB - 1
UNUSED = 100
STATS_FLOPS = 20_000_000_000
WEIGHT_FLOPS = 1
VMEM_LIMIT = 16 * 1024 * 1024
SPAN = SLOTS * BLK
LOWEST = -1e29
MASKED = -1e30
SCALE = HS ** (-0.5)
SETS = ((0, 3), (1, 2))
ORDER = tuple(n for members in SETS for n in members)
KEPT = len(ORDER)
WIDE = KEPT * HS
HALO = WB - 1
WINDOW = (2 * QBD + HALO) * BLK
LINES = 2 * MAXP
VMEM = pl.BlockSpec(memory_space=pltpu.VMEM)
ANY = pl.BlockSpec(memory_space=pl.ANY)


def kernel_call(body, outs, operands, after=(), scratch=(), flops=1):
    count = len(operands)

    def run(*refs):
        body(*refs[:count], *refs[count + len(after) :])

    return pl.pallas_call(
        run,
        out_shape=tuple(outs),
        in_specs=[VMEM] * count + [ANY] * len(after),
        out_specs=tuple([VMEM] * len(outs)),
        scratch_shapes=list(scratch),
        compiler_params=pltpu.CompilerParams(vmem_limit_bytes=VMEM_LIMIT),
        cost_estimate=pl.CostEstimate(flops=flops, bytes_accessed=1, transcendentals=0),
    )(*operands, *after)


def copy_body(value, out):
    out[...] = value[...]


def held(value, *others):
    (copy,) = kernel_call(copy_body, [shape(value.shape, value.dtype)], (value,), after=others)
    return copy


def shape(dims, kind):
    return jax.ShapeDtypeStruct(dims, kind)


def shifted(value, axis, steps):
    count = lax.axis_size(axis)
    return lax.ppermute(
        value, axis, [(s, s + steps) for s in range(max(0, -steps), min(count, count - steps))]
    )


def rolled_pairs(count, far, flip):
    half = count // 2
    return [(((a + far) % half) * 2 + (b ^ flip), a * 2 + b) for a in range(half) for b in range(2)]


def nt(left, right):
    return lax.dot_general(left, right, (((1,), (1,)), ((), ())), preferred_element_type=jnp.float32)


def tn(left, right):
    return lax.dot_general(left, right, (((0,), (0,)), ((), ())), preferred_element_type=jnp.float32)


def nn(left, right):
    return jnp.dot(left, right, preferred_element_type=jnp.float32)


def rules_of(lines):
    lines = lines.astype(jnp.float32)
    queries, keys = lines[:MAXP], lines[MAXP:]
    found = {}
    for query in range(QBD):
        for back in range(WB):
            hit = jnp.where((queries == query) & (keys == query - back), 0.0, MASKED)
            found[query, back] = jnp.max(hit, axis=0, keepdims=True)
    return found


def fill_bias(sets, bias):
    rows = lax.broadcasted_iota(jnp.int32, (BLK, BLK), 0)
    columns = lax.broadcasted_iota(jnp.int32, (BLK, BLK), 1)
    for key in range(QBD):
        for slot in range(SLOTS):
            place = (pl.ds(key * BLK, BLK), pl.ds(slot * BLK, BLK))
            back = slot - key
            if not 0 <= back < WB:
                bias[place] = jnp.full((BLK, BLK), MASKED, jnp.float32)
                continue
            block = jnp.broadcast_to(sets[slot // QBD][slot % QBD, back], (BLK, BLK))
            if slot == key:
                block = jnp.where(rows <= columns, block, MASKED)
            bias[place] = block


def position(axis):
    index = lax.axis_index(axis)
    return index // 2, index % 2


def lanes(index):
    return pl.ds(pl.multiple_of(index * HS, HS), HS)


def split_body(*refs):
    first, second = refs[-4:-2]
    kept, sent = refs[-2:]
    parity = position("tm")[1]
    for side, array in enumerate((first, second)):
        for place, n in enumerate(ORDER):
            columns = slice((side * KEPT + place) * HS, (side * KEPT + place + 1) * HS)
            kept[:, columns] = array[:, lanes(2 * n + parity)]
            sent[: array.shape[0], columns] = array[:, lanes(2 * n + 1 - parity)]
    if len(refs) == 5:
        sent[array.shape[0] :, :] = jnp.zeros((LINES, sent.shape[1]), jnp.bfloat16)
        sent[array.shape[0] :, :BLK] = refs[0][...]


def pair_body(mine, heard, whole):
    tokens = mine.shape[0]
    for parity, parts in enumerate(((mine, heard), (heard, mine))):

        @pl.when(position("tm")[1] == parity)
        def _():
            for n, part in enumerate(parts):
                whole[n * tokens : (n + 1) * tokens, :] = part[:tokens, :]


def pair_lines_body(lines, mine, heard, whole, rules, halo):
    tokens = mine.shape[0]
    pair_body(mine, heard, whole)
    theirs = heard[tokens:, :BLK]
    for parity, parts in enumerate(((lines[...], theirs), (theirs, lines[...]))):

        @pl.when(position("tm")[1] == parity)
        def _():
            for n, part in enumerate(parts):
                rules[n * LINES : (n + 1) * LINES, :] = part

    halo[: HALO * BLK, :] = whole[: HALO * BLK, :]
    halo[HALO * BLK :, :] = jnp.zeros((2 * LINES, halo.shape[1]), jnp.bfloat16)
    halo[HALO * BLK :, :BLK] = rules[...]


def of_head(ref, place, start, count):
    return ref[start : start + count, place * HS : (place + 1) * HS]


def window_of(pair, halo, place, part):
    tokens = QBD * BLK
    rows = [of_head(pair, place, part * tokens, (2 - part) * tokens)]
    rows.append(of_head(halo, place, 0, SPAN - (2 - part) * tokens))
    return jnp.concatenate(rows, axis=0)


def keys_of(pair, place, part):
    return of_head(pair, place, part * QBD * BLK, QBD * BLK)


def thirds(ref, first, last):
    part = ref[:, first * BLK : last * BLK]
    large, mass, dot = (part[i * KEPT : (i + 1) * KEPT] for i in range(3))
    return jnp.where(mass > 0, large, LOWEST), mass, dot


def merged(one, other):
    large = jnp.maximum(one[0], other[0])
    factors = [jnp.exp(part[0] - large) for part in (one, other)]
    return large, *(one[i] * factors[0] + other[i] * factors[1] for i in (1, 2))


def in_row(*parts):
    return tuple(jnp.concatenate(pieces, axis=1) for pieces in zip(*parts))


def stats_body(query, key, rules, halo, own, up, down, bias, partial):
    tables = [rules_of(rules[n * LINES : (n + 1) * LINES, :]) for n in range(2)]
    later = halo[HALO * BLK :, :BLK]
    tables += [rules_of(later[n * LINES : (n + 1) * LINES, :]) for n in range(2)]
    for part in range(2):
        fill_bias(tables[part : part + 3], bias.at[part])
        for place in range(KEPT):
            scores = nt(keys_of(key, place, part), window_of(query, halo, place, part)) * SCALE + bias[part]
            products = nt(keys_of(key, KEPT + place, part), window_of(query, halo, KEPT + place, part))
            largest = jnp.maximum(jnp.max(scores, axis=0, keepdims=True), LOWEST)
            weights = jnp.exp(scores - largest)
            rows = (largest, jnp.sum(weights, axis=0, keepdims=True), jnp.sum(weights * products, axis=0, keepdims=True))
            for i, row in enumerate(rows):
                partial[part, i * KEPT + place : i * KEPT + place + 1, :] = row
    first, second = partial.at[0], partial.at[1]
    whole = in_row(
        thirds(first, 0, QBD),
        merged(thirds(first, QBD, SLOTS), thirds(second, 0, SLOTS - QBD)),
        thirds(second, SLOTS - QBD, SLOTS),
    )
    for i, piece in enumerate(whole):
        own[i * KEPT : (i + 1) * KEPT, :] = piece
    up[...] = own[:, 2 * QBD * BLK :]
    down[...] = own[:, : HALO * BLK]


def totals_of(own, up, down):
    middle = 2 * QBD
    large, mass, dot = in_row(
        merged(thirds(own, 0, HALO), thirds(up, 0, HALO)),
        thirds(own, HALO, middle),
        merged(thirds(own, middle, middle + HALO), thirds(down, 0, HALO)),
    )
    inverse = jnp.where(mass > 0, 1.0 / jnp.where(mass > 0, mass, 1.0), 0.0)
    return large, inverse, dot * inverse


def line_of(total, index, place, part):
    start = part * QBD * BLK
    return total[index * KEPT + place : index * KEPT + place + 1, start : start + SPAN]


def terms_of(query, key, halo, bias, total, place, part):
    rows = window_of(query, halo, place, part)
    cotangent = window_of(query, halo, KEPT + place, part)
    scores = nt(keys_of(key, place, part), rows) * SCALE + bias[part]
    probs = jnp.exp(scores - line_of(total, 0, place, part)) * line_of(total, 1, place, part)
    products = nt(keys_of(key, KEPT + place, part), cotangent)
    return rows, cotangent, probs, (probs * (products - line_of(total, 2, place, part))).astype(jnp.bfloat16)


def lows_body(query, key, halo, bias, own, up, down, mine, other, sent, total):
    for index, value in enumerate(totals_of(own, up, down)):
        total[index * KEPT : (index + 1) * KEPT] = value
    keeps_key = position("fsdp")[1] == 0
    for place in range(KEPT):
        for part in range(2):
            rows, cotangent, probs, grad_scores = terms_of(query, key, halo, bias, total, place, part)
            value_grads = nn(probs.astype(jnp.bfloat16), cotangent)
            key_grads = nn(grad_scores, rows) * SCALE
            where = (slice(part * QBD * BLK, (part + 1) * QBD * BLK), slice(place * HS, (place + 1) * HS))
            mine[where] = jnp.where(keeps_key, key_grads, value_grads).astype(jnp.bfloat16)
            other[where] = jnp.where(keeps_key, value_grads, key_grads).astype(jnp.bfloat16)
    tokens = sent.shape[0]
    theirs = pl.ds(pl.multiple_of((1 - position("tm")[1]) * tokens, tokens), tokens)
    sent[:, :WIDE] = mine[theirs, :]
    sent[:, WIDE:] = other[theirs, :]


def queries_body(query, key, halo, bias, total, own, up):
    middle = 2 * QBD * BLK
    for place in range(KEPT):
        columns = slice(place * HS, (place + 1) * HS)
        terms = []
        for part in range(2):
            grad_scores = terms_of(query, key, halo, bias, total, place, part)[3]
            terms.append(tn(grad_scores, keys_of(key, place, part)) * SCALE)
        shift = QBD * BLK
        own[:shift, columns] = terms[0][:shift]
        own[shift:, columns] = terms[0][shift:middle] + terms[1][: middle - shift]
        up[: SPAN - middle, columns] = (terms[0][middle:] + terms[1][middle - shift : SPAN - shift]).astype(jnp.bfloat16)
        up[SPAN - middle :, columns] = terms[1][SPAN - shift :].astype(jnp.bfloat16)


def queries_sum_body(own, heard, kept, sent):
    tokens = kept.shape[0]
    parity = position("tm")[1]
    start = HALO * BLK
    for part in range(2):
        for out, side in ((kept, parity), (sent, 1 - parity)):

            @pl.when(side == part)
            def _():
                first, last = part * tokens, min((part + 1) * tokens, start)
                count = last - first
                total = own[first:last, :] + heard[first:last, :].astype(jnp.float32)
                out[:count, :] = total.astype(jnp.bfloat16)
                if count < tokens:
                    out[count:, :] = own[last : first + tokens, :].astype(jnp.bfloat16)


def queries_place_body(kept, heard, out, token):
    parity = position("tm")[1]
    for place, n in enumerate(ORDER):
        out[:, lanes(2 * n + parity)] = head_of(kept, place)
        out[:, lanes(2 * n + 1 - parity)] = head_of(heard, place)
    token[...] = jnp.zeros_like(token)


def head_of(ref, place):
    return ref[:, place * HS : (place + 1) * HS]


def turned_back(value, away, count):
    return lax.rem(value + (count - away), count)


def looked_up(table):
    shard = lax.axis_index("tm")
    entry = jnp.int32(table[0])
    for index, value in enumerate(table):
        entry = jnp.where(shard == index, jnp.int32(value), entry)
    return entry


def cut_body(width, x, *outs):
    for away, out in enumerate(outs):
        place = turned_back(position("fsdp")[0], away, len(outs))
        first = pl.multiple_of(place * width, width)
        out[...] = x[:, pl.ds(first, width)].T


def beside_body(*refs):
    out, start = refs[-1], 0
    for ref in refs[:-1]:
        out[:, start : start + ref.shape[1]] = ref[...]
        start += ref.shape[1]


def join_body(mine, heard, *outs):
    count, start = mine.shape[0], 0
    for out in outs:
        width = out.shape[1]
        for n, source in enumerate((mine, heard)):
            out[n * count : (n + 1) * count, :] = source[:, start : start + width]
        start += width


def weight_sum(turned, lows, tokens):
    chips = len(lows)
    parity = position("tm")[1]
    total = None
    for flip in range(2):
        for side in range(2):
            shard = parity if side == 0 else 1 - parity
            for away in range(chips):
                rows = pl.ds(pl.multiple_of(flip * 2 * tokens + shard * tokens, tokens), tokens)
                left = turned[2 * flip + side][:, away * tokens : (away + 1) * tokens]
                term = nn(left, lows[away][rows, :])
                total = term if total is None else total + term
    return total


def weight_body(tables, tokens, *refs):
    turned, lows, outs, total = refs[:4], refs[4 : -len(tables) - 1], refs[-len(tables) - 1 : -1], refs[-1]
    total[...] = weight_sum(turned, lows, tokens)
    for out, table in zip(outs, tables):
        out[...] = total[:, lanes(looked_up(table))].astype(out.dtype)


def plain_weight_body(tokens, *refs):
    refs[-1][...] = weight_sum(refs[:4], refs[4:-1], tokens)


def rows_body(mine, other, heard, *refs):
    weights, (out, token) = refs[:-2], refs[-2:]
    token[...] = jnp.zeros_like(token)
    tokens, width = out.shape[0], weights[0].shape[0]
    chips = len(weights) // 4
    chip, core = position("fsdp")
    parity = position("tm")[1]
    rows = pl.ds(pl.multiple_of(parity * tokens, tokens), tokens)
    first = jnp.where(core == 0, 1.0, 0.0).astype(jnp.bfloat16)
    second = jnp.where(core == 0, 0.0, 1.0).astype(jnp.bfloat16)
    own = (mine[rows, :], other[rows, :])
    theirs = (heard[:, :WIDE], heard[:, WIDE:])
    lows = [
        [pair[0] * a + pair[1] * b for pair in (own, theirs)] for a, b in ((first, second), (second, first))
    ]
    for away in range(chips):
        for flip in range(2):
            total = None
            for kind in range(2):
                weight = weights[4 * away + 2 * kind + flip]
                for low, side in zip(lows[kind], (parity, 1 - parity)):
                    factor = jnp.concatenate([weight[:, lanes(2 * m + side)] for m in ORDER], axis=1)
                    term = nt(low, factor)
                    total = term if total is None else total + term
            owner = 2 * lax.rem(chip + away, chips) + (core if flip == 0 else 1 - core)
            out[:, pl.ds(pl.multiple_of(owner * width, width), width)] = total.astype(out.dtype)


def choose_body(first, second, kept, sent):
    for core, (a, b) in enumerate(((first, second), (second, first))):

        @pl.when(position("fsdp")[1] == core)
        def _():
            kept[...] = a[...]
            sent[...] = b[...]


def grouped(refs, sizes):
    groups, start = [], 0
    for size in sizes:
        groups.append(refs[start : start + size])
        start += size
    return groups


def final_body(belongs, sizes, *refs):
    mine, send = refs[-2:]
    height = mine.shape[0]
    core = position("fsdp")[1]
    for n, parts in enumerate(grouped(refs[:-2], sizes)):

        @pl.when(looked_up(belongs) == n)
        def _():
            for out, side in ((mine, core), (send, 1 - core)):
                rows = pl.ds(pl.multiple_of(side * height, height), height)
                total = None
                for part in parts:
                    term = part[rows, :].astype(jnp.float32)
                    total = term if total is None else total + term
                out[...] = total


def shards(
    inputs, query_rows, saved_key_rows, value_rows, grad_out, key_weight, value_weight, block_pairs, pair_counts
):
    tokens = query_rows.shape[1]
    n_tm, n_fsdp = lax.axis_size("tm"), lax.axis_size("fsdp")
    shard = lax.axis_index("tm")
    d_model = inputs.shape[2]
    rows = d_model // n_fsdp
    half, chips = n_tm // 2, n_fsdp // 2
    q, k, v, g = query_rows[0], saved_key_rows[0], value_rows[0], grad_out[0]
    bf16, f32 = jnp.bfloat16, jnp.float32
    token = shape((8, HS), f32)

    def exchanged(array):
        return lax.ppermute(array, "fsdp", rolled_pairs(n_fsdp, 0, 1))

    def swapped(array):
        return lax.ppermute(array, "tm", rolled_pairs(n_tm, 0, 1))

    def fetched(array, away):
        return lax.ppermute(array, "fsdp", rolled_pairs(n_fsdp, away, 0))

    key_weights = [key_weight, *(fetched(key_weight, away) for away in range(1, chips))]
    value_weights = [value_weight, *(fetched(value_weight, away) for away in range(1, chips))]
    key_parts, value_parts = ([(array, exchanged(array)) for array in arrays] for arrays in (key_weights, value_weights))
    cuts = kernel_call(
        functools.partial(cut_body, 2 * rows), [shape((2 * rows, tokens), bf16)] * chips, (inputs[0],)
    )
    cuts = [fetched(piece, away) if away else piece for away, piece in enumerate(cuts)]

    pairs = jnp.where(jnp.arange(MAXP)[:, None] < pair_counts[0], block_pairs[0] - shard * QBD, UNUSED)
    lines = jnp.broadcast_to(pairs.T.reshape(LINES, 1), (LINES, BLK)).astype(bf16)
    query_kept, query_sent = kernel_call(
        split_body, [shape((tokens, 2 * WIDE), bf16), shape((tokens + LINES, 2 * WIDE), bf16)], (lines, q, g)
    )
    query_heard = swapped(query_sent)
    key_kept, key_sent = kernel_call(
        split_body, [shape((tokens, 2 * WIDE), bf16)] * 2, (k, v), after=(query_heard, *key_weights[1:])
    )
    key_heard = swapped(key_sent)
    query, rules, halo_sent = kernel_call(
        pair_lines_body,
        [
            shape((2 * tokens, 2 * WIDE), bf16),
            shape((2 * LINES, BLK), bf16),
            shape((HALO * BLK + 2 * LINES, 2 * WIDE), bf16),
        ],
        (lines, query_kept, query_heard),
    )
    halo = shifted(halo_sent, "tm", -2)

    (turned,) = kernel_call(
        beside_body, [shape((2 * rows, chips * tokens), bf16)], cuts, after=(key_heard,)
    )
    turned_pair = swapped(turned)
    (key,) = kernel_call(pair_body, [shape((2 * tokens, 2 * WIDE), bf16)], (key_kept, key_heard))

    own, up, down, bias = kernel_call(
        stats_body,
        [shape((3 * KEPT, count), f32) for count in (WINDOW, HALO * BLK, HALO * BLK)]
        + [shape((2, tokens, SPAN), f32)],
        (query, key, rules, halo),
        scratch=[pltpu.VMEM((2, 3 * KEPT, SPAN), f32)],
        flops=STATS_FLOPS,
    )
    up, down = shifted(up, "tm", 2), shifted(down, "tm", -2)
    mine, other, sent, total = kernel_call(
        lows_body,
        [shape((2 * tokens, WIDE), bf16)] * 2 + [shape((tokens, 2 * WIDE), bf16), shape((3 * KEPT, WINDOW), f32)],
        (query, key, halo, bias, own, up, down),
        after=(*(parts[1] for parts in key_parts), value_parts[0][1]),
    )
    widths = [len(members) * HS for members in SETS]
    lows = kernel_call(
        join_body,
        [shape((4 * tokens, width), bf16) for width in widths],
        (mine, exchanged(other)),
        after=(turned_pair, *value_weights[1:]),
    )
    groups = [[low, *(fetched(low, away) for away in range(1, chips))] for low in lows]
    query_kept, query_sent = kernel_call(
        split_body, [shape((tokens, 2 * WIDE), bf16), shape((tokens + LINES, 2 * WIDE), bf16)], (lines, q, g)
    )
    query_heard = swapped(query_sent)
    key_kept, key_sent = kernel_call(
        split_body, [shape((tokens, 2 * WIDE), bf16)] * 2, (k, v), after=(query_heard, *key_weights[1:])
    )
    key_heard = swapped(key_sent)
    query, rules, halo_sent = kernel_call(
        pair_lines_body,
        [
            shape((2 * tokens, 2 * WIDE), bf16),
            shape((2 * LINES, BLK), bf16),
            shape((HALO * BLK + 2 * LINES, 2 * WIDE), bf16),
        ],
        (lines, query_kept, query_heard),
    )
    halo = shifted(halo_sent, "tm", -2)

    (turned,) = kernel_call(
        beside_body, [shape((2 * rows, chips * tokens), bf16)], cuts, after=(key_heard,)
    )
    turned_pair = swapped(turned)
    (key,) = kernel_call(pair_body, [shape((2 * tokens, 2 * WIDE), bf16)], (key_kept, key_heard))

    own, up, down, bias = kernel_call(
        stats_body,
        [shape((3 * KEPT, count), f32) for count in (WINDOW, HALO * BLK, HALO * BLK)]
        + [shape((2, tokens, SPAN), f32)],
        (query, key, rules, halo),
        scratch=[pltpu.VMEM((2, 3 * KEPT, SPAN), f32)],
        flops=STATS_FLOPS,
    )
    up, down = shifted(up, "tm", 2), shifted(down, "tm", -2)
    mine, other, sent, total = kernel_call(
        lows_body,
        [shape((2 * tokens, WIDE), bf16)] * 2 + [shape((tokens, 2 * WIDE), bf16), shape((3 * KEPT, WINDOW), f32)],
        (query, key, halo, bias, own, up, down),
        after=(*(parts[1] for parts in key_parts), value_parts[0][1]),
    )
    widths = [len(members) * HS for members in SETS]
    lows = kernel_call(
        join_body,
        [shape((4 * tokens, width), bf16) for width in widths],
        (mine, exchanged(other)),
        after=(turned_pair, *value_weights[1:]),
    )
    groups = [[low, *(fetched(low, away) for away in range(1, chips))] for low in lows]
    query_own, query_up = kernel_call(
        queries_body,
        [shape((2 * tokens, WIDE), f32), shape((HALO * BLK, WIDE), bf16)],
        (query, key, halo, bias, total),
        after=lows,
    )
    query_kept, query_sent = kernel_call(
        queries_sum_body, [shape((tokens, WIDE), bf16)] * 2, (query_own, shifted(query_up, "tm", 2))
    )
    grad_query, query_token = kernel_call(
        queries_place_body, [shape((tokens, HD), bf16), token], (query_kept, swapped(query_sent))
    )

    result, result_token = kernel_call(
        rows_body,
        [shape((tokens, d_model), bf16), token],
        (
            mine,
            other,
            swapped(sent),
            *(part for pair in zip(key_parts, value_parts) for parts in pair for part in parts),
        ),
    )

    aligned = HD // n_tm == HS
    sides = (turned, turned_pair, exchanged(turned), exchanged(held(turned_pair, *lows)))
    sums, partials = [], []
    for index, (members, group, width) in enumerate(zip(SETS, groups, widths)):
        if not aligned:
            partials += kernel_call(
                functools.partial(plain_weight_body, tokens), [shape((2 * rows, width), f32)], (*sides, *group)
            )
            continue
        tables = []
        for away in range(half):
            tables.append([0] * n_tm)
            for y in range(2):
                for n, z in enumerate(members):
                    tables[-1][((z + away) % half) * 2 + y] = n
        chunks = kernel_call(
            functools.partial(weight_body, tables, tokens),
            [shape((2 * rows, HS), f32 if away == 0 else bf16) for away in range(half)],
            (*sides, *group),
            after=(partials[0], result_token) if index else (query_up,),
            scratch=[pltpu.VMEM((2 * rows, width), f32)],
            flops=1 if index else WEIGHT_FLOPS,
        )
        parcels = [chunks[0]]
        for away in range(1, half):
            routes = [(((z + away) % half) * 2 + y, z * 2 + y) for y in range(2) for z in members]
            parcels.append(lax.ppermute(chunks[away], "tm", routes))
        partials.append(chunks[0])
        sums.append(parcels)

    if aligned:
        belongs = [[j // 2 in members for members in SETS].index(True) for j in range(n_tm)]
        ours, theirs = kernel_call(
            functools.partial(final_body, belongs, [len(parcels) for parcels in sums]),
            [shape((rows, HS), f32)] * 2,
            [parcel for parcels in sums for parcel in parcels],
        )
    else:
        partial = jnp.concatenate(partials, axis=1)
        heads = [partial[:, ORDER.index(n) * HS : (ORDER.index(n) + 1) * HS] for n in range(KEPT)]
        parity, core = shard % 2, lax.axis_index("fsdp") % 2
        spread = [jnp.where(parity == y, heads[n], 0.0) for n in range(KEPT) for y in range(2)]
        whole = lax.psum_scatter(jnp.concatenate(spread, axis=1), "tm", scatter_dimension=1, tiled=True)
        ours, theirs = (lax.dynamic_slice_in_dim(whole, side * rows, rows, 0) for side in (core, 1 - core))
    key_total, value_total = kernel_call(
        choose_body, [shape(ours.shape, f32)] * 2, (ours, exchanged(theirs))
    )
    return (grad_query[None], result[None], key_total, value_total)


def solution(mesh):
    return jax.shard_map(
        shards,
        mesh=mesh,
        in_specs=(
            P("fsdp", "tm", None),
            P("fsdp", "tm", None),
            P("fsdp", "tm", None),
            P("fsdp", "tm", None),
            P("fsdp", "tm", None),
            P("fsdp", None),
            P("fsdp", None),
            P("tm", None, None),
            P("tm"),
        ),
        out_specs=(P("fsdp", "tm", None), P("fsdp", "tm", None), P("fsdp", "tm"), P("fsdp", "tm")),
        check_vma=False,
    )
```

time: 585 us -> 124 us (0.21)
  waiting for transfers between devices: 426 us -> 54.9 us
  matrix products: 83.3 us -> 0 us
  local copies, waits for them, and re-layouts: 30.3 us -> 2.26 us
  starting transfers between devices: 21.7 us -> 43.8 us
  Pallas kernels: 0 us -> 20.1 us
  between operations: 14.6 us -> 1.59 us
  other arithmetic: 6.82 us -> 0.69 us
    reduce_scatter x3 -> x0, waiting for transfers between devices: 280 us -> none  [the longest x1 145 us: shards(): lax.psum_scatter(jnp.einsum('tr,tc->rc', input_slab, paired_lower_rows, p...]
    dot_general x51 -> x0, matrix products: 83.3 us -> none  [the longest x8 16.7 us: head_terms(): jnp.einsum('qk,qd->kd', weights_low, cotangent_head, preferred_element_ty...]
    all_gather x2 -> x0, waiting for transfers between devices: 60.4 us -> none  [shards(): lax.all_gather((key_weight, value_weight), 'fsdp', axis=0, tiled=True)]
    ppermute x8 -> x28, waiting for transfers between devices: 83.8 us -> 54.9 us  [the longest x5 29.2 us: swapped(): return lax.ppermute(array, 'tm', rolled_pairs(n_tm, 0, 1))]
    ppermute x8 -> x28, starting transfers between devices: 21.3 us -> 43.8 us  [the longest x6 17.3 us: shards(): parcels.append(lax.ppermute(chunks[away], 'tm', routes))]
    pallas_call x0 -> x18, Pallas kernels: none -> 20.1 us  [kernel_call(): pl.pallas_call(run, out_shape=tuple(outs), in_specs=[VMEM] * count + [ANY...]
    unnamed x18 -> x14, local copies, waits for them, and re-layouts: 10.5 us -> 2.1 us
    dynamic_update_slice x16 -> x0, local copies, waits for them, and re-layouts: 7.61 us -> none  [shards(): lax.map(per_head, (split_heads(query_rows[0]), split_heads(window_keys),...]
  transfers between devices with their start and end apart: 13 -> 28, of which waited for: 10 -> 12; matrix products, arithmetic and copies ran while one was open for 4% -> 1% of each run, Pallas kernels for 0% -> 16%
where the time goes in v5:
time: 124 us; the launch traced here: 123 us
  waiting for transfers between devices  54.9 us (44%)
  starting transfers between devices  43.8 us (35%)
  Pallas kernels  20.1 us (16%)
  local copies, waits for them, and re-layouts  2.26 us (2%)
  between operations  1.59 us (1%)
    ppermute x5, waiting for transfers between devices, swapped(): return lax.ppermute(array, 'tm', rolled_pairs(n_tm, 0, 1))  29.2 us
    pallas_call x18, Pallas kernels, kernel_call(): pl.pallas_call(run, out_shape=tuple(outs), in_specs=[VMEM] * count + [ANY...  20.1 us
    ppermute x6, starting transfers between devices, shards(): parcels.append(lax.ppermute(chunks[away], 'tm', routes))  17.3 us
    ppermute x5, waiting for transfers between devices, fetched(): return lax.ppermute(array, 'fsdp', rolled_pairs(n_fsdp, away, 0))  16.1 us
    ppermute x4, starting transfers between devices, shifted(): lax.ppermute(value, axis, [(s, s + steps) for s in range(max(0, -steps),...  10.3 us
    ppermute x5, starting transfers between devices, fetched(): return lax.ppermute(array, 'fsdp', rolled_pairs(n_fsdp, away, 0))  8.7 us
    ppermute x5, starting transfers between devices, swapped(): return lax.ppermute(array, 'tm', rolled_pairs(n_tm, 0, 1))  5.81 us
    ppermute x4, waiting for transfers between devices, shifted(): lax.ppermute(value, axis, [(s, s + steps) for s in range(max(0, -steps),...  4.89 us
  transfers between devices with their start and end apart: 28, of which 12 were waited for; matrix products, arithmetic and copies ran while one was open for 1% of the time, Pallas kernels for 16%

profile of v5, /device:TPU:0, one launch (start us, length us, event | category | flops | bytes accessed | tf_op | source)
XLA Modules:
  0.0 123.4 jit_solution(729517874636155348)
XLA Ops:
  0.6 3.0 %collective-permute-start.1 = (bf16[512,1024]{1,0:T(8,128)(2,1)}, bf16[512,1024]{1,0:T(8,128)(2,1)S(1)}, u32[]{:S(2)}, u32[]{:S(2)}) collective-permute-start(bf16[512,1024]{1,0:T(8,128)(2,1)} %refs_3_.1), channel_id=1, source_target_pairs={{2,0},{3,1},{0,2},{1,3},{6,4},{7,5},{4,6},{5,7},{10,8},{11,9},{8,1... | collective-permute-start | bytes 3145736 | tf_op jit(solution)/shard_map/ppermute | solution.py:455
  4.3 0.7 fusion.1
  5.0 0.1 convert_element_type.9
  5.1 0.1 broadcast_in_dim.26.refs_0_
  5.2 1.0 copy-done.3
  6.2 1.0 copy-done.4
  7.2 0.3 shard_map.120
  7.5 1.6 %collective-permute-start = (bf16[272,1024]{1,0:T(8,128)(2,1)S(1)}, bf16[272,1024]{1,0:T(8,128)(2,1)S(1)}, u32[]{:S(2)}, u32[]{:S(2)}) collective-permute-start(bf16[272,1024]{1,0:T(8,128)(2,1)S(1)} %get-tuple-element.43), channel_id=1, source_target_pairs={{4,0},{0,4},{12,8},{8,12},{20,16},{16,20},{28,24},{24,28},{5,1},{1... | collective-permute-start | bytes 1671176 | tf_op jit(solution)/shard_map/ppermute | solution.py:452
  9.1 12.6 %collective-permute-done.refs_2_ = bf16[272,1024]{1,0:T(8,128)(2,1)S(1)} collective-permute-done((bf16[272,1024]{1,0:T(8,128)(2,1)S(1)}, bf16[272,1024]{1,0:T(8,128)(2,1)S(1)}, u32[]{:S(2)}, u32[]{:S(2)}) %collective-permute-start) | collective-permute-done | bytes 557088 | tf_op jit(solution)/shard_map/ppermute | solution.py:452
  21.7 0.1 shard_map.121
  21.8 1.4 %collective-permute-start.3 = (bf16[416,1024]{1,0:T(8,128)(2,1)S(1)}, bf16[416,1024]{1,0:T(8,128)(2,1)S(1)}, u32[]{:S(2)}, u32[]{:S(2)}) collective-permute-start(bf16[416,1024]{1,0:T(8,128)(2,1)S(1)} %get-tuple-element.47), channel_id=1, source_target_pairs={{8,0},{12,4},{16,8},{20,12},{24,16},{28,20},{9,1},{13,5},{17,9},{2... | collective-permute-start | bytes 2555912 | tf_op jit(solution)/shard_map/ppermute | solution.py:70
  23.2 3.8 %collective-permute-done.1.refs_3_.refs_7_ = bf16[512,1024]{1,0:T(8,128)(2,1)S(1)} collective-permute-done((bf16[512,1024]{1,0:T(8,128)(2,1)}, bf16[512,1024]{1,0:T(8,128)(2,1)S(1)}, u32[]{:S(2)}, u32[]{:S(2)}) %collective-permute-start.1) | collective-permute-done | bytes 1048608 | tf_op jit(solution)/shard_map/ppermute | solution.py:455
  27.0 0.3 shard_map.122
  27.3 1.8 %collective-permute-start.2 = (bf16[256,1024]{1,0:T(8,128)(2,1)S(1)}, bf16[256,1024]{1,0:T(8,128)(2,1)S(1)}, u32[]{:S(2)}, u32[]{:S(2)}) collective-permute-start(bf16[256,1024]{1,0:T(8,128)(2,1)S(1)} %get-tuple-element.46), channel_id=1, source_target_pairs={{4,0},{0,4},{12,8},{8,12},{20,16},{16,20},{28,24},{24,28},{5,1},{1... | collective-permute-start | bytes 1572872 | tf_op jit(solution)/shard_map/ppermute | solution.py:452
  29.2 0.3 shard_map.126
  29.5 1.6 %collective-permute-start.10 = (bf16[1024,256]{1,0:T(8,128)(2,1)S(1)}, bf16[1024,256]{1,0:T(8,128)(2,1)S(1)}, u32[]{:S(2)}, u32[]{:S(2)}) collective-permute-start(bf16[1024,256]{1,0:T(8,128)(2,1)S(1)} %get-tuple-element.57), channel_id=1, source_target_pairs={{2,0},{3,1},{0,2},{1,3},{6,4},{7,5},{4,6},{5,7},{10,8},{11,9},{8,1... | collective-permute-start | bytes 1572872 | tf_op jit(solution)/shard_map/ppermute | solution.py:455
  31.0 0.5 collective-permute-start.8
  31.6 8.9 %collective-permute-done.2.refs_1_.refs_2_ = bf16[256,1024]{1,0:T(8,128)(2,1)S(1)} collective-permute-done((bf16[256,1024]{1,0:T(8,128)(2,1)S(1)}, bf16[256,1024]{1,0:T(8,128)(2,1)S(1)}, u32[]{:S(2)}, u32[]{:S(2)}) %collective-permute-start.2) | collective-permute-done | bytes 524320 | tf_op jit(solution)/shard_map/ppermute | solution.py:452
  40.5 1.4 %collective-permute-start.12 = (bf16[512,1024]{1,0:T(8,128)(2,1)S(1)}, bf16[512,1024]{1,0:T(8,128)(2,1)S(1)}, u32[]{:S(2)}, u32[]{:S(2)}) collective-permute-start(bf16[512,1024]{1,0:T(8,128)(2,1)S(1)} %copy-done.1), channel_id=1, source_target_pairs={{2,0},{3,1},{0,2},{1,3},{6,4},{7,5},{4,6},{5,7},{10,8},{11,9},{8,1... | collective-permute-start | bytes 3145736 | tf_op jit(solution)/shard_map/ppermute | solution.py:455
  41.9 0.1 shard_map.123.refs_1_
  42.0 0.6 collective-permute-done.10.refs_1_
  42.6 0.1 shard_map.127.refs_0_
  42.7 0.6 collective-permute-done.3.refs_3_.refs_2_
  43.3 1.5 %collective-permute-start.11 = (bf16[1024,512]{1,0:T(8,128)(2,1)S(1)}, bf16[1024,512]{1,0:T(8,128)(2,1)S(1)}, u32[]{:S(2)}, u32[]{:S(2)}) collective-permute-start(bf16[1024,512]{1,0:T(8,128)(2,1)S(1)} %shard_map.127.refs_0_), channel_id=1, source_target_pairs={{4,0},{0,4},{12,8},{8,12},{20,16},{16,20},{28,24},{24,28},{5,1},{1... | collective-permute-start | bytes 3145736 | tf_op jit(solution)/shard_map/ppermute | solution.py:452
  44.8 2.5 %shard_map.124 = (f32[12,896]{1,0:T(8,128)S(1)}, f32[12,384]{1,0:T(8,128)S(1)}, f32[12,384]{1,0:T(8,128)S(1)}, f32[2,256,640]{2,1,0:T(8,128)S(1)}) custom-call(bf16[512,1024]{1,0:T(8,128)(2,1)S(1)} %get-tuple-element.44.refs_0_, bf16[512,1024]{1,0:T(8,128)(2,1)S(1)} %shard_map.123.refs_1_, bf16[32,128]{1,0:T(8,128)(2,1)S(1)} %get-tuple-element.48.refs_2_, ...), custom_call_target="tpu_custom_call" | custom-call | flops 20000000000 | bytes 1 | tf_op jit(solution)/shard_map/pallas_call | solution.py:44
  47.3 0.0 collective-permute-done.6.refs_7_.refs_4_
  47.3 3.5 %collective-permute-start.4 = (f32[12,384]{1,0:T(8,128)S(1)}, f32[12,384]{1,0:T(8,128)S(1)}, u32[]{:S(2)}, u32[]{:S(2)}) collective-permute-start(f32[12,384]{1,0:T(8,128)S(1)} %get-tuple-element.51), channel_id=1, source_target_pairs={{0,8},{4,12},{8,16},{12,20},{16,24},{20,28},{1,9},{5,13},{9,17},{1... | collective-permute-start | bytes 55304 | tf_op jit(solution)/shard_map/ppermute | solution.py:70
  50.8 1.5 %collective-permute-start.5 = (f32[12,384]{1,0:T(8,128)S(1)}, f32[12,384]{1,0:T(8,128)S(1)}, u32[]{:S(2)}, u32[]{:S(2)}) collective-permute-start(f32[12,384]{1,0:T(8,128)S(1)} %get-tuple-element.52), channel_id=1, source_target_pairs={{8,0},{12,4},{16,8},{20,12},{24,16},{28,20},{9,1},{13,5},{17,9},{2... | collective-permute-start | bytes 55304 | tf_op jit(solution)/shard_map/ppermute | solution.py:70
  52.3 0.0 collective-permute-done.4.refs_5_
  52.3 4.2 %collective-permute-done.5.refs_6_ = f32[12,384]{1,0:T(8,128)S(1)} collective-permute-done((f32[12,384]{1,0:T(8,128)S(1)}, f32[12,384]{1,0:T(8,128)S(1)}, u32[]{:S(2)}, u32[]{:S(2)}) %collective-permute-start.5) | collective-permute-done | bytes 18464 | tf_op jit(solution)/shard_map/ppermute | solution.py:70
  56.5 3.8 %shard_map.125 = (bf16[512,512]{1,0:T(8,128)(2,1)S(1)}, bf16[512,512]{1,0:T(8,128)(2,1)S(1)}, bf16[256,1024]{1,0:T(8,128)(2,1)S(1)}, f32[12,896]{1,0:T(8,128)S(1)}) custom-call(bf16[512,1024]{1,0:T(8,128)(2,1)S(1)} %get-tuple-element.44.refs_0_, bf16[512,1024]{1,0:T(8,128)(2,1)S(1)} %shard_map.123.refs_1_, ...), custom_call_target="tpu_custom_call" | custom-call | flops 1 | bytes 1 | tf_op jit(solution)/shard_map/pallas_call | solution.py:44
  60.3 0.1 collective-permute-start.9
  60.4 0.5 collective-permute-start.17
  60.9 3.6 %collective-permute-done.12.refs_3_.refs_9_ = bf16[512,1024]{1,0:T(8,128)(2,1)S(1)} collective-permute-done((bf16[512,1024]{1,0:T(8,128)(2,1)S(1)}, bf16[512,1024]{1,0:T(8,128)(2,1)S(1)}, u32[]{:S(2)}, u32[]{:S(2)}) %collective-permute-start.12) | collective-permute-done | bytes 1048608 | tf_op jit(solution)/shard_map/ppermute | solution.py:455
  64.5 0.0 collective-permute-done.9.refs_1_
  64.5 3.8 %collective-permute-done.11.refs_2_.refs_0_.refs_1_ = bf16[1024,512]{1,0:T(8,128)(2,1)S(1)} collective-permute-done((bf16[1024,512]{1,0:T(8,128)(2,1)S(1)}, bf16[1024,512]{1,0:T(8,128)(2,1)S(1)}, u32[]{:S(2)}, u32[]{:S(2)}) %collective-permute-start.11) | collective-permute-done | bytes 1048608 | tf_op jit(solution)/shard_map/ppermute | solution.py:452
  68.3 0.1 shard_map.128
  68.4 0.1 shard_map.133
  68.5 0.1 collective-permute-start.18
  68.6 0.5 collective-permute-start.16
  69.1 1.9 %collective-permute-start.19 = (bf16[1024,256]{1,0:T(8,128)(2,1)S(1)}, bf16[1024,256]{1,0:T(8,128)(2,1)S(1)}, u32[]{:S(2)}, u32[]{:S(2)}) collective-permute-start(bf16[1024,256]{1,0:T(8,128)(2,1)S(1)} %get-tuple-element.58.refs_5_.refs_1_.refs_4_), channel_id=1, source_target_pairs={{2,0},{3,1},{0,2},{1,3},{6,4},{7,5},{4,6},{5,7},{10,8},{11,9},{8,1... | collective-permute-start | bytes 1572872 | tf_op jit(solution)/shard_map/ppermute | solution.py:455
  70.9 0.3 collective-permute-start.15
  71.2 0.8 collective-permute-start.23
  72.1 3.7 %shard_map.129 = (f32[512,512]{1,0:T(8,128)S(1)}, bf16[384,512]{1,0:T(8,128)(2,1)S(1)}) custom-call(bf16[512,1024]{1,0:T(8,128)(2,1)S(1)} %get-tuple-element.44.refs_0_, bf16[512,1024]{1,0:T(8,128)(2,1)S(1)} %shard_map.123.refs_1_, bf16[416,1024]{1,0:T(8,128)(2,1)S(1)} %collective-permute-done.3.refs_3_.refs_2_, ...), custom_call_target="tpu_custom_call" | custom-call | flops 1 | bytes 1 | tf_op jit(solution)/shard_map/pallas_call | solution.py:44
  75.8 8.1 %collective-permute-done.19.refs_5_ = bf16[1024,256]{1,0:T(8,128)(2,1)S(1)} collective-permute-done((bf16[1024,256]{1,0:T(8,128)(2,1)S(1)}, bf16[1024,256]{1,0:T(8,128)(2,1)S(1)}, u32[]{:S(2)}, u32[]{:S(2)}) %collective-permute-start.19) | collective-permute-done | bytes 524320 | tf_op jit(solution)/shard_map/ppermute | solution.py:455
  83.8 3.9 %collective-permute-start.13 = (bf16[384,512]{1,0:T(8,128)(2,1)S(1)}, bf16[384,512]{1,0:T(8,128)(2,1)S(1)}, u32[]{:S(2)}, u32[]{:S(2)}) collective-permute-start(bf16[384,512]{1,0:T(8,128)(2,1)S(1)} %get-tuple-element.61.refs_6_), channel_id=1, source_target_pairs={{0,8},{4,12},{8,16},{12,20},{16,24},{20,28},{1,9},{5,13},{9,17},{1... | collective-permute-start | bytes 1179656 | tf_op jit(solution)/shard_map/ppermute | solution.py:70
  87.7 1.7 %shard_map.134 = (f32[1024,128]{1,0:T(8,128)S(1)}, bf16[1024,128]{1,0:T(8,128)(2,1)S(1)}, bf16[1024,128]{1,0:T(8,128)(2,1)S(1)}, bf16[1024,128]{1,0:T(8,128)(2,1)S(1)}) custom-call(bf16[1024,512]{1,0:T(8,128)(2,1)S(1)} %shard_map.127.refs_0_, bf16[1024,512]{1,0:T(8,128)(2,1)S(1)} %collective-permute-done.11.refs_2_.refs_0_.refs_1_, ...), custom_call_target="tpu_custom_call" | custom-call | flops 1 | bytes 1 | tf_op jit(solution)/shard_map/pallas_call | solution.py:44
  89.4 3.3 %collective-permute-start.20 = (bf16[1024,128]{1,0:T(8,128)(2,1)S(1)}, bf16[1024,128]{1,0:T(8,128)(2,1)S(1)}, u32[]{:S(2)}, u32[]{:S(2)}) collective-permute-start(bf16[1024,128]{1,0:T(8,128)(2,1)S(1)} %get-tuple-element.68), channel_id=1, source_target_pairs={{8,0},{0,24},{12,4},{4,28},{9,1},{1,25},{13,5},{5,29},{10,2},{2,26... | collective-permute-start | bytes 786440 | tf_op jit(solution)/shard_map/ppermute | solution.py:613
  92.7 3.6 %shard_map.132 = (bf16[256,2048]{1,0:T(8,128)(2,1)}, f32[8,128]{1,0:T(8,128)S(1)}) custom-call(bf16[512,512]{1,0:T(8,128)(2,1)S(1)} %get-tuple-element.54.refs_0_, bf16[512,512]{1,0:T(8,128)(2,1)S(1)} %get-tuple-element.55.refs_1_, bf16[256,1024]{1,0:T(8,128)(2,1)S(1)} %collective-permute-done.15.refs_2_, bf16[512,1024]{1,0:T(8,128)(2,1)S(1)} %copy-done, ...), custom_call_target="tpu_custom_call" | custom-call | flops 1 | bytes 1 | tf_op jit(solution)/shard_map/pallas_call | solution.py:44
  96.4 1.3 %collective-permute-start.21 = (bf16[1024,128]{1,0:T(8,128)(2,1)S(1)}, bf16[1024,128]{1,0:T(8,128)(2,1)S(1)}, u32[]{:S(2)}, u32[]{:S(2)}) collective-permute-start(bf16[1024,128]{1,0:T(8,128)(2,1)S(1)} %get-tuple-element.69), channel_id=1, source_target_pairs={{16,0},{8,24},{20,4},{12,28},{17,1},{9,25},{21,5},{13,29},{18,2},{... | collective-permute-start | bytes 786440 | tf_op jit(solution)/shard_map/ppermute | solution.py:613
  97.6 1.3 %collective-permute-start.22 = (bf16[1024,128]{1,0:T(8,128)(2,1)S(1)}, bf16[1024,128]{1,0:T(8,128)(2,1)S(1)}, u32[]{:S(2)}, u32[]{:S(2)}) collective-permute-start(bf16[1024,128]{1,0:T(8,128)(2,1)S(1)} %get-tuple-element.70), channel_id=1, source_target_pairs={{24,0},{16,24},{28,4},{20,28},{25,1},{17,25},{29,5},{21,29},{26,2}... | collective-permute-start | bytes 786440 | tf_op jit(solution)/shard_map/ppermute | solution.py:613
  99.0 1.6 %shard_map.135 = (f32[1024,128]{1,0:T(8,128)S(1)}, bf16[1024,128]{1,0:T(8,128)(2,1)S(1)}, bf16[1024,128]{1,0:T(8,128)(2,1)S(1)}, bf16[1024,128]{1,0:T(8,128)(2,1)S(1)}) custom-call(bf16[1024,512]{1,0:T(8,128)(2,1)S(1)} %shard_map.127.refs_0_, bf16[1024,512]{1,0:T(8,128)(2,1)S(1)} %collective-permute-done.11.refs_2_.refs_0_.refs_1_, ...), custom_call_target="tpu_custom_call" | custom-call | flops 1 | bytes 1 | tf_op jit(solution)/shard_map/pallas_call | solution.py:44
  100.6 0.7 collective-permute-start.24
  101.3 9.4 %collective-permute-start.25 = (bf16[1024,128]{1,0:T(8,128)(2,1)S(1)}, bf16[1024,128]{1,0:T(8,128)(2,1)S(1)}, u32[]{:S(2)}, u32[]{:S(2)}) collective-permute-start(bf16[1024,128]{1,0:T(8,128)(2,1)S(1)} %get-tuple-element.74), channel_id=1, source_target_pairs={{24,8},{0,16},{28,12},{4,20},{25,9},{1,17},{29,13},{5,21},{26,10},... | collective-permute-start | bytes 786440 | tf_op jit(solution)/shard_map/ppermute | solution.py:613
  110.7 1.3 %collective-permute-start.26 = (bf16[1024,128]{1,0:T(8,128)(2,1)S(1)}, bf16[1024,128]{1,0:T(8,128)(2,1)S(1)}, u32[]{:S(2)}, u32[]{:S(2)}) collective-permute-start(bf16[1024,128]{1,0:T(8,128)(2,1)S(1)} %get-tuple-element.75), channel_id=1, source_target_pairs={{0,8},{8,16},{4,12},{12,20},{1,9},{9,17},{5,13},{13,21},{2,10},{10... | collective-permute-start | bytes 786440 | tf_op jit(solution)/shard_map/ppermute | solution.py:613
  112.1 0.1 shard_map.130
  112.2 3.0 %collective-permute-done.21.refs_2_ = bf16[1024,128]{1,0:T(8,128)(2,1)S(1)} collective-permute-done((bf16[1024,128]{1,0:T(8,128)(2,1)S(1)}, bf16[1024,128]{1,0:T(8,128)(2,1)S(1)}, u32[]{:S(2)}, u32[]{:S(2)}) %collective-permute-start.21) | collective-permute-done | bytes 262176 | tf_op jit(solution)/shard_map/ppermute | solution.py:613
  115.2 0.6 collective-permute-start.14
  115.8 1.6 %collective-permute-done.26.refs_7_ = bf16[1024,128]{1,0:T(8,128)(2,1)S(1)} collective-permute-done((bf16[1024,128]{1,0:T(8,128)(2,1)S(1)}, bf16[1024,128]{1,0:T(8,128)(2,1)S(1)}, u32[]{:S(2)}, u32[]{:S(2)}) %collective-permute-start.26) | collective-permute-done | bytes 262176 | tf_op jit(solution)/shard_map/ppermute | solution.py:613
  117.4 0.1 shard_map.136
  117.6 0.1 collective-permute-start.27
  117.6 3.9 %collective-permute-done.14.refs_1_ = bf16[256,512]{1,0:T(8,128)(2,1)S(1)} collective-permute-done((bf16[256,512]{1,0:T(8,128)(2,1)S(1)}, bf16[256,512]{1,0:T(8,128)(2,1)S(1)}, u32[]{:S(2)}, u32[]{:S(2)}) %collective-permute-start.14) | collective-permute-done | bytes 262176 | tf_op jit(solution)/shard_map/ppermute | solution.py:452
  121.6 1.0 shard_map.131
  122.5 0.8 shard_map.137
  (28 shorter events, 0.1 us)
Async XLA Ops:
  0.6 26.4 %collective-permute-start.1 = (bf16[512,1024]{1,0:T(8,128)(2,1)}, bf16[512,1024]{1,0:T(8,128)(2,1)S(1)}, u32[]{:S(2)}, u32[]{:S(2)}) collective-permute-start(bf16[512,1024]{1,0:T(8,128)(2,1)} %refs_3_.1), channel_id=1, source_target_pairs={{2,0},{3,1},{0,2},{1,3},{6,4},{7,5},{4,6},{5,7},{10,8},{11,9},{8,1... | collective-permute-start | bytes 3145736 | tf_op jit(solution)/shard_map/ppermute | solution.py:455
  5.2 1.0 copy-start.3
  6.2 1.0 copy-start.4
  7.2 19.8 %copy-start.5 = (bf16[1,256,1024]{2,1,0:T(8,128)(2,1)S(1)}, bf16[1,256,1024]{2,1,0:T(8,128)(2,1)}, u32[]{:S(2)}) copy-start(bf16[1,256,1024]{2,1,0:T(8,128)(2,1)} %param.11) | copy-start | bytes 1572868
  7.2 19.8 %copy-start.6 = (bf16[1,256,1024]{2,1,0:T(8,128)(2,1)S(1)}, bf16[1,256,1024]{2,1,0:T(8,128)(2,1)}, u32[]{:S(2)}) copy-start(bf16[1,256,1024]{2,1,0:T(8,128)(2,1)} %param.12) | copy-start | bytes 1572868
  7.5 14.2 %collective-permute-start = (bf16[272,1024]{1,0:T(8,128)(2,1)S(1)}, bf16[272,1024]{1,0:T(8,128)(2,1)S(1)}, u32[]{:S(2)}, u32[]{:S(2)}) collective-permute-start(bf16[272,1024]{1,0:T(8,128)(2,1)S(1)} %get-tuple-element.43), channel_id=1, source_target_pairs={{4,0},{0,4},{12,8},{8,12},{20,16},{16,20},{28,24},{24,28},{5,1},{1... | collective-permute-start | bytes 1671176 | tf_op jit(solution)/shard_map/ppermute | solution.py:452
  21.7 7.5 %copy-start.2 = (bf16[1,256,2048]{2,1,0:T(8,128)(2,1)S(1)}, bf16[1,256,2048]{2,1,0:T(8,128)(2,1)}, u32[]{:S(2)}) copy-start(bf16[1,256,2048]{2,1,0:T(8,128)(2,1)} %param.9) | copy-start | bytes 3145732
  21.8 21.5 %collective-permute-start.3 = (bf16[416,1024]{1,0:T(8,128)(2,1)S(1)}, bf16[416,1024]{1,0:T(8,128)(2,1)S(1)}, u32[]{:S(2)}, u32[]{:S(2)}) collective-permute-start(bf16[416,1024]{1,0:T(8,128)(2,1)S(1)} %get-tuple-element.47), channel_id=1, source_target_pairs={{8,0},{12,4},{16,8},{20,12},{24,16},{28,20},{9,1},{13,5},{17,9},{2... | collective-permute-start | bytes 2555912 | tf_op jit(solution)/shard_map/ppermute | solution.py:70
  27.0 4.0 %copy-start = (bf16[512,1024]{1,0:T(8,128)(2,1)S(1)}, bf16[512,1024]{1,0:T(8,128)(2,1)}, u32[]{:S(2)}) copy-start(bf16[512,1024]{1,0:T(8,128)(2,1)} %refs_3_.1) | copy-start | bytes 3145732
  27.0 4.0 %copy-start.1 = (bf16[512,1024]{1,0:T(8,128)(2,1)S(1)}, bf16[512,1024]{1,0:T(8,128)(2,1)}, u32[]{:S(2)}) copy-start(bf16[512,1024]{1,0:T(8,128)(2,1)} %refs_5_.1) | copy-start | bytes 3145732
  27.3 13.2 %collective-permute-start.2 = (bf16[256,1024]{1,0:T(8,128)(2,1)S(1)}, bf16[256,1024]{1,0:T(8,128)(2,1)S(1)}, u32[]{:S(2)}, u32[]{:S(2)}) collective-permute-start(bf16[256,1024]{1,0:T(8,128)(2,1)S(1)} %get-tuple-element.46), channel_id=1, source_target_pairs={{4,0},{0,4},{12,8},{8,12},{20,16},{16,20},{28,24},{24,28},{5,1},{1... | collective-permute-start | bytes 1572872 | tf_op jit(solution)/shard_map/ppermute | solution.py:452
  29.5 13.1 %collective-permute-start.10 = (bf16[1024,256]{1,0:T(8,128)(2,1)S(1)}, bf16[1024,256]{1,0:T(8,128)(2,1)S(1)}, u32[]{:S(2)}, u32[]{:S(2)}) collective-permute-start(bf16[1024,256]{1,0:T(8,128)(2,1)S(1)} %get-tuple-element.57), channel_id=1, source_target_pairs={{2,0},{3,1},{0,2},{1,3},{6,4},{7,5},{4,6},{5,7},{10,8},{11,9},{8,1... | collective-permute-start | bytes 1572872 | tf_op jit(solution)/shard_map/ppermute | solution.py:455
  31.0 16.3 %collective-permute-start.6 = (bf16[512,1024]{1,0:T(8,128)(2,1)S(1)}, bf16[512,1024]{1,0:T(8,128)(2,1)S(1)}, u32[]{:S(2)}, u32[]{:S(2)}) collective-permute-start(bf16[512,1024]{1,0:T(8,128)(2,1)S(1)} %copy-done), channel_id=1, source_target_pairs={{1,0},{0,1},{3,2},{2,3},{5,4},{4,5},{7,6},{6,7},{9,8},{8,9},{11,10... | collective-permute-start | bytes 3145736 | tf_op jit(solution)/shard_map/ppermute | solution.py:449
  31.0 19.8 %collective-permute-start.8 = (bf16[512,1024]{1,0:T(8,128)(2,1)S(1)}, bf16[512,1024]{1,0:T(8,128)(2,1)S(1)}, u32[]{:S(2)}, u32[]{:S(2)}) collective-permute-start(bf16[512,1024]{1,0:T(8,128)(2,1)S(1)} %copy-done.1), channel_id=1, source_target_pairs={{1,0},{0,1},{3,2},{2,3},{5,4},{4,5},{7,6},{6,7},{9,8},{8,9},{11,10... | collective-permute-start | bytes 3145736 | tf_op jit(solution)/shard_map/ppermute | solution.py:449
  40.5 24.0 %collective-permute-start.12 = (bf16[512,1024]{1,0:T(8,128)(2,1)S(1)}, bf16[512,1024]{1,0:T(8,128)(2,1)S(1)}, u32[]{:S(2)}, u32[]{:S(2)}) collective-permute-start(bf16[512,1024]{1,0:T(8,128)(2,1)S(1)} %copy-done.1), channel_id=1, source_target_pairs={{2,0},{3,1},{0,2},{1,3},{6,4},{7,5},{4,6},{5,7},{10,8},{11,9},{8,1... | collective-permute-start | bytes 3145736 | tf_op jit(solution)/shard_map/ppermute | solution.py:455
  42.6 13.9 %collective-permute-start.7 = (bf16[512,1024]{1,0:T(8,128)(2,1)S(1)}, bf16[512,1024]{1,0:T(8,128)(2,1)S(1)}, u32[]{:S(2)}, u32[]{:S(2)}) collective-permute-start(bf16[512,1024]{1,0:T(8,128)(2,1)S(1)} %collective-permute-done.1.refs_3_.refs_7_), channel_id=1, source_target_pairs={{1,0},{0,1},{3,2},{2,3},{5,4},{4,5},{7,6},{6,7},{9,8},{8,9},{11,10... | collective-permute-start | bytes 3145736 | tf_op jit(solution)/shard_map/ppermute | solution.py:449
  43.3 25.0 %collective-permute-start.11 = (bf16[1024,512]{1,0:T(8,128)(2,1)S(1)}, bf16[1024,512]{1,0:T(8,128)(2,1)S(1)}, u32[]{:S(2)}, u32[]{:S(2)}) collective-permute-start(bf16[1024,512]{1,0:T(8,128)(2,1)S(1)} %shard_map.127.refs_0_), channel_id=1, source_target_pairs={{4,0},{0,4},{12,8},{8,12},{20,16},{16,20},{28,24},{24,28},{5,1},{1... | collective-permute-start | bytes 3145736 | tf_op jit(solution)/shard_map/ppermute | solution.py:452
  47.3 5.0 %collective-permute-start.4 = (f32[12,384]{1,0:T(8,128)S(1)}, f32[12,384]{1,0:T(8,128)S(1)}, u32[]{:S(2)}, u32[]{:S(2)}) collective-permute-start(f32[12,384]{1,0:T(8,128)S(1)} %get-tuple-element.51), channel_id=1, source_target_pairs={{0,8},{4,12},{8,16},{12,20},{16,24},{20,28},{1,9},{5,13},{9,17},{1... | collective-permute-start | bytes 55304 | tf_op jit(solution)/shard_map/ppermute | solution.py:70
  50.8 5.7 %collective-permute-start.5 = (f32[12,384]{1,0:T(8,128)S(1)}, f32[12,384]{1,0:T(8,128)S(1)}, u32[]{:S(2)}, u32[]{:S(2)}) collective-permute-start(f32[12,384]{1,0:T(8,128)S(1)} %get-tuple-element.52), channel_id=1, source_target_pairs={{8,0},{12,4},{16,8},{20,12},{24,16},{28,20},{9,1},{13,5},{17,9},{2... | collective-permute-start | bytes 55304 | tf_op jit(solution)/shard_map/ppermute | solution.py:70
  60.3 4.2 %collective-permute-start.9 = (bf16[512,512]{1,0:T(8,128)(2,1)S(1)}, bf16[512,512]{1,0:T(8,128)(2,1)S(1)}, u32[]{:S(2)}, u32[]{:S(2)}) collective-permute-start(bf16[512,512]{1,0:T(8,128)(2,1)S(1)} %get-tuple-element.55.refs_1_), channel_id=1, source_target_pairs={{1,0},{0,1},{3,2},{2,3},{5,4},{4,5},{7,6},{6,7},{9,8},{8,9},{11,10... | collective-permute-start | bytes 1572872 | tf_op jit(solution)/shard_map/ppermute | solution.py:449
  60.4 10.8 %collective-permute-start.17 = (bf16[1024,512]{1,0:T(8,128)(2,1)S(1)}, bf16[1024,512]{1,0:T(8,128)(2,1)S(1)}, u32[]{:S(2)}, u32[]{:S(2)}) collective-permute-start(bf16[1024,512]{1,0:T(8,128)(2,1)S(1)} %shard_map.127.refs_0_), channel_id=1, source_target_pairs={{1,0},{0,1},{3,2},{2,3},{5,4},{4,5},{7,6},{6,7},{9,8},{8,9},{11,10... | collective-permute-start | bytes 3145736 | tf_op jit(solution)/shard_map/ppermute | solution.py:449
  68.5 19.2 %collective-permute-start.18 = (bf16[1024,512]{1,0:T(8,128)(2,1)S(1)}, bf16[1024,512]{1,0:T(8,128)(2,1)S(1)}, u32[]{:S(2)}, u32[]{:S(2)}) collective-permute-start(bf16[1024,512]{1,0:T(8,128)(2,1)S(1)} %shard_map.133), channel_id=1, source_target_pairs={{1,0},{0,1},{3,2},{2,3},{5,4},{4,5},{7,6},{6,7},{9,8},{8,9},{11,10... | collective-permute-start | bytes 3145736 | tf_op jit(solution)/shard_map/ppermute | solution.py:449
  68.6 24.2 %collective-permute-start.16 = (bf16[512,1024]{1,0:T(8,128)(2,1)S(1)}, bf16[512,1024]{1,0:T(8,128)(2,1)S(1)}, u32[]{:S(2)}, u32[]{:S(2)}) collective-permute-start(bf16[512,1024]{1,0:T(8,128)(2,1)S(1)} %collective-permute-done.12.refs_3_.refs_9_), channel_id=1, source_target_pairs={{1,0},{0,1},{3,2},{2,3},{5,4},{4,5},{7,6},{6,7},{9,8},{8,9},{11,10... | collective-permute-start | bytes 3145736 | tf_op jit(solution)/shard_map/ppermute | solution.py:449
  69.1 14.8 %collective-permute-start.19 = (bf16[1024,256]{1,0:T(8,128)(2,1)S(1)}, bf16[1024,256]{1,0:T(8,128)(2,1)S(1)}, u32[]{:S(2)}, u32[]{:S(2)}) collective-permute-start(bf16[1024,256]{1,0:T(8,128)(2,1)S(1)} %get-tuple-element.58.refs_5_.refs_1_.refs_4_), channel_id=1, source_target_pairs={{2,0},{3,1},{0,2},{1,3},{6,4},{7,5},{4,6},{5,7},{10,8},{11,9},{8,1... | collective-permute-start | bytes 1572872 | tf_op jit(solution)/shard_map/ppermute | solution.py:455
  70.9 21.8 %collective-permute-start.15 = (bf16[256,1024]{1,0:T(8,128)(2,1)S(1)}, bf16[256,1024]{1,0:T(8,128)(2,1)S(1)}, u32[]{:S(2)}, u32[]{:S(2)}) collective-permute-start(bf16[256,1024]{1,0:T(8,128)(2,1)S(1)} %get-tuple-element.65), channel_id=1, source_target_pairs={{4,0},{0,4},{12,8},{8,12},{20,16},{16,20},{28,24},{24,28},{5,1},{1... | collective-permute-start | bytes 1572872 | tf_op jit(solution)/shard_map/ppermute | solution.py:452
  71.2 27.7 %collective-permute-start.23 = (bf16[1024,256]{1,0:T(8,128)(2,1)S(1)}, bf16[1024,256]{1,0:T(8,128)(2,1)S(1)}, u32[]{:S(2)}, u32[]{:S(2)}) collective-permute-start(bf16[1024,256]{1,0:T(8,128)(2,1)S(1)} %get-tuple-element.59.refs_6_.refs_2_.refs_4_), channel_id=1, source_target_pairs={{2,0},{3,1},{0,2},{1,3},{6,4},{7,5},{4,6},{5,7},{10,8},{11,9},{8,1... | collective-permute-start | bytes 1572872 | tf_op jit(solution)/shard_map/ppermute | solution.py:455
  83.8 17.5 %collective-permute-start.13 = (bf16[384,512]{1,0:T(8,128)(2,1)S(1)}, bf16[384,512]{1,0:T(8,128)(2,1)S(1)}, u32[]{:S(2)}, u32[]{:S(2)}) collective-permute-start(bf16[384,512]{1,0:T(8,128)(2,1)S(1)} %get-tuple-element.61.refs_6_), channel_id=1, source_target_pairs={{0,8},{4,12},{8,16},{12,20},{16,24},{20,28},{1,9},{5,13},{9,17},{1... | collective-permute-start | bytes 1179656 | tf_op jit(solution)/shard_map/ppermute | solution.py:70
  89.4 21.3 %collective-permute-start.20 = (bf16[1024,128]{1,0:T(8,128)(2,1)S(1)}, bf16[1024,128]{1,0:T(8,128)(2,1)S(1)}, u32[]{:S(2)}, u32[]{:S(2)}) collective-permute-start(bf16[1024,128]{1,0:T(8,128)(2,1)S(1)} %get-tuple-element.68), channel_id=1, source_target_pairs={{8,0},{0,24},{12,4},{4,28},{9,1},{1,25},{13,5},{5,29},{10,2},{2,26... | collective-permute-start | bytes 786440 | tf_op jit(solution)/shard_map/ppermute | solution.py:613
  96.4 18.8 %collective-permute-start.21 = (bf16[1024,128]{1,0:T(8,128)(2,1)S(1)}, bf16[1024,128]{1,0:T(8,128)(2,1)S(1)}, u32[]{:S(2)}, u32[]{:S(2)}) collective-permute-start(bf16[1024,128]{1,0:T(8,128)(2,1)S(1)} %get-tuple-element.69), channel_id=1, source_target_pairs={{16,0},{8,24},{20,4},{12,28},{17,1},{9,25},{21,5},{13,29},{18,2},{... | collective-permute-start | bytes 786440 | tf_op jit(solution)/shard_map/ppermute | solution.py:613
  97.6 18.2 %collective-permute-start.22 = (bf16[1024,128]{1,0:T(8,128)(2,1)S(1)}, bf16[1024,128]{1,0:T(8,128)(2,1)S(1)}, u32[]{:S(2)}, u32[]{:S(2)}) collective-permute-start(bf16[1024,128]{1,0:T(8,128)(2,1)S(1)} %get-tuple-element.70), channel_id=1, source_target_pairs={{24,0},{16,24},{28,4},{20,28},{25,1},{17,25},{29,5},{21,29},{26,2}... | collective-permute-start | bytes 786440 | tf_op jit(solution)/shard_map/ppermute | solution.py:613
  100.6 15.2 %collective-permute-start.24 = (bf16[1024,128]{1,0:T(8,128)(2,1)S(1)}, bf16[1024,128]{1,0:T(8,128)(2,1)S(1)}, u32[]{:S(2)}, u32[]{:S(2)}) collective-permute-start(bf16[1024,128]{1,0:T(8,128)(2,1)S(1)} %get-tuple-element.73), channel_id=1, source_target_pairs={{16,8},{24,16},{20,12},{28,20},{17,9},{25,17},{21,13},{29,21},{18,... | collective-permute-start | bytes 786440 | tf_op jit(solution)/shard_map/ppermute | solution.py:613
  101.3 14.5 %collective-permute-start.25 = (bf16[1024,128]{1,0:T(8,128)(2,1)S(1)}, bf16[1024,128]{1,0:T(8,128)(2,1)S(1)}, u32[]{:S(2)}, u32[]{:S(2)}) collective-permute-start(bf16[1024,128]{1,0:T(8,128)(2,1)S(1)} %get-tuple-element.74), channel_id=1, source_target_pairs={{24,8},{0,16},{28,12},{4,20},{25,9},{1,17},{29,13},{5,21},{26,10},... | collective-permute-start | bytes 786440 | tf_op jit(solution)/shard_map/ppermute | solution.py:613
  110.7 6.7 %collective-permute-start.26 = (bf16[1024,128]{1,0:T(8,128)(2,1)S(1)}, bf16[1024,128]{1,0:T(8,128)(2,1)S(1)}, u32[]{:S(2)}, u32[]{:S(2)}) collective-permute-start(bf16[1024,128]{1,0:T(8,128)(2,1)S(1)} %get-tuple-element.75), channel_id=1, source_target_pairs={{0,8},{8,16},{4,12},{12,20},{1,9},{9,17},{5,13},{13,21},{2,10},{10... | collective-permute-start | bytes 786440 | tf_op jit(solution)/shard_map/ppermute | solution.py:613
  115.2 6.4 %collective-permute-start.14 = (bf16[256,512]{1,0:T(8,128)(2,1)S(1)}, bf16[256,512]{1,0:T(8,128)(2,1)S(1)}, u32[]{:S(2)}, u32[]{:S(2)}) collective-permute-start(bf16[256,512]{1,0:T(8,128)(2,1)S(1)} %get-tuple-element.63), channel_id=1, source_target_pairs={{4,0},{0,4},{12,8},{8,12},{20,16},{16,20},{28,24},{24,28},{5,1},{1... | collective-permute-start | bytes 786440 | tf_op jit(solution)/shard_map/ppermute | solution.py:452
  117.6 5.0 %collective-permute-start.27 = (f32[512,128]{1,0:T(8,128)S(1)}, f32[512,128]{1,0:T(8,128)S(1)}, u32[]{:S(2)}, u32[]{:S(2)}) collective-permute-start(f32[512,128]{1,0:T(8,128)S(1)} %get-tuple-element.77), channel_id=1, source_target_pairs={{1,0},{0,1},{3,2},{2,3},{5,4},{4,5},{7,6},{6,7},{9,8},{8,9},{11,10... | collective-permute-start | bytes 786440 | tf_op jit(solution)/shard_map/ppermute | solution.py:449

commit v6 on v5

--- a/solution.py
+++ b/solution.py
@@ -509,7 +509,7 @@
         join_body,
         [shape((4 * tokens, width), bf16) for width in widths],
         (mine, exchanged(other)),
-        after=(turned_pair, *value_weights[1:]),
+        after=(turned_pair,),
     )
     groups = [[low, *(fetched(low, away) for away in range(1, chips))] for low in lows]
     query_kept, query_sent = kernel_call(
@@ -557,7 +557,7 @@
         join_body,
         [shape((4 * tokens, width), bf16) for width in widths],
         (mine, exchanged(other)),
-        after=(turned_pair, *value_weights[1:]),
+        after=(turned_pair,),
     )
     groups = [[low, *(fetched(low, away) for away in range(1, chips))] for low in lows]
     query_own, query_up = kernel_call(
@@ -603,7 +603,7 @@
             functools.partial(weight_body, tables, tokens),
             [shape((2 * rows, HS), f32 if away == 0 else bf16) for away in range(half)],
             (*sides, *group),
-            after=(partials[0], result_token) if index else (query_up,),
+            after=(partials[0],) if index else (query_up,),
             scratch=[pltpu.VMEM((2 * rows, width), f32)],
             flops=1 if index else WEIGHT_FLOPS,
         )
@@ -620,6 +620,7 @@
             functools.partial(final_body, belongs, [len(parcels) for parcels in sums]),
             [shape((rows, HS), f32)] * 2,
             [parcel for parcels in sums for parcel in parcels],
+            after=(result_token,),
         )
     else:
         partial = jnp.concatenate(partials, axis=1)

time: 124 us -> 123 us (level)
    ppermute x5, waiting for transfers between devices: 16.1 us -> 14.2 us  [fetched(): return lax.ppermute(array, 'fsdp', rolled_pairs(n_fsdp, away, 0))]
    ppermute x8, waiting for transfers between devices: 0.02 us -> 1.42 us  [exchanged(): return lax.ppermute(array, 'fsdp', rolled_pairs(n_fsdp, 0, 1))]
  transfers between devices with their start and end apart: 28 -> 28, of which waited for: 12 -> 13; matrix products, arithmetic and copies ran while one was open for 1% -> 1% of each run, Pallas kernels for 16% -> 16%
where the time goes in v6:
time: 123 us; the launch traced here: 122 us
  waiting for transfers between devices  54.1 us (44%)
  starting transfers between devices  43.7 us (36%)
  Pallas kernels  19.8 us (16%)
  local copies, waits for them, and re-layouts  2.26 us (2%)
  between operations  1.59 us (1%)
    ppermute x5, waiting for transfers between devices, swapped(): return lax.ppermute(array, 'tm', rolled_pairs(n_tm, 0, 1))  29.4 us
    pallas_call x18, Pallas kernels, kernel_call(): pl.pallas_call(run, out_shape=tuple(outs), in_specs=[VMEM] * count + [ANY...  19.8 us
    ppermute x6, starting transfers between devices, shards(): parcels.append(lax.ppermute(chunks[away], 'tm', routes))  17.1 us
    ppermute x5, waiting for transfers between devices, fetched(): return lax.ppermute(array, 'fsdp', rolled_pairs(n_fsdp, away, 0))  14.2 us
    ppermute x4, starting transfers between devices, shifted(): lax.ppermute(value, axis, [(s, s + steps) for s in range(max(0, -steps),...  10.3 us
    ppermute x5, starting transfers between devices, fetched(): return lax.ppermute(array, 'fsdp', rolled_pairs(n_fsdp, away, 0))  8.01 us
    ppermute x5, starting transfers between devices, swapped(): return lax.ppermute(array, 'tm', rolled_pairs(n_tm, 0, 1))  6.56 us
    ppermute x4, waiting for transfers between devices, shifted(): lax.ppermute(value, axis, [(s, s + steps) for s in range(max(0, -steps),...  4.89 us
  transfers between devices with their start and end apart: 28, of which 13 were waited for; matrix products, arithmetic and copies ran while one was open for 1% of the time, Pallas kernels for 16%

profile of v6, /device:TPU:0, one launch (start us, length us, event | category | flops | bytes accessed | tf_op | source)
XLA Modules:
  0.0 122.1 jit_solution(17768499986336430523)
XLA Ops:
  0.6 3.0 %collective-permute-start.1 = (bf16[512,1024]{1,0:T(8,128)(2,1)}, bf16[512,1024]{1,0:T(8,128)(2,1)S(1)}, u32[]{:S(2)}, u32[]{:S(2)}) collective-permute-start(bf16[512,1024]{1,0:T(8,128)(2,1)} %refs_3_.1), channel_id=1, source_target_pairs={{2,0},{3,1},{0,2},{1,3},{6,4},{7,5},{4,6},{5,7},{10,8},{11,9},{8,1... | collective-permute-start | bytes 3145736 | tf_op jit(solution)/shard_map/ppermute | solution.py:455
  4.3 0.7 fusion.1
  5.0 0.1 convert_element_type.9
  5.1 0.1 broadcast_in_dim.26.refs_0_
  5.2 1.0 copy-done.3
  6.2 1.0 copy-done.4
  7.2 0.3 shard_map.120
  7.5 1.6 %collective-permute-start = (bf16[272,1024]{1,0:T(8,128)(2,1)S(1)}, bf16[272,1024]{1,0:T(8,128)(2,1)S(1)}, u32[]{:S(2)}, u32[]{:S(2)}) collective-permute-start(bf16[272,1024]{1,0:T(8,128)(2,1)S(1)} %get-tuple-element.43), channel_id=1, source_target_pairs={{4,0},{0,4},{12,8},{8,12},{20,16},{16,20},{28,24},{24,28},{5,1},{1... | collective-permute-start | bytes 1671176 | tf_op jit(solution)/shard_map/ppermute | solution.py:452
  9.1 12.6 %collective-permute-done.refs_2_ = bf16[272,1024]{1,0:T(8,128)(2,1)S(1)} collective-permute-done((bf16[272,1024]{1,0:T(8,128)(2,1)S(1)}, bf16[272,1024]{1,0:T(8,128)(2,1)S(1)}, u32[]{:S(2)}, u32[]{:S(2)}) %collective-permute-start) | collective-permute-done | bytes 557088 | tf_op jit(solution)/shard_map/ppermute | solution.py:452
  21.7 0.1 shard_map.121
  21.8 1.4 %collective-permute-start.3 = (bf16[416,1024]{1,0:T(8,128)(2,1)S(1)}, bf16[416,1024]{1,0:T(8,128)(2,1)S(1)}, u32[]{:S(2)}, u32[]{:S(2)}) collective-permute-start(bf16[416,1024]{1,0:T(8,128)(2,1)S(1)} %get-tuple-element.47), channel_id=1, source_target_pairs={{8,0},{12,4},{16,8},{20,12},{24,16},{28,20},{9,1},{13,5},{17,9},{2... | collective-permute-start | bytes 2555912 | tf_op jit(solution)/shard_map/ppermute | solution.py:70
  23.2 3.8 %collective-permute-done.1.refs_3_.refs_7_ = bf16[512,1024]{1,0:T(8,128)(2,1)S(1)} collective-permute-done((bf16[512,1024]{1,0:T(8,128)(2,1)}, bf16[512,1024]{1,0:T(8,128)(2,1)S(1)}, u32[]{:S(2)}, u32[]{:S(2)}) %collective-permute-start.1) | collective-permute-done | bytes 1048608 | tf_op jit(solution)/shard_map/ppermute | solution.py:455
  27.0 0.3 shard_map.122
  27.3 1.8 %collective-permute-start.2 = (bf16[256,1024]{1,0:T(8,128)(2,1)S(1)}, bf16[256,1024]{1,0:T(8,128)(2,1)S(1)}, u32[]{:S(2)}, u32[]{:S(2)}) collective-permute-start(bf16[256,1024]{1,0:T(8,128)(2,1)S(1)} %get-tuple-element.46), channel_id=1, source_target_pairs={{4,0},{0,4},{12,8},{8,12},{20,16},{16,20},{28,24},{24,28},{5,1},{1... | collective-permute-start | bytes 1572872 | tf_op jit(solution)/shard_map/ppermute | solution.py:452
  29.2 0.3 shard_map.126
  29.5 1.6 %collective-permute-start.10 = (bf16[1024,256]{1,0:T(8,128)(2,1)S(1)}, bf16[1024,256]{1,0:T(8,128)(2,1)S(1)}, u32[]{:S(2)}, u32[]{:S(2)}) collective-permute-start(bf16[1024,256]{1,0:T(8,128)(2,1)S(1)} %get-tuple-element.57), channel_id=1, source_target_pairs={{2,0},{3,1},{0,2},{1,3},{6,4},{7,5},{4,6},{5,7},{10,8},{11,9},{8,1... | collective-permute-start | bytes 1572872 | tf_op jit(solution)/shard_map/ppermute | solution.py:455
  31.0 0.5 collective-permute-start.8
  31.6 8.9 %collective-permute-done.2.refs_1_.refs_2_ = bf16[256,1024]{1,0:T(8,128)(2,1)S(1)} collective-permute-done((bf16[256,1024]{1,0:T(8,128)(2,1)S(1)}, bf16[256,1024]{1,0:T(8,128)(2,1)S(1)}, u32[]{:S(2)}, u32[]{:S(2)}) %collective-permute-start.2) | collective-permute-done | bytes 524320 | tf_op jit(solution)/shard_map/ppermute | solution.py:452
  40.5 1.4 %collective-permute-start.15 = (bf16[512,1024]{1,0:T(8,128)(2,1)S(1)}, bf16[512,1024]{1,0:T(8,128)(2,1)S(1)}, u32[]{:S(2)}, u32[]{:S(2)}) collective-permute-start(bf16[512,1024]{1,0:T(8,128)(2,1)S(1)} %copy-done.1), channel_id=1, source_target_pairs={{2,0},{3,1},{0,2},{1,3},{6,4},{7,5},{4,6},{5,7},{10,8},{11,9},{8,1... | collective-permute-start | bytes 3145736 | tf_op jit(solution)/shard_map/ppermute | solution.py:455
  41.9 0.1 shard_map.123.refs_1_
  42.0 0.6 collective-permute-done.10.refs_1_
  42.6 0.1 shard_map.127.refs_0_
  42.7 0.6 collective-permute-done.3.refs_3_.refs_2_
  43.3 1.5 %collective-permute-start.11 = (bf16[1024,512]{1,0:T(8,128)(2,1)S(1)}, bf16[1024,512]{1,0:T(8,128)(2,1)S(1)}, u32[]{:S(2)}, u32[]{:S(2)}) collective-permute-start(bf16[1024,512]{1,0:T(8,128)(2,1)S(1)} %shard_map.127.refs_0_), channel_id=1, source_target_pairs={{4,0},{0,4},{12,8},{8,12},{20,16},{16,20},{28,24},{24,28},{5,1},{1... | collective-permute-start | bytes 3145736 | tf_op jit(solution)/shard_map/ppermute | solution.py:452
  44.8 2.4 %shard_map.124 = (f32[12,896]{1,0:T(8,128)S(1)}, f32[12,384]{1,0:T(8,128)S(1)}, f32[12,384]{1,0:T(8,128)S(1)}, f32[2,256,640]{2,1,0:T(8,128)S(1)}) custom-call(bf16[512,1024]{1,0:T(8,128)(2,1)S(1)} %get-tuple-element.44.refs_0_, bf16[512,1024]{1,0:T(8,128)(2,1)S(1)} %shard_map.123.refs_1_, bf16[32,128]{1,0:T(8,128)(2,1)S(1)} %get-tuple-element.48.refs_2_, ...), custom_call_target="tpu_custom_call" | custom-call | flops 20000000000 | bytes 1 | tf_op jit(solution)/shard_map/pallas_call | solution.py:44
  47.2 3.5 %collective-permute-start.4 = (f32[12,384]{1,0:T(8,128)S(1)}, f32[12,384]{1,0:T(8,128)S(1)}, u32[]{:S(2)}, u32[]{:S(2)}) collective-permute-start(f32[12,384]{1,0:T(8,128)S(1)} %get-tuple-element.51), channel_id=1, source_target_pairs={{0,8},{4,12},{8,16},{12,20},{16,24},{20,28},{1,9},{5,13},{9,17},{1... | collective-permute-start | bytes 55304 | tf_op jit(solution)/shard_map/ppermute | solution.py:70
  50.7 0.0 collective-permute-done.8.refs_9_.refs_6_
  50.7 1.5 %collective-permute-start.5 = (f32[12,384]{1,0:T(8,128)S(1)}, f32[12,384]{1,0:T(8,128)S(1)}, u32[]{:S(2)}, u32[]{:S(2)}) collective-permute-start(f32[12,384]{1,0:T(8,128)S(1)} %get-tuple-element.52), channel_id=1, source_target_pairs={{8,0},{12,4},{16,8},{20,12},{24,16},{28,20},{9,1},{13,5},{17,9},{2... | collective-permute-start | bytes 55304 | tf_op jit(solution)/shard_map/ppermute | solution.py:70
  52.2 0.0 collective-permute-done.4.refs_5_
  52.2 4.2 %collective-permute-done.5.refs_6_ = f32[12,384]{1,0:T(8,128)S(1)} collective-permute-done((f32[12,384]{1,0:T(8,128)S(1)}, f32[12,384]{1,0:T(8,128)S(1)}, u32[]{:S(2)}, u32[]{:S(2)}) %collective-permute-start.5) | collective-permute-done | bytes 18464 | tf_op jit(solution)/shard_map/ppermute | solution.py:70
  56.4 3.7 %shard_map.125 = (bf16[512,512]{1,0:T(8,128)(2,1)S(1)}, bf16[512,512]{1,0:T(8,128)(2,1)S(1)}, bf16[256,1024]{1,0:T(8,128)(2,1)S(1)}, f32[12,896]{1,0:T(8,128)S(1)}) custom-call(bf16[512,1024]{1,0:T(8,128)(2,1)S(1)} %get-tuple-element.44.refs_0_, bf16[512,1024]{1,0:T(8,128)(2,1)S(1)} %shard_map.123.refs_1_, ...), custom_call_target="tpu_custom_call" | custom-call | flops 1 | bytes 1 | tf_op jit(solution)/shard_map/pallas_call | solution.py:44
  60.1 0.1 collective-permute-start.9
  60.2 0.5 collective-permute-start.17
  60.7 1.4 %collective-permute-done.9.refs_1_ = bf16[512,512]{1,0:T(8,128)(2,1)S(1)} collective-permute-done((bf16[512,512]{1,0:T(8,128)(2,1)S(1)}, bf16[512,512]{1,0:T(8,128)(2,1)S(1)}, u32[]{:S(2)}, u32[]{:S(2)}) %collective-permute-start.9) | collective-permute-done | bytes 524320 | tf_op jit(solution)/shard_map/ppermute | solution.py:449
  62.1 6.2 %collective-permute-done.11.refs_2_.refs_0_.refs_1_ = bf16[1024,512]{1,0:T(8,128)(2,1)S(1)} collective-permute-done((bf16[1024,512]{1,0:T(8,128)(2,1)S(1)}, bf16[1024,512]{1,0:T(8,128)(2,1)S(1)}, u32[]{:S(2)}, u32[]{:S(2)}) %collective-permute-start.11) | collective-permute-done | bytes 1048608 | tf_op jit(solution)/shard_map/ppermute | solution.py:452
  68.3 0.1 shard_map.128
  68.4 0.1 shard_map.133
  68.5 0.1 collective-permute-start.18
  68.6 0.5 collective-permute-start.16
  69.1 1.9 %collective-permute-start.19 = (bf16[1024,256]{1,0:T(8,128)(2,1)S(1)}, bf16[1024,256]{1,0:T(8,128)(2,1)S(1)}, u32[]{:S(2)}, u32[]{:S(2)}) collective-permute-start(bf16[1024,256]{1,0:T(8,128)(2,1)S(1)} %get-tuple-element.58.refs_5_.refs_1_.refs_4_), channel_id=1, source_target_pairs={{2,0},{3,1},{0,2},{1,3},{6,4},{7,5},{4,6},{5,7},{10,8},{11,9},{8,1... | collective-permute-start | bytes 1572872 | tf_op jit(solution)/shard_map/ppermute | solution.py:455
  70.9 0.1 collective-permute-start.23
  71.1 1.0 collective-permute-start.14
  72.1 3.6 %shard_map.129 = (f32[512,512]{1,0:T(8,128)S(1)}, bf16[384,512]{1,0:T(8,128)(2,1)S(1)}) custom-call(bf16[512,1024]{1,0:T(8,128)(2,1)S(1)} %get-tuple-element.44.refs_0_, bf16[512,1024]{1,0:T(8,128)(2,1)S(1)} %shard_map.123.refs_1_, bf16[416,1024]{1,0:T(8,128)(2,1)S(1)} %collective-permute-done.3.refs_3_.refs_2_, ...), custom_call_target="tpu_custom_call" | custom-call | flops 1 | bytes 1 | tf_op jit(solution)/shard_map/pallas_call | solution.py:44
  75.7 8.2 %collective-permute-done.19.refs_5_ = bf16[1024,256]{1,0:T(8,128)(2,1)S(1)} collective-permute-done((bf16[1024,256]{1,0:T(8,128)(2,1)S(1)}, bf16[1024,256]{1,0:T(8,128)(2,1)S(1)}, u32[]{:S(2)}, u32[]{:S(2)}) %collective-permute-start.19) | collective-permute-done | bytes 524320 | tf_op jit(solution)/shard_map/ppermute | solution.py:455
  83.8 3.9 %collective-permute-start.12 = (bf16[384,512]{1,0:T(8,128)(2,1)S(1)}, bf16[384,512]{1,0:T(8,128)(2,1)S(1)}, u32[]{:S(2)}, u32[]{:S(2)}) collective-permute-start(bf16[384,512]{1,0:T(8,128)(2,1)S(1)} %get-tuple-element.61.refs_6_), channel_id=1, source_target_pairs={{0,8},{4,12},{8,16},{12,20},{16,24},{20,28},{1,9},{5,13},{9,17},{1... | collective-permute-start | bytes 1179656 | tf_op jit(solution)/shard_map/ppermute | solution.py:70
  87.7 1.6 %shard_map.134 = (f32[1024,128]{1,0:T(8,128)S(1)}, bf16[1024,128]{1,0:T(8,128)(2,1)S(1)}, bf16[1024,128]{1,0:T(8,128)(2,1)S(1)}, bf16[1024,128]{1,0:T(8,128)(2,1)S(1)}) custom-call(bf16[1024,512]{1,0:T(8,128)(2,1)S(1)} %shard_map.127.refs_0_, bf16[1024,512]{1,0:T(8,128)(2,1)S(1)} %collective-permute-done.11.refs_2_.refs_0_.refs_1_, ...), custom_call_target="tpu_custom_call" | custom-call | flops 1 | bytes 1 | tf_op jit(solution)/shard_map/pallas_call | solution.py:44
  89.4 3.3 %collective-permute-start.20 = (bf16[1024,128]{1,0:T(8,128)(2,1)S(1)}, bf16[1024,128]{1,0:T(8,128)(2,1)S(1)}, u32[]{:S(2)}, u32[]{:S(2)}) collective-permute-start(bf16[1024,128]{1,0:T(8,128)(2,1)S(1)} %get-tuple-element.68), channel_id=1, source_target_pairs={{8,0},{0,24},{12,4},{4,28},{9,1},{1,25},{13,5},{5,29},{10,2},{2,26... | collective-permute-start | bytes 786440 | tf_op jit(solution)/shard_map/ppermute | solution.py:613
  92.7 1.7 %collective-permute-done.23.refs_5_ = bf16[1024,256]{1,0:T(8,128)(2,1)S(1)} collective-permute-done((bf16[1024,256]{1,0:T(8,128)(2,1)S(1)}, bf16[1024,256]{1,0:T(8,128)(2,1)S(1)}, u32[]{:S(2)}, u32[]{:S(2)}) %collective-permute-start.23) | collective-permute-done | bytes 524320 | tf_op jit(solution)/shard_map/ppermute | solution.py:455
  94.3 1.3 %collective-permute-start.21 = (bf16[1024,128]{1,0:T(8,128)(2,1)S(1)}, bf16[1024,128]{1,0:T(8,128)(2,1)S(1)}, u32[]{:S(2)}, u32[]{:S(2)}) collective-permute-start(bf16[1024,128]{1,0:T(8,128)(2,1)S(1)} %get-tuple-element.69), channel_id=1, source_target_pairs={{16,0},{8,24},{20,4},{12,28},{17,1},{9,25},{21,5},{13,29},{18,2},{... | collective-permute-start | bytes 786440 | tf_op jit(solution)/shard_map/ppermute | solution.py:613
  95.6 1.7 %shard_map.135 = (f32[1024,128]{1,0:T(8,128)S(1)}, bf16[1024,128]{1,0:T(8,128)(2,1)S(1)}, bf16[1024,128]{1,0:T(8,128)(2,1)S(1)}, bf16[1024,128]{1,0:T(8,128)(2,1)S(1)}) custom-call(bf16[1024,512]{1,0:T(8,128)(2,1)S(1)} %shard_map.127.refs_0_, bf16[1024,512]{1,0:T(8,128)(2,1)S(1)} %collective-permute-done.11.refs_2_.refs_0_.refs_1_, ...), custom_call_target="tpu_custom_call" | custom-call | flops 1 | bytes 1 | tf_op jit(solution)/shard_map/pallas_call | solution.py:44
  97.3 1.3 %collective-permute-start.22 = (bf16[1024,128]{1,0:T(8,128)(2,1)S(1)}, bf16[1024,128]{1,0:T(8,128)(2,1)S(1)}, u32[]{:S(2)}, u32[]{:S(2)}) collective-permute-start(bf16[1024,128]{1,0:T(8,128)(2,1)S(1)} %get-tuple-element.70), channel_id=1, source_target_pairs={{24,0},{16,24},{28,4},{20,28},{25,1},{17,25},{29,5},{21,29},{26,2}... | collective-permute-start | bytes 786440 | tf_op jit(solution)/shard_map/ppermute | solution.py:613
  98.6 0.7 collective-permute-start.24
  99.3 9.0 %collective-permute-start.25 = (bf16[1024,128]{1,0:T(8,128)(2,1)S(1)}, bf16[1024,128]{1,0:T(8,128)(2,1)S(1)}, u32[]{:S(2)}, u32[]{:S(2)}) collective-permute-start(bf16[1024,128]{1,0:T(8,128)(2,1)S(1)} %get-tuple-element.73), channel_id=1, source_target_pairs={{24,8},{0,16},{28,12},{4,20},{25,9},{1,17},{29,13},{5,21},{26,10},... | collective-permute-start | bytes 786440 | tf_op jit(solution)/shard_map/ppermute | solution.py:613
  108.4 1.5 %collective-permute-start.26 = (bf16[1024,128]{1,0:T(8,128)(2,1)S(1)}, bf16[1024,128]{1,0:T(8,128)(2,1)S(1)}, u32[]{:S(2)}, u32[]{:S(2)}) collective-permute-start(bf16[1024,128]{1,0:T(8,128)(2,1)S(1)} %get-tuple-element.74), channel_id=1, source_target_pairs={{0,8},{8,16},{4,12},{12,20},{1,9},{9,17},{5,13},{13,21},{2,10},{10... | collective-permute-start | bytes 786440 | tf_op jit(solution)/shard_map/ppermute | solution.py:613
  109.9 3.6 %shard_map.132 = (bf16[256,2048]{1,0:T(8,128)(2,1)}, f32[8,128]{1,0:T(8,128)S(1)}) custom-call(bf16[512,512]{1,0:T(8,128)(2,1)S(1)} %get-tuple-element.54.refs_0_, bf16[512,512]{1,0:T(8,128)(2,1)S(1)} %get-tuple-element.55.refs_1_, bf16[256,1024]{1,0:T(8,128)(2,1)S(1)} %collective-permute-done.14.refs_2_, bf16[512,1024]{1,0:T(8,128)(2,1)S(1)} %copy-done, ...), custom_call_target="tpu_custom_call" | custom-call | flops 1 | bytes 1 | tf_op jit(solution)/shard_map/pallas_call | solution.py:44
  113.5 0.1 shard_map.130
  113.6 0.7 collective-permute-start.13
  114.3 0.8 collective-permute-done.25.refs_6_
  115.1 3.3 %collective-permute-done.26.refs_7_ = bf16[1024,128]{1,0:T(8,128)(2,1)S(1)} collective-permute-done((bf16[1024,128]{1,0:T(8,128)(2,1)S(1)}, bf16[1024,128]{1,0:T(8,128)(2,1)S(1)}, u32[]{:S(2)}, u32[]{:S(2)}) %collective-permute-start.26) | collective-permute-done | bytes 262176 | tf_op jit(solution)/shard_map/ppermute | solution.py:613
  118.4 0.1 shard_map.136
  118.5 0.1 collective-permute-start.27
  118.6 1.7 %collective-permute-done.13.refs_1_ = bf16[256,512]{1,0:T(8,128)(2,1)S(1)} collective-permute-done((bf16[256,512]{1,0:T(8,128)(2,1)S(1)}, bf16[256,512]{1,0:T(8,128)(2,1)S(1)}, u32[]{:S(2)}, u32[]{:S(2)}) %collective-permute-start.13) | collective-permute-done | bytes 262176 | tf_op jit(solution)/shard_map/ppermute | solution.py:452
  120.3 1.0 shard_map.131
  121.3 0.8 shard_map.137
  (28 shorter events, 0.1 us)
Async XLA Ops:
  0.6 26.4 %collective-permute-start.1 = (bf16[512,1024]{1,0:T(8,128)(2,1)}, bf16[512,1024]{1,0:T(8,128)(2,1)S(1)}, u32[]{:S(2)}, u32[]{:S(2)}) collective-permute-start(bf16[512,1024]{1,0:T(8,128)(2,1)} %refs_3_.1), channel_id=1, source_target_pairs={{2,0},{3,1},{0,2},{1,3},{6,4},{7,5},{4,6},{5,7},{10,8},{11,9},{8,1... | collective-permute-start | bytes 3145736 | tf_op jit(solution)/shard_map/ppermute | solution.py:455
  5.2 1.0 copy-start.3
  6.2 1.0 copy-start.4
  7.2 19.8 %copy-start.5 = (bf16[1,256,1024]{2,1,0:T(8,128)(2,1)S(1)}, bf16[1,256,1024]{2,1,0:T(8,128)(2,1)}, u32[]{:S(2)}) copy-start(bf16[1,256,1024]{2,1,0:T(8,128)(2,1)} %param.11) | copy-start | bytes 1572868
  7.2 19.8 %copy-start.6 = (bf16[1,256,1024]{2,1,0:T(8,128)(2,1)S(1)}, bf16[1,256,1024]{2,1,0:T(8,128)(2,1)}, u32[]{:S(2)}) copy-start(bf16[1,256,1024]{2,1,0:T(8,128)(2,1)} %param.12) | copy-start | bytes 1572868
  7.5 14.2 %collective-permute-start = (bf16[272,1024]{1,0:T(8,128)(2,1)S(1)}, bf16[272,1024]{1,0:T(8,128)(2,1)S(1)}, u32[]{:S(2)}, u32[]{:S(2)}) collective-permute-start(bf16[272,1024]{1,0:T(8,128)(2,1)S(1)} %get-tuple-element.43), channel_id=1, source_target_pairs={{4,0},{0,4},{12,8},{8,12},{20,16},{16,20},{28,24},{24,28},{5,1},{1... | collective-permute-start | bytes 1671176 | tf_op jit(solution)/shard_map/ppermute | solution.py:452
  21.7 7.5 %copy-start.2 = (bf16[1,256,2048]{2,1,0:T(8,128)(2,1)S(1)}, bf16[1,256,2048]{2,1,0:T(8,128)(2,1)}, u32[]{:S(2)}) copy-start(bf16[1,256,2048]{2,1,0:T(8,128)(2,1)} %param.9) | copy-start | bytes 3145732
  21.8 21.5 %collective-permute-start.3 = (bf16[416,1024]{1,0:T(8,128)(2,1)S(1)}, bf16[416,1024]{1,0:T(8,128)(2,1)S(1)}, u32[]{:S(2)}, u32[]{:S(2)}) collective-permute-start(bf16[416,1024]{1,0:T(8,128)(2,1)S(1)} %get-tuple-element.47), channel_id=1, source_target_pairs={{8,0},{12,4},{16,8},{20,12},{24,16},{28,20},{9,1},{13,5},{17,9},{2... | collective-permute-start | bytes 2555912 | tf_op jit(solution)/shard_map/ppermute | solution.py:70
  27.0 4.0 %copy-start = (bf16[512,1024]{1,0:T(8,128)(2,1)S(1)}, bf16[512,1024]{1,0:T(8,128)(2,1)}, u32[]{:S(2)}) copy-start(bf16[512,1024]{1,0:T(8,128)(2,1)} %refs_3_.1) | copy-start | bytes 3145732
  27.0 4.0 %copy-start.1 = (bf16[512,1024]{1,0:T(8,128)(2,1)S(1)}, bf16[512,1024]{1,0:T(8,128)(2,1)}, u32[]{:S(2)}) copy-start(bf16[512,1024]{1,0:T(8,128)(2,1)} %refs_5_.1) | copy-start | bytes 3145732
  27.3 13.2 %collective-permute-start.2 = (bf16[256,1024]{1,0:T(8,128)(2,1)S(1)}, bf16[256,1024]{1,0:T(8,128)(2,1)S(1)}, u32[]{:S(2)}, u32[]{:S(2)}) collective-permute-start(bf16[256,1024]{1,0:T(8,128)(2,1)S(1)} %get-tuple-element.46), channel_id=1, source_target_pairs={{4,0},{0,4},{12,8},{8,12},{20,16},{16,20},{28,24},{24,28},{5,1},{1... | collective-permute-start | bytes 1572872 | tf_op jit(solution)/shard_map/ppermute | solution.py:452
  29.5 13.1 %collective-permute-start.10 = (bf16[1024,256]{1,0:T(8,128)(2,1)S(1)}, bf16[1024,256]{1,0:T(8,128)(2,1)S(1)}, u32[]{:S(2)}, u32[]{:S(2)}) collective-permute-start(bf16[1024,256]{1,0:T(8,128)(2,1)S(1)} %get-tuple-element.57), channel_id=1, source_target_pairs={{2,0},{3,1},{0,2},{1,3},{6,4},{7,5},{4,6},{5,7},{10,8},{11,9},{8,1... | collective-permute-start | bytes 1572872 | tf_op jit(solution)/shard_map/ppermute | solution.py:455
  31.0 16.2 %collective-permute-start.6 = (bf16[512,1024]{1,0:T(8,128)(2,1)S(1)}, bf16[512,1024]{1,0:T(8,128)(2,1)S(1)}, u32[]{:S(2)}, u32[]{:S(2)}) collective-permute-start(bf16[512,1024]{1,0:T(8,128)(2,1)S(1)} %copy-done), channel_id=1, source_target_pairs={{1,0},{0,1},{3,2},{2,3},{5,4},{4,5},{7,6},{6,7},{9,8},{8,9},{11,10... | collective-permute-start | bytes 3145736 | tf_op jit(solution)/shard_map/ppermute | solution.py:449
  31.0 19.7 %collective-permute-start.8 = (bf16[512,1024]{1,0:T(8,128)(2,1)S(1)}, bf16[512,1024]{1,0:T(8,128)(2,1)S(1)}, u32[]{:S(2)}, u32[]{:S(2)}) collective-permute-start(bf16[512,1024]{1,0:T(8,128)(2,1)S(1)} %copy-done.1), channel_id=1, source_target_pairs={{1,0},{0,1},{3,2},{2,3},{5,4},{4,5},{7,6},{6,7},{9,8},{8,9},{11,10... | collective-permute-start | bytes 3145736 | tf_op jit(solution)/shard_map/ppermute | solution.py:449
  40.5 28.1 %collective-permute-start.15 = (bf16[512,1024]{1,0:T(8,128)(2,1)S(1)}, bf16[512,1024]{1,0:T(8,128)(2,1)S(1)}, u32[]{:S(2)}, u32[]{:S(2)}) collective-permute-start(bf16[512,1024]{1,0:T(8,128)(2,1)S(1)} %copy-done.1), channel_id=1, source_target_pairs={{2,0},{3,1},{0,2},{1,3},{6,4},{7,5},{4,6},{5,7},{10,8},{11,9},{8,1... | collective-permute-start | bytes 3145736 | tf_op jit(solution)/shard_map/ppermute | solution.py:455
  42.6 13.8 %collective-permute-start.7 = (bf16[512,1024]{1,0:T(8,128)(2,1)S(1)}, bf16[512,1024]{1,0:T(8,128)(2,1)S(1)}, u32[]{:S(2)}, u32[]{:S(2)}) collective-permute-start(bf16[512,1024]{1,0:T(8,128)(2,1)S(1)} %collective-permute-done.1.refs_3_.refs_7_), channel_id=1, source_target_pairs={{1,0},{0,1},{3,2},{2,3},{5,4},{4,5},{7,6},{6,7},{9,8},{8,9},{11,10... | collective-permute-start | bytes 3145736 | tf_op jit(solution)/shard_map/ppermute | solution.py:449
  43.3 25.0 %collective-permute-start.11 = (bf16[1024,512]{1,0:T(8,128)(2,1)S(1)}, bf16[1024,512]{1,0:T(8,128)(2,1)S(1)}, u32[]{:S(2)}, u32[]{:S(2)}) collective-permute-start(bf16[1024,512]{1,0:T(8,128)(2,1)S(1)} %shard_map.127.refs_0_), channel_id=1, source_target_pairs={{4,0},{0,4},{12,8},{8,12},{20,16},{16,20},{28,24},{24,28},{5,1},{1... | collective-permute-start | bytes 3145736 | tf_op jit(solution)/shard_map/ppermute | solution.py:452
  47.2 5.0 %collective-permute-start.4 = (f32[12,384]{1,0:T(8,128)S(1)}, f32[12,384]{1,0:T(8,128)S(1)}, u32[]{:S(2)}, u32[]{:S(2)}) collective-permute-start(f32[12,384]{1,0:T(8,128)S(1)} %get-tuple-element.51), channel_id=1, source_target_pairs={{0,8},{4,12},{8,16},{12,20},{16,24},{20,28},{1,9},{5,13},{9,17},{1... | collective-permute-start | bytes 55304 | tf_op jit(solution)/shard_map/ppermute | solution.py:70
  50.7 5.7 %collective-permute-start.5 = (f32[12,384]{1,0:T(8,128)S(1)}, f32[12,384]{1,0:T(8,128)S(1)}, u32[]{:S(2)}, u32[]{:S(2)}) collective-permute-start(f32[12,384]{1,0:T(8,128)S(1)} %get-tuple-element.52), channel_id=1, source_target_pairs={{8,0},{12,4},{16,8},{20,12},{24,16},{28,20},{9,1},{13,5},{17,9},{2... | collective-permute-start | bytes 55304 | tf_op jit(solution)/shard_map/ppermute | solution.py:70
  60.1 2.0 %collective-permute-start.9 = (bf16[512,512]{1,0:T(8,128)(2,1)S(1)}, bf16[512,512]{1,0:T(8,128)(2,1)S(1)}, u32[]{:S(2)}, u32[]{:S(2)}) collective-permute-start(bf16[512,512]{1,0:T(8,128)(2,1)S(1)} %get-tuple-element.55.refs_1_), channel_id=1, source_target_pairs={{1,0},{0,1},{3,2},{2,3},{5,4},{4,5},{7,6},{6,7},{9,8},{8,9},{11,10... | collective-permute-start | bytes 1572872 | tf_op jit(solution)/shard_map/ppermute | solution.py:449
  60.2 10.9 %collective-permute-start.17 = (bf16[1024,512]{1,0:T(8,128)(2,1)S(1)}, bf16[1024,512]{1,0:T(8,128)(2,1)S(1)}, u32[]{:S(2)}, u32[]{:S(2)}) collective-permute-start(bf16[1024,512]{1,0:T(8,128)(2,1)S(1)} %shard_map.127.refs_0_), channel_id=1, source_target_pairs={{1,0},{0,1},{3,2},{2,3},{5,4},{4,5},{7,6},{6,7},{9,8},{8,9},{11,10... | collective-permute-start | bytes 3145736 | tf_op jit(solution)/shard_map/ppermute | solution.py:449
  68.5 19.3 %collective-permute-start.18 = (bf16[1024,512]{1,0:T(8,128)(2,1)S(1)}, bf16[1024,512]{1,0:T(8,128)(2,1)S(1)}, u32[]{:S(2)}, u32[]{:S(2)}) collective-permute-start(bf16[1024,512]{1,0:T(8,128)(2,1)S(1)} %shard_map.133), channel_id=1, source_target_pairs={{1,0},{0,1},{3,2},{2,3},{5,4},{4,5},{7,6},{6,7},{9,8},{8,9},{11,10... | collective-permute-start | bytes 3145736 | tf_op jit(solution)/shard_map/ppermute | solution.py:449
  68.6 28.7 %collective-permute-start.16 = (bf16[512,1024]{1,0:T(8,128)(2,1)S(1)}, bf16[512,1024]{1,0:T(8,128)(2,1)S(1)}, u32[]{:S(2)}, u32[]{:S(2)}) collective-permute-start(bf16[512,1024]{1,0:T(8,128)(2,1)S(1)} %collective-permute-done.15.refs_9_), channel_id=1, source_target_pairs={{1,0},{0,1},{3,2},{2,3},{5,4},{4,5},{7,6},{6,7},{9,8},{8,9},{11,10... | collective-permute-start | bytes 3145736 | tf_op jit(solution)/shard_map/ppermute | solution.py:449
  69.1 14.8 %collective-permute-start.19 = (bf16[1024,256]{1,0:T(8,128)(2,1)S(1)}, bf16[1024,256]{1,0:T(8,128)(2,1)S(1)}, u32[]{:S(2)}, u32[]{:S(2)}) collective-permute-start(bf16[1024,256]{1,0:T(8,128)(2,1)S(1)} %get-tuple-element.58.refs_5_.refs_1_.refs_4_), channel_id=1, source_target_pairs={{2,0},{3,1},{0,2},{1,3},{6,4},{7,5},{4,6},{5,7},{10,8},{11,9},{8,1... | collective-permute-start | bytes 1572872 | tf_op jit(solution)/shard_map/ppermute | solution.py:455
  70.9 23.4 %collective-permute-start.23 = (bf16[1024,256]{1,0:T(8,128)(2,1)S(1)}, bf16[1024,256]{1,0:T(8,128)(2,1)S(1)}, u32[]{:S(2)}, u32[]{:S(2)}) collective-permute-start(bf16[1024,256]{1,0:T(8,128)(2,1)S(1)} %get-tuple-element.59.refs_6_.refs_2_.refs_4_), channel_id=1, source_target_pairs={{2,0},{3,1},{0,2},{1,3},{6,4},{7,5},{4,6},{5,7},{10,8},{11,9},{8,1... | collective-permute-start | bytes 1572872 | tf_op jit(solution)/shard_map/ppermute | solution.py:455
  71.1 27.5 %collective-permute-start.14 = (bf16[256,1024]{1,0:T(8,128)(2,1)S(1)}, bf16[256,1024]{1,0:T(8,128)(2,1)S(1)}, u32[]{:S(2)}, u32[]{:S(2)}) collective-permute-start(bf16[256,1024]{1,0:T(8,128)(2,1)S(1)} %get-tuple-element.65), channel_id=1, source_target_pairs={{4,0},{0,4},{12,8},{8,12},{20,16},{16,20},{28,24},{24,28},{5,1},{1... | collective-permute-start | bytes 1572872 | tf_op jit(solution)/shard_map/ppermute | solution.py:452
  83.8 15.5 %collective-permute-start.12 = (bf16[384,512]{1,0:T(8,128)(2,1)S(1)}, bf16[384,512]{1,0:T(8,128)(2,1)S(1)}, u32[]{:S(2)}, u32[]{:S(2)}) collective-permute-start(bf16[384,512]{1,0:T(8,128)(2,1)S(1)} %get-tuple-element.61.refs_6_), channel_id=1, source_target_pairs={{0,8},{4,12},{8,16},{12,20},{16,24},{20,28},{1,9},{5,13},{9,17},{1... | collective-permute-start | bytes 1179656 | tf_op jit(solution)/shard_map/ppermute | solution.py:70
  89.4 19.0 %collective-permute-start.20 = (bf16[1024,128]{1,0:T(8,128)(2,1)S(1)}, bf16[1024,128]{1,0:T(8,128)(2,1)S(1)}, u32[]{:S(2)}, u32[]{:S(2)}) collective-permute-start(bf16[1024,128]{1,0:T(8,128)(2,1)S(1)} %get-tuple-element.68), channel_id=1, source_target_pairs={{8,0},{0,24},{12,4},{4,28},{9,1},{1,25},{13,5},{5,29},{10,2},{2,26... | collective-permute-start | bytes 786440 | tf_op jit(solution)/shard_map/ppermute | solution.py:613
  94.3 19.2 %collective-permute-start.21 = (bf16[1024,128]{1,0:T(8,128)(2,1)S(1)}, bf16[1024,128]{1,0:T(8,128)(2,1)S(1)}, u32[]{:S(2)}, u32[]{:S(2)}) collective-permute-start(bf16[1024,128]{1,0:T(8,128)(2,1)S(1)} %get-tuple-element.69), channel_id=1, source_target_pairs={{16,0},{8,24},{20,4},{12,28},{17,1},{9,25},{21,5},{13,29},{18,2},{... | collective-permute-start | bytes 786440 | tf_op jit(solution)/shard_map/ppermute | solution.py:613
  97.3 17.0 %collective-permute-start.22 = (bf16[1024,128]{1,0:T(8,128)(2,1)S(1)}, bf16[1024,128]{1,0:T(8,128)(2,1)S(1)}, u32[]{:S(2)}, u32[]{:S(2)}) collective-permute-start(bf16[1024,128]{1,0:T(8,128)(2,1)S(1)} %get-tuple-element.70), channel_id=1, source_target_pairs={{24,0},{16,24},{28,4},{20,28},{25,1},{17,25},{29,5},{21,29},{26,2}... | collective-permute-start | bytes 786440 | tf_op jit(solution)/shard_map/ppermute | solution.py:613
  98.6 15.7 %collective-permute-start.24 = (bf16[1024,128]{1,0:T(8,128)(2,1)S(1)}, bf16[1024,128]{1,0:T(8,128)(2,1)S(1)}, u32[]{:S(2)}, u32[]{:S(2)}) collective-permute-start(bf16[1024,128]{1,0:T(8,128)(2,1)S(1)} %get-tuple-element.72), channel_id=1, source_target_pairs={{16,8},{24,16},{20,12},{28,20},{17,9},{25,17},{21,13},{29,21},{18,... | collective-permute-start | bytes 786440 | tf_op jit(solution)/shard_map/ppermute | solution.py:613
  99.3 15.8 %collective-permute-start.25 = (bf16[1024,128]{1,0:T(8,128)(2,1)S(1)}, bf16[1024,128]{1,0:T(8,128)(2,1)S(1)}, u32[]{:S(2)}, u32[]{:S(2)}) collective-permute-start(bf16[1024,128]{1,0:T(8,128)(2,1)S(1)} %get-tuple-element.73), channel_id=1, source_target_pairs={{24,8},{0,16},{28,12},{4,20},{25,9},{1,17},{29,13},{5,21},{26,10},... | collective-permute-start | bytes 786440 | tf_op jit(solution)/shard_map/ppermute | solution.py:613
  108.4 10.0 %collective-permute-start.26 = (bf16[1024,128]{1,0:T(8,128)(2,1)S(1)}, bf16[1024,128]{1,0:T(8,128)(2,1)S(1)}, u32[]{:S(2)}, u32[]{:S(2)}) collective-permute-start(bf16[1024,128]{1,0:T(8,128)(2,1)S(1)} %get-tuple-element.74), channel_id=1, source_target_pairs={{0,8},{8,16},{4,12},{12,20},{1,9},{9,17},{5,13},{13,21},{2,10},{10... | collective-permute-start | bytes 786440 | tf_op jit(solution)/shard_map/ppermute | solution.py:613
  113.6 6.7 %collective-permute-start.13 = (bf16[256,512]{1,0:T(8,128)(2,1)S(1)}, bf16[256,512]{1,0:T(8,128)(2,1)S(1)}, u32[]{:S(2)}, u32[]{:S(2)}) collective-permute-start(bf16[256,512]{1,0:T(8,128)(2,1)S(1)} %get-tuple-element.63), channel_id=1, source_target_pairs={{4,0},{0,4},{12,8},{8,12},{20,16},{16,20},{28,24},{24,28},{5,1},{1... | collective-permute-start | bytes 786440 | tf_op jit(solution)/shard_map/ppermute | solution.py:452
  118.5 2.7 %collective-permute-start.27 = (f32[512,128]{1,0:T(8,128)S(1)}, f32[512,128]{1,0:T(8,128)S(1)}, u32[]{:S(2)}, u32[]{:S(2)}) collective-permute-start(f32[512,128]{1,0:T(8,128)S(1)} %get-tuple-element.77), channel_id=1, source_target_pairs={{1,0},{0,1},{3,2},{2,3},{5,4},{4,5},{7,6},{6,7},{9,8},{8,9},{11,10... | collective-permute-start | bytes 786440 | tf_op jit(solution)/shard_map/ppermute | solution.py:449
